TPU v7x, 128 devices: a whole 4x4x4 slice. The times are simulated.
128 devices in a mesh: dp: 16 (over y_lo, z, core), fsdp: 4 (over x), seq: 2 (over y_hi).
Axes of the slice: x: 4, y: 4 (y_hi: 2, y_lo: 2; y = y_hi * 2 + y_lo), z: 4, core: 2. Of those that a mesh axis runs over, the one named last changes fastest.
Arguments:
- hidden: bfloat16 [16384, 14336], P(('dp', 'seq'), 'fsdp'), may hold values from -6 to 6
- grad_out: bfloat16 [16384, 8192], P(('dp', 'seq'), 'fsdp'), may hold values from -1.5 to 1.5
- projection: bfloat16 [8192, 1024], P('fsdp'), may hold values from -0.0625 to 0.0625
- first_moment: float32 [4, 3584, 1024], P('fsdp', ('dp', 'seq')), may hold values from -6 to 6
- second_moment: float32 [4, 3584, 1024], P('fsdp', ('dp', 'seq')), may hold values from 0.5 to 8
Outputs:
- moment_one: float32 [4, 3584, 1024], P('fsdp', ('dp', 'seq'))
- moment_two: float32 [4, 3584, 1024], P('fsdp', ('dp', 'seq'))
- update: bfloat16 [4, 3584, 8192], P(None, ('dp', 'seq'), 'fsdp')
All inputs are finite; a program needn't handle non-finite values.
Results may differ from a plain program's by a relative error of at most 0.0086.
Values may be sent and summed in bfloat16 or wider, within the bound.
No kernel may reach another device: no remote copies, remote signals or barrier semaphores. Data moves between devices by JAX's collectives and lax.ppermute only.
A program may use at most 128 MiB of HBM per device.

v0:
```python
import jax
import jax.numpy as jnp
from jax import lax
from jax.sharding import PartitionSpec as P

STEP = 20


beta_one = 0.9
beta_two = 0.95
adam_eps = 1e-08


def local(hidden, grad_out, projection, first_moment, second_moment):
    partial_proj = jnp.dot(grad_out, projection, preferred_element_type=jnp.float32)
    projected = lax.psum(partial_proj, "fsdp").astype(jnp.bfloat16)
    owned_rows = first_moment.shape[1]
    lowrank = lax.psum_scatter(
        lax.dot_general(
            hidden, projected, (((0,), (0,)), ((), ())), preferred_element_type=jnp.float32
        ),
        ("dp", "seq"),
        scatter_dimension=0,
        tiled=True,
    )
    lowrank = lowrank.reshape(first_moment.shape)
    moment_one = beta_one * first_moment + (1.0 - beta_one) * lowrank
    moment_two = beta_two * second_moment + (1.0 - beta_two) * lowrank * lowrank
    corrected = moment_one / (1.0 - beta_one**STEP)
    spread = jnp.sqrt(moment_two / (1.0 - beta_two**STEP)) + adam_eps
    direction = (corrected / spread).astype(jnp.bfloat16)[0]
    product = lax.dot_general(
        lax.all_gather(direction, "fsdp", axis=0, tiled=True),
        projection,
        (((1,), (1,)), ((), ())),
        preferred_element_type=jnp.float32,
    )
    stacked = product.astype(jnp.bfloat16)
    update = stacked.reshape(lax.axis_size("fsdp"), owned_rows, projection.shape[0])
    return (moment_one, moment_two, update)


def solution(mesh):
    return jax.shard_map(
        local,
        mesh=mesh,
        in_specs=(
            P(("dp", "seq"), "fsdp"),
            P(("dp", "seq"), "fsdp"),
            P("fsdp", None),
            P("fsdp", ("dp", "seq"), None),
            P("fsdp", ("dp", "seq"), None),
        ),
        out_specs=(
            P("fsdp", ("dp", "seq"), None),
            P("fsdp", ("dp", "seq"), None),
            P(None, ("dp", "seq"), "fsdp"),
        ),
        check_vma=False,
    )
```

profile of v0, /device:TPU:0, one launch (start us, length us, event | category | flops | bytes accessed | tf_op | source)
XLA Modules:
  0.0 441.4 jit_solution(12527697814306078715)
XLA Ops:
  7.2 0.0 copy-start
  7.2 0.0 reduce-scatter.4.cloned.1.call-start
  7.2 1.5 copy-done
  8.8 5.9 %fusion.5 = f32[512,1024]{1,0:T(8,128)} fusion(bf16[512,2048]{1,0:T(8,128)(2,1)S(1)} %copy-done, bf16[2048,1024]{1,0:T(8,128)(2,1)} %param.7), kind=kOutput, calls=%fused_computation.9 | convolution fusion | flops 2147483648 | bytes 8388608 | tf_op jit(solution)/shard_map/dot_general | solution.py:15
  14.6 43.7 %all-reduce.1 = bf16[512,1024]{1,0:T(8,128)(2,1)S(1)} all-reduce(f32[512,1024]{1,0:T(8,128)} %fusion.5), channel_id=1, replica_groups=mesh['dp'=16,'fsdp'=4,'seq'=2] {'fsdp'}, use_global_device_ids=true, to_apply=%region_0.0 | all-reduce | flops 524288 | bytes 3145728 | tf_op jit(solution)/shard_map/psum | solution.py:16
  58.3 9.3 %convolution_bitcast_fusion = f32[3584,1024]{0,1:T(8,128)} fusion(bf16[512,3584]{1,0:T(8,128)(2,1)} %param.5, bf16[512,1024]{1,0:T(8,128)(2,1)S(1)} %all-reduce.1), kind=kOutput, calls=%fused_computation | convolution fusion | flops 3758096384 | bytes 19398656 | tf_op jit(solution)/shard_map/dot_general | solution.py:19
  67.6 15.3 %copy.17 = f32[3584,1024]{1,0:T(8,128)} copy(f32[3584,1024]{0,1:T(8,128)} %convolution_bitcast_fusion) | data formatting | bytes 29360128
  82.9 0.0 copy-start.1
  82.9 0.0 copy-start.2
  82.9 0.0 reduce-scatter.4.cloned.1.call-update
  83.0 1.0 copy-done.1
  84.0 1.0 copy.12
  85.0 0.0 copy-done.2
  85.0 1.0 copy.13
  86.0 321.7 %reduce-scatter.4.cloned.1.call-done = f32[112,1024]{1,0:T(8,128)} async-done(((f32[3584,1024]{1,0:T(8,128)}), f32[112,1024]{1,0:T(8,128)}) %reduce-scatter.4.cloned.1.call-update) | async-done | bytes 458768
  407.7 2.0 copy.18
  409.7 1.7 divide_convert_fusion
  411.4 0.8 copy.14
  412.2 14.8 %all-gather = bf16[1,448,1024]{2,1,0:T(8,128)(2,1)S(1)} all-gather(bf16[1,112,1024]{2,1,0:T(8,128)(2,1)} %copy.14), channel_id=2, replica_groups=mesh['dp'=16,'fsdp'=4,'seq'=2] {'fsdp'}, dimensions={1}, use_global_device_ids=true | all-gather | bytes 1146880 | tf_op jit(solution)/shard_map/all_gather | solution.py:33
  427.1 5.5 %convolution_convert_fusion = bf16[448,2048]{1,0:T(8,128)(2,1)} fusion(bf16[2048,1024]{1,0:T(8,128)(2,1)} %param.7, bf16[1,448,1024]{2,1,0:T(8,128)(2,1)S(1)} %all-gather), kind=kOutput, calls=%fused_computation.1 | convolution fusion | flops 1879965696 | bytes 6946816 | tf_op jit(solution)/shard_map/dot_general | solution.py:32
  432.6 1.0 copy.15
  433.6 1.0 copy.16
Async XLA Ops:
  7.2 1.6 copy-start
  7.2 400.5 %reduce-scatter.4.cloned.1.call-start = ((), (), s32[]{:S(2)}) async-start(), calls=%async_computation.1 | async-start | bytes 15138816
  82.9 1.0 copy-start.1
  82.9 2.0 copy-start.2
Sparse Core Ops, SparseCore 0:
  83.1 324.5 reduce-scatter.3
where the time goes:
time: 442 us; the launch traced here: 441 us
  waiting for transfers between devices  322 us (73%)
  blocking collectives  58.5 us (13%)
  local copies, waits for them, and re-layouts  24.7 us (6%)
  matrix products  20.7 us (5%)
  between operations  14.1 us (3%)
    unnamed x2, waiting for transfers between devices  322 us
    psum x1, blocking collectives, local(): projected = lax.psum(partial_proj, 'fsdp').astype(jnp.bfloat16)  43.7 us
    unnamed x12, local copies, waits for them, and re-layouts  23.8 us
    all_gather x1, blocking collectives, local(): lax.all_gather(direction, 'fsdp', axis=0, tiled=True)  14.8 us
    dot_general x1, matrix products, local(): lax.dot_general(hidden, projected, (((0,), (0,)), ((), ())), preferred_el...  9.35 us
  transfers between devices with their start and end apart: 1, of which 1 were waited for; matrix products, arithmetic and copies ran while one was open for 0% of the time, Pallas kernels for 0%

commit v1 on v0

v1 whole, which is shorter than its diff:
```python
import jax
import jax.numpy as jnp
from jax import lax
from jax.experimental import pallas as pl
from jax.experimental.pallas import tpu as pltpu
from jax.sharding import PartitionSpec as P

STEP = 20
beta_one = 0.9
beta_two = 0.95
adam_eps = 1e-08

AXES = ("dp", "fsdp", "seq")
WIDTHS = (512, 512)
STARTS = (0, 512)
RANK = 1024
PARTS = (6, 5, 5)
SHARES = 2
N = 4
ROWS = 112
SCALE = 2.0**22
LEAST = 2.0**-126
VMEM = pl.BlockSpec(memory_space=pltpu.VMEM)
SMEM = pl.BlockSpec(memory_space=pltpu.SMEM)
ANY = pl.BlockSpec(memory_space=pl.ANY)
HBM = pl.BlockSpec(memory_space=pltpu.HBM)
BF16, F32 = jnp.bfloat16, jnp.float32


def place(device):
    device, y_hi = divmod(device, 2)
    device, x = divmod(device, N)
    device, core = divmod(device, 2)
    y_lo, z = divmod(device, N)
    return y_hi * 2 + y_lo, z, core, x


def index(y, z, core, x):
    return ((((y % 2) * N + z) * 2 + core) * N + x) * 2 + y // 2


def along(where):
    return [(device, index(*where(*place(device)))) for device in range(128)]


def exchange(array, pairs):
    return lax.ppermute(array, AXES, pairs)


OTHER_CORE = along(lambda y, z, core, x: (y, z, 1 - core, x))
X_FIRST = along(lambda y, z, core, x: (y, z, core, x ^ (3 if core else 1)))
X_SECOND = along(lambda y, z, core, x: (y, z, core, x ^ (1 if core else 3)))


def plane_pairs(on_z, flip):
    return along(lambda y, z, core, x: (y, z ^ flip, core, x) if on_z == (core == 0) else (y ^ flip, z, core, x))


PLANE = (plane_pairs(True, 1), plane_pairs(False, 1), plane_pairs(True, 3), plane_pairs(False, 3))
ORDERS = ((0, 1, 2, 3), (2, 0, 1, 3))


def tiles(width):
    return [slice(j, min(j + 256, width)) for j in range(0, width, 256)]


def encode(value):
    value = value * SCALE
    square = value * value
    return jnp.where(value < 0, -square * square, square * square).astype(BF16)


def decode(code):
    code = code.astype(F32)
    root = lax.rsqrt(lax.rsqrt(jnp.maximum(jnp.abs(code), LEAST))) * (1.0 / SCALE)
    return jnp.where(code < 0, -root, jnp.where(code > 0, root, 0.0))


def turn_kernel(pos, hidden, _, mine, *refs):
    theirs, turned = refs[:-1], refs[-1]
    y, z, core = pos[0], pos[1], pos[2]
    tile = 512
    for j in range(0, hidden.shape[1], tile):
        turned[j : j + tile, :] = hidden[:, j : j + tile].T
    places = [(k, at * ROWS) for k, blocks in enumerate(PARTS) for at in range(blocks)]
    for outs, c in (((mine,), core), (theirs, 1 - core)):
        for block in range(N * N):
            a = (block >> 3 & 1) ^ 3 * (block >> 1 & 1)
            b = (block >> 2 & 1) ^ 3 * (block & 1)
            z_to = z ^ jnp.where(c == 0, a, b)
            y_to = y ^ jnp.where(c == 0, b, a)
            source = (((y_to & 1) * N + z_to) * 2 + c) * 2 + (y_to >> 1)
            part, at = places[block] if len(outs) > 1 else (0, block * ROWS)
            outs[part][at : at + ROWS, :] = turned[pl.ds(pl.multiple_of(source * ROWS, ROWS), ROWS), :]


def flip_kernel(projection, _, flipped):
    tile = 256
    for j in range(0, projection.shape[0], tile):
        flipped[:, j : j + tile] = projection[j : j + tile, :].T


def project_kernel(start, grad, projection, *refs):
    total, code = refs[-2:]
    for at in tiles(total.shape[1]):
        part = jnp.dot(grad[...], projection[:, start + at.start : start + at.stop], preferred_element_type=F32)
        total[:, at] = part
        code[:, at] = encode(part)


def add_kernel(total, got, *refs):
    out, code = refs[-2:]
    value = total[...] + decode(got[...])
    out[...] = value
    code[...] = encode(value)


def round_kernel(total, got, *refs):
    outs = refs[-SHARES:]
    rows = total.shape[0] // SHARES
    for k, out in enumerate(outs):
        at = slice(k * rows, (k + 1) * rows)
        out[...] = (total[at, :] + decode(got[at, :])).astype(BF16)


def lowrank_kernel(order, mine, *refs):
    ps, qs, other, (keep, give) = refs[:SHARES], refs[SHARES : 2 * SHARES], refs[2 * SHARES : -2], refs[-2:]
    tokens = ps[0].shape[0]
    for at in tiles(keep.shape[1]):
        base = 0
        for blocks, there in zip(PARTS, other):
            lines = slice(base * ROWS, (base + blocks) * ROWS)
            part = jnp.zeros((blocks * ROWS, at.stop - at.start), F32)
            for k, (p, q) in enumerate(zip(ps, qs)):
                share = slice(k * tokens, (k + 1) * tokens)
                part += jnp.dot(mine[lines, share], p[:, at], preferred_element_type=F32)
                part += jnp.dot(there[:, share], q[:, at], preferred_element_type=F32)
            for k in range(blocks):
                to = 0
                for step in order:
                    to = to * 2 + (base + k >> (3 - step) & 1)
                ref = give if to >= 8 else keep
                to = to % 8 * ROWS
                ref[to : to + ROWS, at] = part[k * ROWS : (k + 1) * ROWS, :].astype(ref.dtype)
            base += blocks


def halve_kernel(own, got, *refs):
    keep, give = refs[-2:]
    half = own.shape[0] // 2
    keep[...] = own[:half, :] + got[:half, :].astype(F32)
    give[...] = (own[half:, :] + got[half:, :].astype(F32)).astype(BF16)


def adam_kernel(start, own, got, first, second, moment_one, moment_two, direction):
    lowrank = own[...] + got[...].astype(F32)
    at = slice(start, start + lowrank.shape[1])
    m_one = beta_one * first[0, :, at] + (1.0 - beta_one) * lowrank
    m_two = beta_two * second[0, :, at] + (1.0 - beta_two) * lowrank * lowrank
    moment_one[...] = m_one
    moment_two[...] = m_two
    corrected = m_one / (1.0 - beta_one**STEP)
    spread = jnp.sqrt(m_two / (1.0 - beta_two**STEP)) + adam_eps
    direction[...] = (corrected / spread).astype(BF16)


def join_kernel(own, got, out):
    out[:ROWS, :] = own[...]
    out[ROWS:, :] = got[...]


def update_kernel(start, pos, flipped, near, far, before, out, left):
    core, x = pos[2], pos[3]
    a, b = jnp.where(core == 0, 1, 3), jnp.where(core == 0, 3, 1)
    width = near.shape[1]
    for d, block in enumerate((x, x ^ a, x ^ b, x ^ 2)):
        rows = pl.ds(pl.multiple_of(block * ROWS, ROWS), ROWS)
        left[rows, :] = (near, far)[d // 2][d % 2 * ROWS : (d % 2 + 1) * ROWS, :]
    tile = 512
    for j in range(0, flipped.shape[1], tile):
        at = slice(j, j + tile)
        part = jnp.dot(left[...], flipped[start : start + width, at], preferred_element_type=F32)
        if start:
            part = (part + before[:, at]).astype(BF16)
            for block in range(N):
                out[block, :, at] = part[block * ROWS : (block + 1) * ROWS, :]
        else:
            out[:, at] = part


def call(kernel, outs, scratch=(), flops=0, nbytes=0, specs=None, limit=16):
    def run(*args, after=None):
        return pl.pallas_call(
            kernel,
            out_shape=[jax.ShapeDtypeStruct(s, t) for s, t in outs],
            in_specs=(specs or [SMEM if a.dtype == jnp.int32 else VMEM for a in args]) + [ANY] * (after is not None),
            out_specs=[VMEM] * len(outs),
            scratch_shapes=list(scratch),
            compiler_params=pltpu.CompilerParams(vmem_limit_bytes=limit << 20),
            cost_estimate=pl.CostEstimate(flops=flops, bytes_accessed=nbytes, transcendentals=0),
        )(*args, *([] if after is None else [after]))

    return run


def local(hidden, grad_out, projection, first_moment, second_moment):
    dp, x, seq = (lax.axis_index(a) for a in AXES)
    y = seq * 2 + dp // (2 * N)
    z = (dp // 2) % N
    pos = jnp.stack([y, z, dp % 2, x]).astype(jnp.int32)
    tokens, units = hidden.shape
    depth = grad_out.shape[1]
    half = units // 2

    def project(c, after=None):
        width = WIDTHS[c]
        return call(
            lambda *refs: project_kernel(STARTS[c], *refs),
            [((tokens, width), F32), ((tokens, width), BF16)],
            flops=2 * tokens * depth * width,
            nbytes=2 * tokens * depth + 2 * depth * width,
        )(grad_out, projection, after=after)

    partials = [project(0)]
    partials.append(project(1, partials[0][0]))
    mine, *theirs = call(
        turn_kernel, [((half, tokens), BF16)] + [((blocks * ROWS, tokens), BF16) for blocks in PARTS], [pltpu.VMEM((units, tokens), BF16)], nbytes=4 * units * tokens
    )(pos, hidden, after=partials[1][0])
    other = [exchange(part, OTHER_CORE) for part in theirs]

    ones, twos, nears, fars = [], [], [], []
    flipped = sent = ahead = None
    for c, width in enumerate(WIDTHS):
        total, code = partials[c]
        total, code = call(add_kernel, [((tokens, width), F32), ((tokens, width), BF16)], nbytes=12 * tokens * width)(
            total, exchange(code, X_FIRST), after=flipped
        )
        if c == 0:
            (flipped,) = call(
                flip_kernel,
                [(projection.shape[::-1], BF16)],
                nbytes=4 * projection.size,
            )(projection, after=code)
        projected = call(round_kernel, [((tokens // SHARES, width), BF16)] * SHARES, nbytes=8 * tokens * width)(
            total, exchange(code, X_SECOND), after=sent
        )
        partner = [exchange(share, OTHER_CORE) for share in projected]
        order = ORDERS[c]
        rows = half // 2
        keep, give = call(
            lambda *refs, o=order: lowrank_kernel(o, *refs),
            [((rows, width), F32), ((rows, width), BF16)],
            flops=4 * half * tokens * width,
            nbytes=4 * half * tokens,
        )(mine, *projected, *partner, *other)
        sent = give
        for k, step in enumerate(order[:3]):
            rows //= 2
            keep, give = call(halve_kernel, [((rows, width), F32), ((rows, width), BF16)], nbytes=18 * rows * width)(
                keep, exchange(give, PLANE[step]), after=ahead if k == 0 else None
            )
            if k == 1:
                ahead = give
        m_one, m_two, direction = call(
            lambda *refs, c=c: adam_kernel(STARTS[c], *refs),
            [((ROWS, width), F32)] * 2 + [((ROWS, width), BF16)],
            nbytes=28 * ROWS * width,
        )(keep, exchange(give, PLANE[order[3]]), first_moment, second_moment)
        ones.append(m_one)
        twos.append(m_two)
        (near,) = call(join_kernel, [((2 * ROWS, width), BF16)], nbytes=8 * ROWS * width)(
            direction, exchange(direction, X_FIRST)
        )
        nears.append(near)
        fars.append(exchange(near, X_SECOND))

    update = nears[1]
    for c, (width, out) in enumerate(zip(WIDTHS, (((N * ROWS, depth), F32), ((N, ROWS, depth), BF16)))):
        (update,) = call(
            lambda *refs, c=c: update_kernel(STARTS[c], *refs),
            [out],
            [pltpu.VMEM((N * ROWS, width), BF16)],
            flops=2 * N * ROWS * width * depth,
            nbytes=2 * width * depth + 6 * N * ROWS * depth,
            specs=[SMEM, VMEM, VMEM, VMEM, VMEM if c else ANY],
        )(pos, flipped, nears[c], fars[c], update)
    shape = first_moment.shape
    return jnp.concatenate(ones, axis=1).reshape(shape), jnp.concatenate(twos, axis=1).reshape(shape), update


def solution(mesh):
    return jax.shard_map(
        local,
        mesh=mesh,
        in_specs=(
            P(("dp", "seq"), "fsdp"),
            P(("dp", "seq"), "fsdp"),
            P("fsdp", None),
            P("fsdp", ("dp", "seq"), None),
            P("fsdp", ("dp", "seq"), None),
        ),
        out_specs=(
            P("fsdp", ("dp", "seq"), None),
            P("fsdp", ("dp", "seq"), None),
            P(None, ("dp", "seq"), "fsdp"),
        ),
        check_vma=False,
    )
```

time: 442 us -> 93 us (0.21)
  waiting for transfers between devices: 322 us -> 29.8 us
  blocking collectives: 58.5 us -> 0 us
  starting transfers between devices: 0.04 us -> 35.9 us
  matrix products: 20.7 us -> 0 us
  Pallas kernels: 0 us -> 19.4 us
  local copies, waits for them, and re-layouts: 24.7 us -> 5.83 us
  between operations: 14.1 us -> 0.79 us
    unnamed x2 -> x0, waiting for transfers between devices: 322 us -> none
    psum x1 -> x0, blocking collectives: 43.7 us -> none  [local(): projected = lax.psum(partial_proj, 'fsdp').astype(jnp.bfloat16)]
    ppermute x0 -> x23, starting transfers between devices: none -> 35.9 us  [exchange(): return lax.ppermute(array, AXES, pairs)]
    ppermute x0 -> x23, waiting for transfers between devices: none -> 29.8 us  [exchange(): return lax.ppermute(array, AXES, pairs)]
    dot_general x3 -> x0, matrix products: 20.7 us -> none  [the longest x1 9.35 us: local(): lax.dot_general(hidden, projected, (((0,), (0,)), ((), ())), preferred_el...]
    pallas_call x0 -> x22, Pallas kernels: none -> 19.4 us  [run(): pl.pallas_call(kernel, out_shape=[jax.ShapeDtypeStruct(s, t) for s, t in...]
    unnamed x12, local copies, waits for them, and re-layouts: 23.8 us -> 5.83 us
    all_gather x1 -> x0, blocking collectives: 14.8 us -> none  [local(): lax.all_gather(direction, 'fsdp', axis=0, tiled=True)]
  transfers between devices with their start and end apart: 1 -> 23, of which waited for: 1 -> 16; matrix products, arithmetic and copies ran while one was open for 0% -> 1% of each run, Pallas kernels for 0% -> 15%
where the time goes in v1:
time: 93 us; the launch traced here: 92.8 us
  starting transfers between devices  35.9 us (39%)
  waiting for transfers between devices  29.8 us (32%)
  Pallas kernels  19.4 us (21%)
  local copies, waits for them, and re-layouts  5.83 us (6%)
  other arithmetic  1.07 us (1%)
    ppermute x23, starting transfers between devices, exchange(): return lax.ppermute(array, AXES, pairs)  35.9 us
    ppermute x23, waiting for transfers between devices, exchange(): return lax.ppermute(array, AXES, pairs)  29.8 us
    pallas_call x22, Pallas kernels, run(): pl.pallas_call(kernel, out_shape=[jax.ShapeDtypeStruct(s, t) for s, t in...  19.4 us
    unnamed x12, local copies, waits for them, and re-layouts  5.83 us
  transfers between devices with their start and end apart: 23, of which 16 were waited for; matrix products, arithmetic and copies ran while one was open for 1% of the time, Pallas kernels for 15%

profile of v1, /device:TPU:0, one launch (start us, length us, event | category | flops | bytes accessed | tf_op | source)
XLA Modules:
  0.0 92.8 jit_solution(17781732490670851871)
XLA Ops:
  0.6 0.0 copy-start
  0.6 2.2 %copy-done = bf16[2048,1024]{1,0:T(8,128)(2,1)S(1)} copy-done((bf16[2048,1024]{1,0:T(8,128)(2,1)S(1)}, bf16[2048,1024]{1,0:T(8,128)(2,1)}, u32[]{:S(2)}) %copy-start) | copy-done | bytes 4194328
  2.8 1.6 %copy-done.2 = bf16[512,2048]{1,0:T(8,128)(2,1)S(1)} copy-done((bf16[512,2048]{1,0:T(8,128)(2,1)S(1)}, bf16[512,2048]{1,0:T(8,128)(2,1)}, u32[]{:S(2)}) %copy-start.2) | copy-done | bytes 2097176
  4.4 2.2 %shard_map.76 = (f32[512,512]{1,0:T(8,128)S(1)}, bf16[512,512]{1,0:T(8,128)(2,1)}) custom-call(bf16[512,2048]{1,0:T(8,128)(2,1)S(1)} %copy-done.2, bf16[2048,1024]{1,0:T(8,128)(2,1)S(1)} %copy-done), custom_call_target="tpu_custom_call" | custom-call | flops 1073741824 | bytes 4194304 | tf_op jit(solution)/shard_map/pallas_call | solution.py:193
  6.6 1.6 %collective-permute-start = (bf16[512,512]{1,0:T(8,128)(2,1)}, bf16[512,512]{1,0:T(8,128)(2,1)S(1)}, u32[]{:S(2)}, u32[]{:S(2)}) collective-permute-start(bf16[512,512]{1,0:T(8,128)(2,1)} %get-tuple-element.44), channel_id=1, source_target_pairs={{0,2},{1,3},{2,0},{3,1},{4,6},{5,7},{6,4},{7,5},{8,14},{9,15},{10,... | collective-permute-start | bytes 1572872 | tf_op jit(solution)/shard_map/ppermute | solution.py:47
  8.2 2.2 %shard_map.77 = (f32[512,512]{1,0:T(8,128)S(1)}, bf16[512,512]{1,0:T(8,128)(2,1)}) custom-call(bf16[512,2048]{1,0:T(8,128)(2,1)S(1)} %copy-done.2, bf16[2048,1024]{1,0:T(8,128)(2,1)S(1)} %copy-done, f32[512,512]{1,0:T(8,128)S(1)} %get-tuple-element.41.refs_2_.total), custom_call_target="tpu_custom_call" | custom-call | flops 1073741824 | bytes 4194304 | tf_op jit(solution)/shard_map/pallas_call | solution.py:193
  10.3 0.5 collective-permute-start.11
  10.8 0.1 pad_add_fusion.pos.refs_0_
  10.9 2.0 %copy-done.3 = bf16[512,3584]{1,0:T(8,128)(2,1)S(1)} copy-done((bf16[512,3584]{1,0:T(8,128)(2,1)S(1)}, bf16[512,3584]{1,0:T(8,128)(2,1)}, u32[]{:S(2)}) %copy-start.3) | copy-done | bytes 3670040
  12.9 1.8 %shard_map.78 = (bf16[1792,512]{1,0:T(8,128)(2,1)S(1)}, bf16[672,512]{1,0:T(8,128)(2,1)S(1)}, bf16[560,512]{1,0:T(8,128)(2,1)S(1)}, bf16[560,512]{1,0:T(8,128)(2,1)S(1)}) custom-call(s32[4]{0:T(128)S(1)} %pad_add_fusion.pos.refs_0_, bf16[512,3584]{1,0:T(8,128)(2,1)S(1)} %copy-done.3, f32[512,512]{1,0:T(8,128)S(1)} %get-tuple-element.42._.total), custom_call_target="tpu_custom_call" | custom-call | bytes 7340032 | tf_op jit(solution)/shard_map/pallas_call | solution.py:193
  14.7 0.5 collective-permute-start.5
  15.1 0.8 collective-permute-done.got
  16.0 0.7 shard_map.79
  16.7 2.9 %collective-permute-start.1 = (bf16[512,512]{1,0:T(8,128)(2,1)S(1)}, bf16[512,512]{1,0:T(8,128)(2,1)S(1)}, u32[]{:S(2)}, u32[]{:S(2)}) collective-permute-start(bf16[512,512]{1,0:T(8,128)(2,1)S(1)} %get-tuple-element.46._), channel_id=1, source_target_pairs={{0,6},{1,7},{2,4},{3,5},{4,2},{5,3},{6,0},{7,1},{8,10},{9,11},{10,... | collective-permute-start | bytes 1572872 | tf_op jit(solution)/shard_map/ppermute | solution.py:47
  19.6 0.5 collective-permute-start.6
  20.1 1.2 %shard_map.86.refs_0_.refs_1_ = bf16[1024,2048]{1,0:T(8,128)(2,1)S(1)} custom-call(bf16[2048,1024]{1,0:T(8,128)(2,1)S(1)} %copy-done.1, bf16[512,512]{1,0:T(8,128)(2,1)S(1)} %get-tuple-element.46._), custom_call_target="tpu_custom_call" | custom-call | bytes 8388608 | tf_op jit(solution)/shard_map/pallas_call | solution.py:193
  21.3 2.6 %collective-permute-done.11.got = bf16[512,512]{1,0:T(8,128)(2,1)S(1)} collective-permute-done((bf16[512,512]{1,0:T(8,128)(2,1)}, bf16[512,512]{1,0:T(8,128)(2,1)S(1)}, u32[]{:S(2)}, u32[]{:S(2)}) %collective-permute-start.11) | collective-permute-done | bytes 524320 | tf_op jit(solution)/shard_map/ppermute | solution.py:47
  24.0 0.7 shard_map.87
  24.7 2.8 %collective-permute-start.12 = (bf16[512,512]{1,0:T(8,128)(2,1)S(1)}, bf16[512,512]{1,0:T(8,128)(2,1)S(1)}, u32[]{:S(2)}, u32[]{:S(2)}) collective-permute-start(bf16[512,512]{1,0:T(8,128)(2,1)S(1)} %get-tuple-element.63), channel_id=1, source_target_pairs={{0,6},{1,7},{2,4},{3,5},{4,2},{5,3},{6,0},{7,1},{8,10},{9,11},{10,... | collective-permute-start | bytes 1572872 | tf_op jit(solution)/shard_map/ppermute | solution.py:47
  27.5 0.4 shard_map.80
  27.9 0.1 collective-permute-start.2
  28.0 0.5 collective-permute-start.3
  28.5 1.0 %collective-permute-done.2.refs_3_ = bf16[256,512]{1,0:T(8,128)(2,1)S(1)} collective-permute-done((bf16[256,512]{1,0:T(8,128)(2,1)S(1)}, bf16[256,512]{1,0:T(8,128)(2,1)S(1)}, u32[]{:S(2)}, u32[]{:S(2)}) %collective-permute-start.2) | collective-permute-done | bytes 262176 | tf_op jit(solution)/shard_map/ppermute | solution.py:47
  29.5 0.4 collective-permute-done.3.refs_4_
  29.9 2.1 %shard_map.81 = (f32[896,512]{1,0:T(8,128)S(1)}, bf16[896,512]{1,0:T(8,128)(2,1)S(1)}) custom-call(bf16[1792,512]{1,0:T(8,128)(2,1)S(1)} %get-tuple-element.43.refs_0_, bf16[256,512]{1,0:T(8,128)(2,1)S(1)} %get-tuple-element.47.refs_1_, bf16[256,512]{1,0:T(8,128)(2,1)S(1)} %get-tuple-element.48.refs_2_, bf16[256,512]{1,0:T(8,128)(2,1)S(1)} %collective-permute-done.2.refs_3_, ...), custom_call_target="tpu_custom_call" | custom-call | flops 1879048192 | bytes 3670016 | tf_op jit(solution)/shard_map/pallas_call | solution.py:193
  32.0 2.0 %collective-permute-start.7 = (bf16[896,512]{1,0:T(8,128)(2,1)S(1)}, bf16[896,512]{1,0:T(8,128)(2,1)S(1)}, u32[]{:S(2)}, u32[]{:S(2)}) collective-permute-start(bf16[896,512]{1,0:T(8,128)(2,1)S(1)} %get-tuple-element.53.refs_0_), channel_id=1, source_target_pairs={{0,16},{1,17},{2,18},{3,19},{4,20},{5,21},{6,22},{7,23},{8,72},{9,... | collective-permute-start | bytes 2752520 | tf_op jit(solution)/shard_map/ppermute | solution.py:47
  34.0 1.2 %collective-permute-done.12.got = bf16[512,512]{1,0:T(8,128)(2,1)S(1)} collective-permute-done((bf16[512,512]{1,0:T(8,128)(2,1)S(1)}, bf16[512,512]{1,0:T(8,128)(2,1)S(1)}, u32[]{:S(2)}, u32[]{:S(2)}) %collective-permute-start.12) | collective-permute-done | bytes 524320 | tf_op jit(solution)/shard_map/ppermute | solution.py:47
  35.2 0.4 shard_map.88
  35.6 0.1 collective-permute-start.13
  35.7 0.5 collective-permute-start.14
  36.2 1.0 %collective-permute-done.13.refs_3_ = bf16[256,512]{1,0:T(8,128)(2,1)S(1)} collective-permute-done((bf16[256,512]{1,0:T(8,128)(2,1)S(1)}, bf16[256,512]{1,0:T(8,128)(2,1)S(1)}, u32[]{:S(2)}, u32[]{:S(2)}) %collective-permute-start.13) | collective-permute-done | bytes 262176 | tf_op jit(solution)/shard_map/ppermute | solution.py:47
  37.2 0.4 collective-permute-done.14.refs_4_
  37.6 2.1 %shard_map.89 = (f32[896,512]{1,0:T(8,128)S(1)}, bf16[896,512]{1,0:T(8,128)(2,1)S(1)}) custom-call(bf16[1792,512]{1,0:T(8,128)(2,1)S(1)} %get-tuple-element.43.refs_0_, bf16[256,512]{1,0:T(8,128)(2,1)S(1)} %get-tuple-element.64.refs_1_, bf16[256,512]{1,0:T(8,128)(2,1)S(1)} %get-tuple-element.65.refs_2_, ...), custom_call_target="tpu_custom_call" | custom-call | flops 1879048192 | bytes 3670016 | tf_op jit(solution)/shard_map/pallas_call | solution.py:193
  39.7 4.1 %collective-permute-start.15 = (bf16[896,512]{1,0:T(8,128)(2,1)S(1)}, bf16[896,512]{1,0:T(8,128)(2,1)S(1)}, u32[]{:S(2)}, u32[]{:S(2)}) collective-permute-start(bf16[896,512]{1,0:T(8,128)(2,1)S(1)} %get-tuple-element.67), channel_id=1, source_target_pairs={{0,48},{1,49},{2,50},{3,51},{4,52},{5,53},{6,54},{7,55},{8,73},{9,... | collective-permute-start | bytes 2752520 | tf_op jit(solution)/shard_map/ppermute | solution.py:47
  43.7 1.7 %collective-permute-done.7.got = bf16[896,512]{1,0:T(8,128)(2,1)S(1)} collective-permute-done((bf16[896,512]{1,0:T(8,128)(2,1)S(1)}, bf16[896,512]{1,0:T(8,128)(2,1)S(1)}, u32[]{:S(2)}, u32[]{:S(2)}) %collective-permute-start.7) | collective-permute-done | bytes 917536 | tf_op jit(solution)/shard_map/ppermute | solution.py:47
  45.5 0.2 shard_map.82
  45.6 1.7 %collective-permute-start.8 = (bf16[448,512]{1,0:T(8,128)(2,1)S(1)}, bf16[448,512]{1,0:T(8,128)(2,1)S(1)}, u32[]{:S(2)}, u32[]{:S(2)}) collective-permute-start(bf16[448,512]{1,0:T(8,128)(2,1)S(1)} %get-tuple-element.55), channel_id=1, source_target_pairs={{0,64},{1,65},{2,66},{3,67},{4,68},{5,69},{6,70},{7,71},{8,24},{9,... | collective-permute-start | bytes 1376264 | tf_op jit(solution)/shard_map/ppermute | solution.py:47
  47.3 6.9 %collective-permute-done.8.got = bf16[448,512]{1,0:T(8,128)(2,1)S(1)} collective-permute-done((bf16[448,512]{1,0:T(8,128)(2,1)S(1)}, bf16[448,512]{1,0:T(8,128)(2,1)S(1)}, u32[]{:S(2)}, u32[]{:S(2)}) %collective-permute-start.8) | collective-permute-done | bytes 458784 | tf_op jit(solution)/shard_map/ppermute | solution.py:47
  54.2 0.1 shard_map.83
  54.3 0.9 collective-permute-done.15.got
  55.1 0.2 shard_map.90
  55.3 0.0 copy-start.4
  55.3 0.0 copy-start.5
  55.3 1.2 %collective-permute-start.16 = (bf16[448,512]{1,0:T(8,128)(2,1)S(1)}, bf16[448,512]{1,0:T(8,128)(2,1)S(1)}, u32[]{:S(2)}, u32[]{:S(2)}) collective-permute-start(bf16[448,512]{1,0:T(8,128)(2,1)S(1)} %get-tuple-element.69), channel_id=1, source_target_pairs={{0,16},{1,17},{2,18},{3,19},{4,20},{5,21},{6,22},{7,23},{8,72},{9,... | collective-permute-start | bytes 1376264 | tf_op jit(solution)/shard_map/ppermute | solution.py:47
  56.4 2.5 %collective-permute-start.9 = (bf16[224,512]{1,0:T(8,128)(2,1)S(1)}, bf16[224,512]{1,0:T(8,128)(2,1)S(1)}, u32[]{:S(2)}, u32[]{:S(2)}) collective-permute-start(bf16[224,512]{1,0:T(8,128)(2,1)S(1)} %get-tuple-element.57.refs_0_), channel_id=1, source_target_pairs={{0,48},{1,49},{2,50},{3,51},{4,52},{5,53},{6,54},{7,55},{8,73},{9,... | collective-permute-start | bytes 688136 | tf_op jit(solution)/shard_map/ppermute | solution.py:47
  59.0 4.9 %collective-permute-done.16.got = bf16[448,512]{1,0:T(8,128)(2,1)S(1)} collective-permute-done((bf16[448,512]{1,0:T(8,128)(2,1)S(1)}, bf16[448,512]{1,0:T(8,128)(2,1)S(1)}, u32[]{:S(2)}, u32[]{:S(2)}) %collective-permute-start.16) | collective-permute-done | bytes 458784 | tf_op jit(solution)/shard_map/ppermute | solution.py:47
  63.9 0.1 shard_map.91
  63.9 1.9 %collective-permute-start.17 = (bf16[224,512]{1,0:T(8,128)(2,1)S(1)}, bf16[224,512]{1,0:T(8,128)(2,1)S(1)}, u32[]{:S(2)}, u32[]{:S(2)}) collective-permute-start(bf16[224,512]{1,0:T(8,128)(2,1)S(1)} %get-tuple-element.71), channel_id=1, source_target_pairs={{0,64},{1,65},{2,66},{3,67},{4,68},{5,69},{6,70},{7,71},{8,24},{9,... | collective-permute-start | bytes 688136 | tf_op jit(solution)/shard_map/ppermute | solution.py:47
  65.9 2.0 %collective-permute-start.10 = (bf16[112,512]{1,0:T(8,128)(2,1)S(1)}, bf16[112,512]{1,0:T(8,128)(2,1)S(1)}, u32[]{:S(2)}, u32[]{:S(2)}) collective-permute-start(bf16[112,512]{1,0:T(8,128)(2,1)S(1)} %get-tuple-element.59), channel_id=1, source_target_pairs={{0,65},{1,64},{2,67},{3,66},{4,69},{5,68},{6,71},{7,70},{8,56},{9,... | collective-permute-start | bytes 344072 | tf_op jit(solution)/shard_map/ppermute | solution.py:47
  67.9 2.1 %collective-permute-done.17.got = bf16[224,512]{1,0:T(8,128)(2,1)S(1)} collective-permute-done((bf16[224,512]{1,0:T(8,128)(2,1)S(1)}, bf16[224,512]{1,0:T(8,128)(2,1)S(1)}, u32[]{:S(2)}, u32[]{:S(2)}) %collective-permute-start.17) | collective-permute-done | bytes 229408 | tf_op jit(solution)/shard_map/ppermute | solution.py:47
  70.1 3.1 %collective-permute-start.18 = (bf16[112,512]{1,0:T(8,128)(2,1)S(1)}, bf16[112,512]{1,0:T(8,128)(2,1)S(1)}, u32[]{:S(2)}, u32[]{:S(2)}) collective-permute-start(bf16[112,512]{1,0:T(8,128)(2,1)S(1)} %get-tuple-element.73), channel_id=1, source_target_pairs={{0,65},{1,64},{2,67},{3,66},{4,69},{5,68},{6,71},{7,70},{8,56},{9,... | collective-permute-start | bytes 344072 | tf_op jit(solution)/shard_map/ppermute | solution.py:47
  73.2 0.2 shard_map.85
  73.4 1.0 %collective-permute-start.21 = (bf16[112,512]{1,0:T(8,128)(2,1)S(1)}, bf16[112,512]{1,0:T(8,128)(2,1)S(1)}, u32[]{:S(2)}, u32[]{:S(2)}) collective-permute-start(bf16[112,512]{1,0:T(8,128)(2,1)S(1)} %get-tuple-element.78.own), channel_id=1, source_target_pairs={{0,2},{1,3},{2,0},{3,1},{4,6},{5,7},{6,4},{7,5},{8,14},{9,15},{10,... | collective-permute-start | bytes 344072 | tf_op jit(solution)/shard_map/ppermute | solution.py:47
  74.4 1.8 %collective-permute-done.18.refs_1_ = bf16[112,512]{1,0:T(8,128)(2,1)S(1)} collective-permute-done((bf16[112,512]{1,0:T(8,128)(2,1)S(1)}, bf16[112,512]{1,0:T(8,128)(2,1)S(1)}, u32[]{:S(2)}, u32[]{:S(2)}) %collective-permute-start.18) | collective-permute-done | bytes 114720 | tf_op jit(solution)/shard_map/ppermute | solution.py:47
  76.2 0.2 shard_map.93
  76.4 1.0 %collective-permute-start.19 = (bf16[112,512]{1,0:T(8,128)(2,1)S(1)}, bf16[112,512]{1,0:T(8,128)(2,1)S(1)}, u32[]{:S(2)}, u32[]{:S(2)}) collective-permute-start(bf16[112,512]{1,0:T(8,128)(2,1)S(1)} %get-tuple-element.77.own), channel_id=1, source_target_pairs={{0,2},{1,3},{2,0},{3,1},{4,6},{5,7},{6,4},{7,5},{8,14},{9,15},{10,... | collective-permute-start | bytes 344072 | tf_op jit(solution)/shard_map/ppermute | solution.py:47
  77.3 0.9 %collective-permute-done.21.got = bf16[112,512]{1,0:T(8,128)(2,1)S(1)} collective-permute-done((bf16[112,512]{1,0:T(8,128)(2,1)S(1)}, bf16[112,512]{1,0:T(8,128)(2,1)S(1)}, u32[]{:S(2)}, u32[]{:S(2)}) %collective-permute-start.21) | collective-permute-done | bytes 114720 | tf_op jit(solution)/shard_map/ppermute | solution.py:47
  78.3 2.8 %collective-permute-start.22 = (bf16[224,512]{1,0:T(8,128)(2,1)S(1)}, bf16[224,512]{1,0:T(8,128)(2,1)S(1)}, u32[]{:S(2)}, u32[]{:S(2)}) collective-permute-start(bf16[224,512]{1,0:T(8,128)(2,1)S(1)} %shard_map.95.refs_2_), channel_id=1, source_target_pairs={{0,6},{1,7},{2,4},{3,5},{4,2},{5,3},{6,0},{7,1},{8,10},{9,11},{10,... | collective-permute-start | bytes 688136 | tf_op jit(solution)/shard_map/ppermute | solution.py:47
  81.1 1.4 %collective-permute-done.19.got = bf16[112,512]{1,0:T(8,128)(2,1)S(1)} collective-permute-done((bf16[112,512]{1,0:T(8,128)(2,1)S(1)}, bf16[112,512]{1,0:T(8,128)(2,1)S(1)}, u32[]{:S(2)}, u32[]{:S(2)}) %collective-permute-start.19) | collective-permute-done | bytes 114720 | tf_op jit(solution)/shard_map/ppermute | solution.py:47
  82.6 2.8 %collective-permute-start.20 = (bf16[224,512]{1,0:T(8,128)(2,1)S(1)}, bf16[224,512]{1,0:T(8,128)(2,1)S(1)}, u32[]{:S(2)}, u32[]{:S(2)}) collective-permute-start(bf16[224,512]{1,0:T(8,128)(2,1)S(1)} %shard_map.94.refs_4_.refs_2_), channel_id=1, source_target_pairs={{0,6},{1,7},{2,4},{3,5},{4,2},{5,3},{6,0},{7,1},{8,10},{9,11},{10,... | collective-permute-start | bytes 688136 | tf_op jit(solution)/shard_map/ppermute | solution.py:47
  85.4 1.0 %maximum_bitcast_fusion = (f32[1,112,1024]{2,1,0:T(8,128)}, f32[1,112,1024]{2,1,0:T(8,128)}) fusion(f32[112,512]{1,0:T(8,128)S(1)} %get-tuple-element.74, f32[112,512]{1,0:T(8,128)S(1)} %get-tuple-element.60, f32[112,512]{1,0:T(8,128)S(1)} %get-tuple-element.76, f32[112,512]{1,0:T(8,128)S(1)} %get-tuple-element.75), kind=kLoop, calls=%fused_computation | loop fusion | flops 229376 | bytes 1835008 | tf_op jit(solution)/shard_map/reshape | solution.py:288
  86.4 1.7 %shard_map.96.refs_4_ = f32[448,2048]{1,0:T(8,128)S(1)} custom-call(s32[4]{0:T(128)S(1)} %pad_add_fusion.pos.refs_0_, bf16[1024,2048]{1,0:T(8,128)(2,1)S(1)} %shard_map.86.refs_0_.refs_1_, bf16[224,512]{1,0:T(8,128)(2,1)S(1)} %shard_map.95.refs_2_, bf16[224,512]{1,0:T(8,128)(2,1)S(1)} %collective-permute-done.22.refs_3_, ...), custom_call_target="tpu_custom_call" | custom-call | flops 939524096 | bytes 7602176 | tf_op jit(solution)/shard_map/pallas_call | solution.py:193
  88.1 1.8 %collective-permute-done.20.refs_3_ = bf16[224,512]{1,0:T(8,128)(2,1)S(1)} collective-permute-done((bf16[224,512]{1,0:T(8,128)(2,1)S(1)}, bf16[224,512]{1,0:T(8,128)(2,1)S(1)}, u32[]{:S(2)}, u32[]{:S(2)}) %collective-permute-start.20) | collective-permute-done | bytes 229408 | tf_op jit(solution)/shard_map/ppermute | solution.py:47
  89.9 2.9 %shard_map.97 = bf16[4,112,2048]{2,1,0:T(8,128)(2,1)} custom-call(s32[4]{0:T(128)S(1)} %pad_add_fusion.pos.refs_0_, bf16[1024,2048]{1,0:T(8,128)(2,1)S(1)} %shard_map.86.refs_0_.refs_1_, bf16[224,512]{1,0:T(8,128)(2,1)S(1)} %shard_map.94.refs_4_.refs_2_, bf16[224,512]{1,0:T(8,128)(2,1)S(1)} %collective-permute-done.20.refs_3_, f32[448,2048]{1,0:T(8,128)S(1)} %shard_map.96.refs_4_), custom_call_target="tpu_custom_call" | custom-call | flops 939524096 | bytes 7602176 | tf_op jit(solution)/shard_map/pallas_call | solution.py:193
  (18 shorter events, 0.1 us)
Async XLA Ops:
  0.6 2.2 %copy-start = (bf16[2048,1024]{1,0:T(8,128)(2,1)S(1)}, bf16[2048,1024]{1,0:T(8,128)(2,1)}, u32[]{:S(2)}) copy-start(bf16[2048,1024]{1,0:T(8,128)(2,1)} %projection.1) | copy-start | bytes 12582916
  2.8 1.6 %copy-start.2 = (bf16[512,2048]{1,0:T(8,128)(2,1)S(1)}, bf16[512,2048]{1,0:T(8,128)(2,1)}, u32[]{:S(2)}) copy-start(bf16[512,2048]{1,0:T(8,128)(2,1)} %refs_0_.3) | copy-start | bytes 6291460
  6.6 9.4 %collective-permute-start = (bf16[512,512]{1,0:T(8,128)(2,1)}, bf16[512,512]{1,0:T(8,128)(2,1)S(1)}, u32[]{:S(2)}, u32[]{:S(2)}) collective-permute-start(bf16[512,512]{1,0:T(8,128)(2,1)} %get-tuple-element.44), channel_id=1, source_target_pairs={{0,2},{1,3},{2,0},{3,1},{4,6},{5,7},{6,4},{7,5},{8,14},{9,15},{10,... | collective-permute-start | bytes 1572872 | tf_op jit(solution)/shard_map/ppermute | solution.py:47
  10.3 13.7 %collective-permute-start.11 = (bf16[512,512]{1,0:T(8,128)(2,1)}, bf16[512,512]{1,0:T(8,128)(2,1)S(1)}, u32[]{:S(2)}, u32[]{:S(2)}) collective-permute-start(bf16[512,512]{1,0:T(8,128)(2,1)} %get-tuple-element.61), channel_id=1, source_target_pairs={{0,2},{1,3},{2,0},{3,1},{4,6},{5,7},{6,4},{7,5},{8,14},{9,15},{10,... | collective-permute-start | bytes 1572872 | tf_op jit(solution)/shard_map/ppermute | solution.py:47
  10.9 2.0 %copy-start.3 = (bf16[512,3584]{1,0:T(8,128)(2,1)S(1)}, bf16[512,3584]{1,0:T(8,128)(2,1)}, u32[]{:S(2)}) copy-start(bf16[512,3584]{1,0:T(8,128)(2,1)} %hidden.1) | copy-start | bytes 11010052
  12.9 7.2 %copy-start.1 = (bf16[2048,1024]{1,0:T(8,128)(2,1)S(1)}, bf16[2048,1024]{1,0:T(8,128)(2,1)}, u32[]{:S(2)}) copy-start(bf16[2048,1024]{1,0:T(8,128)(2,1)} %projection.1) | copy-start | bytes 12582916
  14.7 13.3 %collective-permute-start.5 = (bf16[560,512]{1,0:T(8,128)(2,1)S(1)}, bf16[560,512]{1,0:T(8,128)(2,1)S(1)}, u32[]{:S(2)}, u32[]{:S(2)}) collective-permute-start(bf16[560,512]{1,0:T(8,128)(2,1)S(1)} %get-tuple-element.50), channel_id=1, source_target_pairs={{0,8},{1,9},{2,10},{3,11},{4,12},{5,13},{6,14},{7,15},{8,0},{9,1},... | collective-permute-start | bytes 1720328 | tf_op jit(solution)/shard_map/ppermute | solution.py:47
  16.7 10.8 %collective-permute-start.1 = (bf16[512,512]{1,0:T(8,128)(2,1)S(1)}, bf16[512,512]{1,0:T(8,128)(2,1)S(1)}, u32[]{:S(2)}, u32[]{:S(2)}) collective-permute-start(bf16[512,512]{1,0:T(8,128)(2,1)S(1)} %get-tuple-element.46._), channel_id=1, source_target_pairs={{0,6},{1,7},{2,4},{3,5},{4,2},{5,3},{6,0},{7,1},{8,10},{9,11},{10,... | collective-permute-start | bytes 1572872 | tf_op jit(solution)/shard_map/ppermute | solution.py:47
  19.6 8.9 %collective-permute-start.4 = (bf16[672,512]{1,0:T(8,128)(2,1)S(1)}, bf16[672,512]{1,0:T(8,128)(2,1)S(1)}, u32[]{:S(2)}, u32[]{:S(2)}) collective-permute-start(bf16[672,512]{1,0:T(8,128)(2,1)S(1)} %get-tuple-element.49), channel_id=1, source_target_pairs={{0,8},{1,9},{2,10},{3,11},{4,12},{5,13},{6,14},{7,15},{8,0},{9,1},... | collective-permute-start | bytes 2064392 | tf_op jit(solution)/shard_map/ppermute | solution.py:47
  19.6 8.9 %collective-permute-start.6 = (bf16[560,512]{1,0:T(8,128)(2,1)S(1)}, bf16[560,512]{1,0:T(8,128)(2,1)S(1)}, u32[]{:S(2)}, u32[]{:S(2)}) collective-permute-start(bf16[560,512]{1,0:T(8,128)(2,1)S(1)} %get-tuple-element.51), channel_id=1, source_target_pairs={{0,8},{1,9},{2,10},{3,11},{4,12},{5,13},{6,14},{7,15},{8,0},{9,1},... | collective-permute-start | bytes 1720328 | tf_op jit(solution)/shard_map/ppermute | solution.py:47
  24.7 10.5 %collective-permute-start.12 = (bf16[512,512]{1,0:T(8,128)(2,1)S(1)}, bf16[512,512]{1,0:T(8,128)(2,1)S(1)}, u32[]{:S(2)}, u32[]{:S(2)}) collective-permute-start(bf16[512,512]{1,0:T(8,128)(2,1)S(1)} %get-tuple-element.63), channel_id=1, source_target_pairs={{0,6},{1,7},{2,4},{3,5},{4,2},{5,3},{6,0},{7,1},{8,10},{9,11},{10,... | collective-permute-start | bytes 1572872 | tf_op jit(solution)/shard_map/ppermute | solution.py:47
  27.9 1.6 %collective-permute-start.2 = (bf16[256,512]{1,0:T(8,128)(2,1)S(1)}, bf16[256,512]{1,0:T(8,128)(2,1)S(1)}, u32[]{:S(2)}, u32[]{:S(2)}) collective-permute-start(bf16[256,512]{1,0:T(8,128)(2,1)S(1)} %get-tuple-element.47.refs_1_), channel_id=1, source_target_pairs={{0,8},{1,9},{2,10},{3,11},{4,12},{5,13},{6,14},{7,15},{8,0},{9,1},... | collective-permute-start | bytes 786440 | tf_op jit(solution)/shard_map/ppermute | solution.py:47
  28.0 1.9 %collective-permute-start.3 = (bf16[256,512]{1,0:T(8,128)(2,1)S(1)}, bf16[256,512]{1,0:T(8,128)(2,1)S(1)}, u32[]{:S(2)}, u32[]{:S(2)}) collective-permute-start(bf16[256,512]{1,0:T(8,128)(2,1)S(1)} %get-tuple-element.48.refs_2_), channel_id=1, source_target_pairs={{0,8},{1,9},{2,10},{3,11},{4,12},{5,13},{6,14},{7,15},{8,0},{9,1},... | collective-permute-start | bytes 786440 | tf_op jit(solution)/shard_map/ppermute | solution.py:47
  32.0 13.5 %collective-permute-start.7 = (bf16[896,512]{1,0:T(8,128)(2,1)S(1)}, bf16[896,512]{1,0:T(8,128)(2,1)S(1)}, u32[]{:S(2)}, u32[]{:S(2)}) collective-permute-start(bf16[896,512]{1,0:T(8,128)(2,1)S(1)} %get-tuple-element.53.refs_0_), channel_id=1, source_target_pairs={{0,16},{1,17},{2,18},{3,19},{4,20},{5,21},{6,22},{7,23},{8,72},{9,... | collective-permute-start | bytes 2752520 | tf_op jit(solution)/shard_map/ppermute | solution.py:47
  35.6 1.6 %collective-permute-start.13 = (bf16[256,512]{1,0:T(8,128)(2,1)S(1)}, bf16[256,512]{1,0:T(8,128)(2,1)S(1)}, u32[]{:S(2)}, u32[]{:S(2)}) collective-permute-start(bf16[256,512]{1,0:T(8,128)(2,1)S(1)} %get-tuple-element.64.refs_1_), channel_id=1, source_target_pairs={{0,8},{1,9},{2,10},{3,11},{4,12},{5,13},{6,14},{7,15},{8,0},{9,1},... | collective-permute-start | bytes 786440 | tf_op jit(solution)/shard_map/ppermute | solution.py:47
  35.7 1.9 %collective-permute-start.14 = (bf16[256,512]{1,0:T(8,128)(2,1)S(1)}, bf16[256,512]{1,0:T(8,128)(2,1)S(1)}, u32[]{:S(2)}, u32[]{:S(2)}) collective-permute-start(bf16[256,512]{1,0:T(8,128)(2,1)S(1)} %get-tuple-element.65.refs_2_), channel_id=1, source_target_pairs={{0,8},{1,9},{2,10},{3,11},{4,12},{5,13},{6,14},{7,15},{8,0},{9,1},... | collective-permute-start | bytes 786440 | tf_op jit(solution)/shard_map/ppermute | solution.py:47
  39.7 15.5 %collective-permute-start.15 = (bf16[896,512]{1,0:T(8,128)(2,1)S(1)}, bf16[896,512]{1,0:T(8,128)(2,1)S(1)}, u32[]{:S(2)}, u32[]{:S(2)}) collective-permute-start(bf16[896,512]{1,0:T(8,128)(2,1)S(1)} %get-tuple-element.67), channel_id=1, source_target_pairs={{0,48},{1,49},{2,50},{3,51},{4,52},{5,53},{6,54},{7,55},{8,73},{9,... | collective-permute-start | bytes 2752520 | tf_op jit(solution)/shard_map/ppermute | solution.py:47
  45.6 8.6 %collective-permute-start.8 = (bf16[448,512]{1,0:T(8,128)(2,1)S(1)}, bf16[448,512]{1,0:T(8,128)(2,1)S(1)}, u32[]{:S(2)}, u32[]{:S(2)}) collective-permute-start(bf16[448,512]{1,0:T(8,128)(2,1)S(1)} %get-tuple-element.55), channel_id=1, source_target_pairs={{0,64},{1,65},{2,66},{3,67},{4,68},{5,69},{6,70},{7,71},{8,24},{9,... | collective-permute-start | bytes 1376264 | tf_op jit(solution)/shard_map/ppermute | solution.py:47
  55.3 17.9 %copy-start.4 = (f32[1,112,1024]{2,1,0:T(8,128)S(1)}, f32[1,112,1024]{2,1,0:T(8,128)}, u32[]{:S(2)}) copy-start(f32[1,112,1024]{2,1,0:T(8,128)} %refs_2_.3) | copy-start | bytes 1376260
  55.3 17.9 %copy-start.5 = (f32[1,112,1024]{2,1,0:T(8,128)S(1)}, f32[1,112,1024]{2,1,0:T(8,128)}, u32[]{:S(2)}) copy-start(f32[1,112,1024]{2,1,0:T(8,128)} %refs_3_.3) | copy-start | bytes 1376260
  55.3 8.6 %collective-permute-start.16 = (bf16[448,512]{1,0:T(8,128)(2,1)S(1)}, bf16[448,512]{1,0:T(8,128)(2,1)S(1)}, u32[]{:S(2)}, u32[]{:S(2)}) collective-permute-start(bf16[448,512]{1,0:T(8,128)(2,1)S(1)} %get-tuple-element.69), channel_id=1, source_target_pairs={{0,16},{1,17},{2,18},{3,19},{4,20},{5,21},{6,22},{7,23},{8,72},{9,... | collective-permute-start | bytes 1376264 | tf_op jit(solution)/shard_map/ppermute | solution.py:47
  56.4 9.4 %collective-permute-start.9 = (bf16[224,512]{1,0:T(8,128)(2,1)S(1)}, bf16[224,512]{1,0:T(8,128)(2,1)S(1)}, u32[]{:S(2)}, u32[]{:S(2)}) collective-permute-start(bf16[224,512]{1,0:T(8,128)(2,1)S(1)} %get-tuple-element.57.refs_0_), channel_id=1, source_target_pairs={{0,48},{1,49},{2,50},{3,51},{4,52},{5,53},{6,54},{7,55},{8,73},{9,... | collective-permute-start | bytes 688136 | tf_op jit(solution)/shard_map/ppermute | solution.py:47
  63.9 6.1 %collective-permute-start.17 = (bf16[224,512]{1,0:T(8,128)(2,1)S(1)}, bf16[224,512]{1,0:T(8,128)(2,1)S(1)}, u32[]{:S(2)}, u32[]{:S(2)}) collective-permute-start(bf16[224,512]{1,0:T(8,128)(2,1)S(1)} %get-tuple-element.71), channel_id=1, source_target_pairs={{0,64},{1,65},{2,66},{3,67},{4,68},{5,69},{6,70},{7,71},{8,24},{9,... | collective-permute-start | bytes 688136 | tf_op jit(solution)/shard_map/ppermute | solution.py:47
  65.9 7.3 %collective-permute-start.10 = (bf16[112,512]{1,0:T(8,128)(2,1)S(1)}, bf16[112,512]{1,0:T(8,128)(2,1)S(1)}, u32[]{:S(2)}, u32[]{:S(2)}) collective-permute-start(bf16[112,512]{1,0:T(8,128)(2,1)S(1)} %get-tuple-element.59), channel_id=1, source_target_pairs={{0,65},{1,64},{2,67},{3,66},{4,69},{5,68},{6,71},{7,70},{8,56},{9,... | collective-permute-start | bytes 344072 | tf_op jit(solution)/shard_map/ppermute | solution.py:47
  70.1 6.1 %collective-permute-start.18 = (bf16[112,512]{1,0:T(8,128)(2,1)S(1)}, bf16[112,512]{1,0:T(8,128)(2,1)S(1)}, u32[]{:S(2)}, u32[]{:S(2)}) collective-permute-start(bf16[112,512]{1,0:T(8,128)(2,1)S(1)} %get-tuple-element.73), channel_id=1, source_target_pairs={{0,65},{1,64},{2,67},{3,66},{4,69},{5,68},{6,71},{7,70},{8,56},{9,... | collective-permute-start | bytes 344072 | tf_op jit(solution)/shard_map/ppermute | solution.py:47
  73.4 4.9 %collective-permute-start.21 = (bf16[112,512]{1,0:T(8,128)(2,1)S(1)}, bf16[112,512]{1,0:T(8,128)(2,1)S(1)}, u32[]{:S(2)}, u32[]{:S(2)}) collective-permute-start(bf16[112,512]{1,0:T(8,128)(2,1)S(1)} %get-tuple-element.78.own), channel_id=1, source_target_pairs={{0,2},{1,3},{2,0},{3,1},{4,6},{5,7},{6,4},{7,5},{8,14},{9,15},{10,... | collective-permute-start | bytes 344072 | tf_op jit(solution)/shard_map/ppermute | solution.py:47
  76.4 6.2 %collective-permute-start.19 = (bf16[112,512]{1,0:T(8,128)(2,1)S(1)}, bf16[112,512]{1,0:T(8,128)(2,1)S(1)}, u32[]{:S(2)}, u32[]{:S(2)}) collective-permute-start(bf16[112,512]{1,0:T(8,128)(2,1)S(1)} %get-tuple-element.77.own), channel_id=1, source_target_pairs={{0,2},{1,3},{2,0},{3,1},{4,6},{5,7},{6,4},{7,5},{8,14},{9,15},{10,... | collective-permute-start | bytes 344072 | tf_op jit(solution)/shard_map/ppermute | solution.py:47
  78.3 8.1 %collective-permute-start.22 = (bf16[224,512]{1,0:T(8,128)(2,1)S(1)}, bf16[224,512]{1,0:T(8,128)(2,1)S(1)}, u32[]{:S(2)}, u32[]{:S(2)}) collective-permute-start(bf16[224,512]{1,0:T(8,128)(2,1)S(1)} %shard_map.95.refs_2_), channel_id=1, source_target_pairs={{0,6},{1,7},{2,4},{3,5},{4,2},{5,3},{6,0},{7,1},{8,10},{9,11},{10,... | collective-permute-start | bytes 688136 | tf_op jit(solution)/shard_map/ppermute | solution.py:47
  82.6 7.3 %collective-permute-start.20 = (bf16[224,512]{1,0:T(8,128)(2,1)S(1)}, bf16[224,512]{1,0:T(8,128)(2,1)S(1)}, u32[]{:S(2)}, u32[]{:S(2)}) collective-permute-start(bf16[224,512]{1,0:T(8,128)(2,1)S(1)} %shard_map.94.refs_4_.refs_2_), channel_id=1, source_target_pairs={{0,6},{1,7},{2,4},{3,5},{4,2},{5,3},{6,0},{7,1},{8,10},{9,11},{10,... | collective-permute-start | bytes 688136 | tf_op jit(solution)/shard_map/ppermute | solution.py:47

commit v2 on v1

--- a/solution.py
+++ b/solution.py
@@ -15,6 +15,7 @@
 STARTS = (0, 512)
 RANK = 1024
 PARTS = (6, 5, 5)
+AHEAD = 1
 SHARES = 2
 N = 4
 ROWS = 112
@@ -57,7 +58,7 @@
 
 
 PLANE = (plane_pairs(True, 1), plane_pairs(False, 1), plane_pairs(True, 3), plane_pairs(False, 3))
-ORDERS = ((0, 1, 2, 3), (2, 0, 1, 3))
+ORDERS = (((0, 1, 2, 3),), ((2, 0, 1, 3),))
 
 
 def tiles(width):
@@ -123,36 +124,52 @@
         out[...] = (total[at, :] + decode(got[at, :])).astype(BF16)
 
 
-def lowrank_kernel(order, mine, *refs):
-    ps, qs, other, (keep, give) = refs[:SHARES], refs[SHARES : 2 * SHARES], refs[2 * SHARES : -2], refs[-2:]
+def lowrank_kernel(order, leaving, mine, *refs):
+    ps, qs, other, out = refs[:SHARES], refs[SHARES : 2 * SHARES], refs[2 * SHARES : 2 * SHARES + len(PARTS)], refs[-1]
     tokens = ps[0].shape[0]
-    for at in tiles(keep.shape[1]):
+    bit = 3 - order[0]
+    for at in tiles(out.shape[1]):
         base = 0
         for blocks, there in zip(PARTS, other):
-            lines = slice(base * ROWS, (base + blocks) * ROWS)
-            part = jnp.zeros((blocks * ROWS, at.stop - at.start), F32)
-            for k, (p, q) in enumerate(zip(ps, qs)):
-                share = slice(k * tokens, (k + 1) * tokens)
-                part += jnp.dot(mine[lines, share], p[:, at], preferred_element_type=F32)
-                part += jnp.dot(there[:, share], q[:, at], preferred_element_type=F32)
-            for k in range(blocks):
-                to = 0
-                for step in order:
-                    to = to * 2 + (base + k >> (3 - step) & 1)
-                ref = give if to >= 8 else keep
-                to = to % 8 * ROWS
-                ref[to : to + ROWS, at] = part[k * ROWS : (k + 1) * ROWS, :].astype(ref.dtype)
+            taken = [k for k in range(blocks) if (base + k >> bit & 1) == leaving]
+            runs = []
+            for k in taken:
+                if runs and runs[-1][1] == k:
+                    runs[-1][1] = k + 1
+                else:
+                    runs.append([k, k + 1])
+            for first, end in runs:
+                part = jnp.zeros(((end - first) * ROWS, at.stop - at.start), F32)
+                for k, (p, q) in enumerate(zip(ps, qs)):
+                    share = slice(k * tokens, (k + 1) * tokens)
+                    here = slice((base + first) * ROWS, (base + end) * ROWS)
+                    part += jnp.dot(mine[here, share], p[:, at], preferred_element_type=F32)
+                    part += jnp.dot(there[first * ROWS : end * ROWS, share], q[:, at], preferred_element_type=F32)
+                for k in range(first, end):
+                    to = 0
+                    for step in order[1:]:
+                        to = to * 2 + (base + k >> (3 - step) & 1)
+                    lines = slice((k - first) * ROWS, (k - first + 1) * ROWS)
+                    out[to * ROWS : (to + 1) * ROWS, at] = part[lines, :].astype(out.dtype)
             base += blocks
 
 
-def halve_kernel(own, got, *refs):
-    keep, give = refs[-2:]
-    half = own.shape[0] // 2
-    keep[...] = own[:half, :] + got[:half, :].astype(F32)
-    give[...] = (own[half:, :] + got[half:, :].astype(F32)).astype(BF16)
-
-
-def adam_kernel(start, own, got, first, second, moment_one, moment_two, direction):
+def halve_kernel(sides, into, *refs):
+    outs = refs[-2 * into :]
+    column = 0
+    for side in range(sides):
+        own, got = refs[2 * side : 2 * side + 2]
+        keep, give = outs[2 * side : 2 * side + 2] if into == sides else outs
+        half, width = own.shape[0] // 2, own.shape[1]
+        at = slice(column, column + width)
+        keep[:, at] = own[:half, :] + got[:half, :].astype(F32)
+        give[:, at] = (own[half:, :] + got[half:, :].astype(F32)).astype(BF16)
+        if into != sides:
+            column += width
+
+
+def adam_kernel(start, own, got, first, second, *refs):
+    moment_one, moment_two, direction = refs[-3:]
     lowrank = own[...] + got[...].astype(F32)
     at = slice(start, start + lowrank.shape[1])
     m_one = beta_one * first[0, :, at] + (1.0 - beta_one) * lowrank
@@ -169,23 +186,35 @@
     out[ROWS:, :] = got[...]
 
 
-def update_kernel(start, pos, flipped, near, far, before, out, left):
+def update_kernel(start, flipped, near, far, out):
+    width = near.shape[1]
+    for j in range(0, flipped.shape[1], 512):
+        at = slice(j, j + 512)
+        for k, half in enumerate((near, far)):
+            lines = slice(k * 2 * ROWS, (k + 1) * 2 * ROWS)
+            out[lines, at] = jnp.dot(half[...], flipped[start : start + width, at], preferred_element_type=F32)
+
+
+def finish_kernel(start, far, pos, flipped, left, before, *refs):
+    out, held, sems = refs[-3:]
     core, x = pos[2], pos[3]
     a, b = jnp.where(core == 0, 1, 3), jnp.where(core == 0, 3, 1)
-    width = near.shape[1]
-    for d, block in enumerate((x, x ^ a, x ^ b, x ^ 2)):
-        rows = pl.ds(pl.multiple_of(block * ROWS, ROWS), ROWS)
-        left[rows, :] = (near, far)[d // 2][d % 2 * ROWS : (d % 2 + 1) * ROWS, :]
-    tile = 512
-    for j in range(0, flipped.shape[1], tile):
-        at = slice(j, j + tile)
+    blocks = (x ^ b, x ^ 2) if far else (x, x ^ a)
+    width = left.shape[1]
+    copies = []
+    for j in range(0, flipped.shape[1], 512):
+        at = slice(j, j + 512)
         part = jnp.dot(left[...], flipped[start : start + width, at], preferred_element_type=F32)
-        if start:
-            part = (part + before[:, at]).astype(BF16)
-            for block in range(N):
-                out[block, :, at] = part[block * ROWS : (block + 1) * ROWS, :]
-        else:
-            out[:, at] = part
+        lines = slice(2 * ROWS * far, 2 * ROWS * (far + 1))
+        held[:, at] = (part + before[lines, at]).astype(BF16)
+        for k, block in enumerate(blocks):
+            copy = pltpu.make_async_copy(
+                held.at[k * ROWS : (k + 1) * ROWS, at], out.at[block, :, at], sems.at[len(copies)]
+            )
+            copy.start()
+            copies.append(copy)
+    for copy in copies:
+        copy.wait()
 
 
 def call(kernel, outs, scratch=(), flops=0, nbytes=0, specs=None, limit=16):
@@ -221,15 +250,15 @@
             nbytes=2 * tokens * depth + 2 * depth * width,
         )(grad_out, projection, after=after)
 
-    partials = [project(0)]
+    partials = [project(0, pos)]
     partials.append(project(1, partials[0][0]))
     mine, *theirs = call(
         turn_kernel, [((half, tokens), BF16)] + [((blocks * ROWS, tokens), BF16) for blocks in PARTS], [pltpu.VMEM((units, tokens), BF16)], nbytes=4 * units * tokens
     )(pos, hidden, after=partials[1][0])
     other = [exchange(part, OTHER_CORE) for part in theirs]
 
-    ones, twos, nears, fars = [], [], [], []
-    flipped = sent = ahead = None
+    last, ones, twos, nears, fars = [], [], [], [], []
+    flipped = sent = ahead = kept = None
     for c, width in enumerate(WIDTHS):
         total, code = partials[c]
         total, code = call(add_kernel, [((tokens, width), F32), ((tokens, width), BF16)], nbytes=12 * tokens * width)(
@@ -245,27 +274,41 @@
             total, exchange(code, X_SECOND), after=sent
         )
         partner = [exchange(share, OTHER_CORE) for share in projected]
-        order = ORDERS[c]
+        orders = ORDERS[c]
         rows = half // 2
-        keep, give = call(
-            lambda *refs, o=order: lowrank_kernel(o, *refs),
-            [((rows, width), F32), ((rows, width), BF16)],
-            flops=4 * half * tokens * width,
-            nbytes=4 * half * tokens,
-        )(mine, *projected, *partner, *other)
+        parts = []
+        for leaving, kind in ((1, BF16), (0, F32)):
+            parts += call(
+                lambda *refs, o=orders[0], n=leaving: lowrank_kernel(o, n, *refs),
+                [((rows, width), kind)],
+                flops=2 * half * tokens * width,
+                nbytes=2 * half * tokens,
+            )(mine, *projected, *partner, *other, after=kept if leaving else None)
+        give, kept = parts
+        held = kept, give
         sent = give
-        for k, step in enumerate(order[:3]):
+        for k in range(3):
             rows //= 2
-            keep, give = call(halve_kernel, [((rows, width), F32), ((rows, width), BF16)], nbytes=18 * rows * width)(
-                keep, exchange(give, PLANE[step]), after=ahead if k == 0 else None
-            )
-            if k == 1:
-                ahead = give
+            sides = len(held) // 2
+            into = sides if k == 0 else 1
+            steps = [order[k] for order in orders[:sides]]
+            got = [exchange(give, PLANE[step]) for give, step in zip(held[1::2], steps)]
+            held = call(
+                lambda *refs, n=sides, m=into: halve_kernel(n, m, *refs),
+                [((rows, width // into), F32), ((rows, width // into), BF16)] * into,
+                nbytes=18 * rows * width,
+            )(*[a for pair in zip(held[::2], got) for a in pair], after=ahead if k == 0 else None)
+            if k == AHEAD:
+                ahead = held[1]
+        last.append((held[0], exchange(held[1], PLANE[orders[0][3]])))
+        ahead_last = held[1]
+
+    for c, width in enumerate(WIDTHS):
         m_one, m_two, direction = call(
             lambda *refs, c=c: adam_kernel(STARTS[c], *refs),
             [((ROWS, width), F32)] * 2 + [((ROWS, width), BF16)],
             nbytes=28 * ROWS * width,
-        )(keep, exchange(give, PLANE[order[3]]), first_moment, second_moment)
+        )(*last[c], first_moment, second_moment, after=ahead_last)
         ones.append(m_one)
         twos.append(m_two)
         (near,) = call(join_kernel, [((2 * ROWS, width), BF16)], nbytes=8 * ROWS * width)(
@@ -274,16 +317,26 @@
         nears.append(near)
         fars.append(exchange(near, X_SECOND))
 
-    update = nears[1]
-    for c, (width, out) in enumerate(zip(WIDTHS, (((N * ROWS, depth), F32), ((N, ROWS, depth), BF16)))):
-        (update,) = call(
-            lambda *refs, c=c: update_kernel(STARTS[c], *refs),
-            [out],
-            [pltpu.VMEM((N * ROWS, width), BF16)],
-            flops=2 * N * ROWS * width * depth,
-            nbytes=2 * width * depth + 6 * N * ROWS * depth,
-            specs=[SMEM, VMEM, VMEM, VMEM, VMEM if c else ANY],
-        )(pos, flipped, nears[c], fars[c], update)
+    (before,) = call(
+        lambda *refs: update_kernel(STARTS[0], *refs),
+        [((N * ROWS, depth), F32)],
+        flops=2 * N * ROWS * WIDTHS[0] * depth,
+        nbytes=2 * WIDTHS[0] * depth + 4 * N * ROWS * depth,
+    )(flipped, nears[0], fars[0])
+    update = None
+    for far, left in enumerate((nears[1], fars[1])):
+        update = pl.pallas_call(
+            lambda *refs, far=far: finish_kernel(STARTS[1], far, *refs),
+            out_shape=jax.ShapeDtypeStruct((N, ROWS, depth), BF16),
+            in_specs=[SMEM, VMEM, VMEM, VMEM] + [HBM] * far,
+            out_specs=HBM,
+            scratch_shapes=[pltpu.VMEM((2 * ROWS, depth), BF16), pltpu.SemaphoreType.DMA((8,))],
+            input_output_aliases={4: 0} if far else {},
+            compiler_params=pltpu.CompilerParams(vmem_limit_bytes=16 << 20),
+            cost_estimate=pl.CostEstimate(
+                flops=4 * ROWS * WIDTHS[1] * depth, bytes_accessed=2 * WIDTHS[1] * depth, transcendentals=0
+            ),
+        )(pos, flipped, left, before, *([update] if far else []))
     shape = first_moment.shape
     return jnp.concatenate(ones, axis=1).reshape(shape), jnp.concatenate(twos, axis=1).reshape(shape), update
 

time: 93 us -> 90.5 us (0.973)
  local copies, waits for them, and re-layouts: 5.83 us -> 3.93 us
  starting transfers between devices: 35.9 us -> 37.2 us
  waiting for transfers between devices: 29.8 us -> 28.5 us
    pallas_call x22 -> x23, Pallas kernels: 19.4 us -> 14.7 us  [run(): pl.pallas_call(kernel, out_shape=[jax.ShapeDtypeStruct(s, t) for s, t in...]
    pallas_call x0 -> x2, Pallas kernels: none -> 3.93 us  [local(): pl.pallas_call(lambda *refs, far=far: finish_kernel(STARTS[1], far, *refs...]
    unnamed x12, local copies, waits for them, and re-layouts: 5.83 us -> 3.93 us
    ppermute x23, waiting for transfers between devices: 29.8 us -> 28.5 us  [exchange(): return lax.ppermute(array, AXES, pairs)]
    ppermute x23, starting transfers between devices: 35.9 us -> 37.2 us  [exchange(): return lax.ppermute(array, AXES, pairs)]
  transfers between devices with their start and end apart: 23 -> 23, of which waited for: 16 -> 15; matrix products, arithmetic and copies ran while one was open for 1% -> 1% of each run, Pallas kernels for 15% -> 17%
where the time goes in v2:
time: 90.5 us; the launch traced here: 90.3 us
  starting transfers between devices  37.2 us (41%)
  waiting for transfers between devices  28.5 us (31%)
  Pallas kernels  18.6 us (21%)
  local copies, waits for them, and re-layouts  3.93 us (4%)
  other arithmetic  1.07 us (1%)
  between operations  1.03 us (1%)
    ppermute x23, starting transfers between devices, exchange(): return lax.ppermute(array, AXES, pairs)  37.2 us
    ppermute x23, waiting for transfers between devices, exchange(): return lax.ppermute(array, AXES, pairs)  28.5 us
    pallas_call x23, Pallas kernels, run(): pl.pallas_call(kernel, out_shape=[jax.ShapeDtypeStruct(s, t) for s, t in...  14.7 us
    pallas_call x2, Pallas kernels, local(): pl.pallas_call(lambda *refs, far=far: finish_kernel(STARTS[1], far, *refs...  3.93 us
    unnamed x12, local copies, waits for them, and re-layouts  3.93 us
  transfers between devices with their start and end apart: 23, of which 15 were waited for; matrix products, arithmetic and copies ran while one was open for 1% of the time, Pallas kernels for 17%

profile of v2, /device:TPU:0, one launch (start us, length us, event | category | flops | bytes accessed | tf_op | source)
XLA Modules:
  0.0 90.3 jit_solution(18384770724468174766)
XLA Ops:
  0.7 0.1 pad_add_fusion.refs_2_.pos.refs_0_
  0.8 2.2 %copy-done = bf16[2048,1024]{1,0:T(8,128)(2,1)S(1)} copy-done((bf16[2048,1024]{1,0:T(8,128)(2,1)S(1)}, bf16[2048,1024]{1,0:T(8,128)(2,1)}, u32[]{:S(2)}) %copy-start) | copy-done | bytes 4194328
  2.9 1.6 %copy-done.2 = bf16[512,2048]{1,0:T(8,128)(2,1)S(1)} copy-done((bf16[512,2048]{1,0:T(8,128)(2,1)S(1)}, bf16[512,2048]{1,0:T(8,128)(2,1)}, u32[]{:S(2)}) %copy-start.2) | copy-done | bytes 2097176
  4.5 1.4 %shard_map.76 = (f32[512,512]{1,0:T(8,128)S(1)}, bf16[512,512]{1,0:T(8,128)(2,1)S(1)}) custom-call(bf16[512,2048]{1,0:T(8,128)(2,1)S(1)} %copy-done.2, bf16[2048,1024]{1,0:T(8,128)(2,1)S(1)} %copy-done, s32[4]{0:T(128)S(1)} %pad_add_fusion.refs_2_.pos.refs_0_), custom_call_target="tpu_custom_call" | custom-call | flops 1073741824 | bytes 4194304 | tf_op jit(solution)/shard_map/pallas_call | solution.py:222
  5.9 1.7 %collective-permute-start = (bf16[512,512]{1,0:T(8,128)(2,1)S(1)}, bf16[512,512]{1,0:T(8,128)(2,1)S(1)}, u32[]{:S(2)}, u32[]{:S(2)}) collective-permute-start(bf16[512,512]{1,0:T(8,128)(2,1)S(1)} %get-tuple-element.40), channel_id=1, source_target_pairs={{0,2},{1,3},{2,0},{3,1},{4,6},{5,7},{6,4},{7,5},{8,14},{9,15},{10,... | collective-permute-start | bytes 1572872 | tf_op jit(solution)/shard_map/ppermute | solution.py:48
  7.6 1.4 %shard_map.77 = (f32[512,512]{1,0:T(8,128)S(1)}, bf16[512,512]{1,0:T(8,128)(2,1)S(1)}) custom-call(bf16[512,2048]{1,0:T(8,128)(2,1)S(1)} %copy-done.2, bf16[2048,1024]{1,0:T(8,128)(2,1)S(1)} %copy-done, f32[512,512]{1,0:T(8,128)S(1)} %get-tuple-element.37.refs_2_.total), custom_call_target="tpu_custom_call" | custom-call | flops 1073741824 | bytes 4194304 | tf_op jit(solution)/shard_map/pallas_call | solution.py:222
  8.9 0.5 collective-permute-start.11
  9.5 0.1 copy-done.3
  9.6 1.8 %shard_map.78 = (bf16[1792,512]{1,0:T(8,128)(2,1)S(1)}, bf16[672,512]{1,0:T(8,128)(2,1)S(1)}, bf16[560,512]{1,0:T(8,128)(2,1)S(1)}, bf16[560,512]{1,0:T(8,128)(2,1)S(1)}) custom-call(s32[4]{0:T(128)S(1)} %pad_add_fusion.refs_2_.pos.refs_0_, bf16[512,3584]{1,0:T(8,128)(2,1)S(1)} %copy-done.3, f32[512,512]{1,0:T(8,128)S(1)} %get-tuple-element.38._.total), custom_call_target="tpu_custom_call" | custom-call | bytes 7340032 | tf_op jit(solution)/shard_map/pallas_call | solution.py:222
  11.4 0.9 collective-permute-start.5
  12.3 2.9 %collective-permute-done.got = bf16[512,512]{1,0:T(8,128)(2,1)S(1)} collective-permute-done((bf16[512,512]{1,0:T(8,128)(2,1)S(1)}, bf16[512,512]{1,0:T(8,128)(2,1)S(1)}, u32[]{:S(2)}, u32[]{:S(2)}) %collective-permute-start) | collective-permute-done | bytes 524320 | tf_op jit(solution)/shard_map/ppermute | solution.py:48
  15.2 0.7 shard_map.79
  15.9 2.9 %collective-permute-start.1 = (bf16[512,512]{1,0:T(8,128)(2,1)S(1)}, bf16[512,512]{1,0:T(8,128)(2,1)S(1)}, u32[]{:S(2)}, u32[]{:S(2)}) collective-permute-start(bf16[512,512]{1,0:T(8,128)(2,1)S(1)} %get-tuple-element.42._), channel_id=1, source_target_pairs={{0,6},{1,7},{2,4},{3,5},{4,2},{5,3},{6,0},{7,1},{8,10},{9,11},{10,... | collective-permute-start | bytes 1572872 | tf_op jit(solution)/shard_map/ppermute | solution.py:48
  18.8 0.5 collective-permute-start.6
  19.3 1.2 %shard_map.86.refs_0_.refs_1_ = bf16[1024,2048]{1,0:T(8,128)(2,1)S(1)} custom-call(bf16[2048,1024]{1,0:T(8,128)(2,1)S(1)} %copy-done.1, bf16[512,512]{1,0:T(8,128)(2,1)S(1)} %get-tuple-element.42._), custom_call_target="tpu_custom_call" | custom-call | bytes 8388608 | tf_op jit(solution)/shard_map/pallas_call | solution.py:222
  20.5 2.6 %collective-permute-done.11.got = bf16[512,512]{1,0:T(8,128)(2,1)S(1)} collective-permute-done((bf16[512,512]{1,0:T(8,128)(2,1)S(1)}, bf16[512,512]{1,0:T(8,128)(2,1)S(1)}, u32[]{:S(2)}, u32[]{:S(2)}) %collective-permute-start.11) | collective-permute-done | bytes 524320 | tf_op jit(solution)/shard_map/ppermute | solution.py:48
  23.2 0.7 shard_map.87
  23.9 2.8 %collective-permute-start.12 = (bf16[512,512]{1,0:T(8,128)(2,1)S(1)}, bf16[512,512]{1,0:T(8,128)(2,1)S(1)}, u32[]{:S(2)}, u32[]{:S(2)}) collective-permute-start(bf16[512,512]{1,0:T(8,128)(2,1)S(1)} %get-tuple-element.56), channel_id=1, source_target_pairs={{0,6},{1,7},{2,4},{3,5},{4,2},{5,3},{6,0},{7,1},{8,10},{9,11},{10,... | collective-permute-start | bytes 1572872 | tf_op jit(solution)/shard_map/ppermute | solution.py:48
  26.7 0.4 shard_map.80
  27.1 0.1 collective-permute-start.2
  27.2 0.5 collective-permute-start.3
  27.7 1.0 %collective-permute-done.2.refs_3_ = bf16[256,512]{1,0:T(8,128)(2,1)S(1)} collective-permute-done((bf16[256,512]{1,0:T(8,128)(2,1)S(1)}, bf16[256,512]{1,0:T(8,128)(2,1)S(1)}, u32[]{:S(2)}, u32[]{:S(2)}) %collective-permute-start.2) | collective-permute-done | bytes 262176 | tf_op jit(solution)/shard_map/ppermute | solution.py:48
  28.7 0.4 collective-permute-done.3.refs_4_
  29.1 1.1 %shard_map.82.refs_0_ = bf16[896,512]{1,0:T(8,128)(2,1)S(1)} custom-call(bf16[1792,512]{1,0:T(8,128)(2,1)S(1)} %get-tuple-element.39.refs_0_, bf16[256,512]{1,0:T(8,128)(2,1)S(1)} %get-tuple-element.43.refs_1_, bf16[256,512]{1,0:T(8,128)(2,1)S(1)} %get-tuple-element.44.refs_2_, bf16[256,512]{1,0:T(8,128)(2,1)S(1)} %collective-permute-done.2.refs_3_, ...), custom_call_target="tpu_custom_call" | custom-call | flops 939524096 | bytes 1835008 | tf_op jit(solution)/shard_map/pallas_call | solution.py:222
  30.2 2.0 %collective-permute-start.7 = (bf16[896,512]{1,0:T(8,128)(2,1)S(1)}, bf16[896,512]{1,0:T(8,128)(2,1)S(1)}, u32[]{:S(2)}, u32[]{:S(2)}) collective-permute-start(bf16[896,512]{1,0:T(8,128)(2,1)S(1)} %shard_map.82.refs_0_), channel_id=1, source_target_pairs={{0,16},{1,17},{2,18},{3,19},{4,20},{5,21},{6,22},{7,23},{8,72},{9,... | collective-permute-start | bytes 2752520 | tf_op jit(solution)/shard_map/ppermute | solution.py:48
  32.2 2.1 %collective-permute-done.12.got = bf16[512,512]{1,0:T(8,128)(2,1)S(1)} collective-permute-done((bf16[512,512]{1,0:T(8,128)(2,1)S(1)}, bf16[512,512]{1,0:T(8,128)(2,1)S(1)}, u32[]{:S(2)}, u32[]{:S(2)}) %collective-permute-start.12) | collective-permute-done | bytes 524320 | tf_op jit(solution)/shard_map/ppermute | solution.py:48
  34.3 0.4 shard_map.88
  34.8 0.1 collective-permute-start.13
  34.9 0.5 collective-permute-start.14
  35.4 1.1 %shard_map.81.refs_0_.refs_8_ = f32[896,512]{1,0:T(8,128)S(1)} custom-call(bf16[1792,512]{1,0:T(8,128)(2,1)S(1)} %get-tuple-element.39.refs_0_, bf16[256,512]{1,0:T(8,128)(2,1)S(1)} %get-tuple-element.43.refs_1_, bf16[256,512]{1,0:T(8,128)(2,1)S(1)} %get-tuple-element.44.refs_2_, bf16[256,512]{1,0:T(8,128)(2,1)S(1)} %collective-permute-done.2.refs_3_, ...), custom_call_target="tpu_custom_call" | custom-call | flops 939524096 | bytes 1835008 | tf_op jit(solution)/shard_map/pallas_call | solution.py:222
  36.5 0.3 collective-permute-done.14.refs_4_
  36.8 1.2 %shard_map.90 = bf16[896,512]{1,0:T(8,128)(2,1)S(1)} custom-call(bf16[1792,512]{1,0:T(8,128)(2,1)S(1)} %get-tuple-element.39.refs_0_, bf16[256,512]{1,0:T(8,128)(2,1)S(1)} %get-tuple-element.57.refs_1_, bf16[256,512]{1,0:T(8,128)(2,1)S(1)} %get-tuple-element.58.refs_2_, bf16[256,512]{1,0:T(8,128)(2,1)S(1)} %collective-permute-done.13.refs_3_, ...), custom_call_target="tpu_custom_call" | custom-call | flops 939524096 | bytes 1835008 | tf_op jit(solution)/shard_map/pallas_call | solution.py:222
  37.9 4.1 %collective-permute-start.15 = (bf16[896,512]{1,0:T(8,128)(2,1)S(1)}, bf16[896,512]{1,0:T(8,128)(2,1)S(1)}, u32[]{:S(2)}, u32[]{:S(2)}) collective-permute-start(bf16[896,512]{1,0:T(8,128)(2,1)S(1)} %shard_map.90), channel_id=1, source_target_pairs={{0,48},{1,49},{2,50},{3,51},{4,52},{5,53},{6,54},{7,55},{8,73},{9,... | collective-permute-start | bytes 2752520 | tf_op jit(solution)/shard_map/ppermute | solution.py:48
  42.0 1.7 %collective-permute-done.7.refs_1_ = bf16[896,512]{1,0:T(8,128)(2,1)S(1)} collective-permute-done((bf16[896,512]{1,0:T(8,128)(2,1)S(1)}, bf16[896,512]{1,0:T(8,128)(2,1)S(1)}, u32[]{:S(2)}, u32[]{:S(2)}) %collective-permute-start.7) | collective-permute-done | bytes 917536 | tf_op jit(solution)/shard_map/ppermute | solution.py:48
  43.7 0.2 shard_map.83
  43.9 1.7 %collective-permute-start.8 = (bf16[448,512]{1,0:T(8,128)(2,1)S(1)}, bf16[448,512]{1,0:T(8,128)(2,1)S(1)}, u32[]{:S(2)}, u32[]{:S(2)}) collective-permute-start(bf16[448,512]{1,0:T(8,128)(2,1)S(1)} %get-tuple-element.49), channel_id=1, source_target_pairs={{0,64},{1,65},{2,66},{3,67},{4,68},{5,69},{6,70},{7,71},{8,24},{9,... | collective-permute-start | bytes 1376264 | tf_op jit(solution)/shard_map/ppermute | solution.py:48
  45.5 1.1 %shard_map.89.refs_0_ = f32[896,512]{1,0:T(8,128)S(1)} custom-call(bf16[1792,512]{1,0:T(8,128)(2,1)S(1)} %get-tuple-element.39.refs_0_, bf16[256,512]{1,0:T(8,128)(2,1)S(1)} %get-tuple-element.57.refs_1_, bf16[256,512]{1,0:T(8,128)(2,1)S(1)} %get-tuple-element.58.refs_2_, bf16[256,512]{1,0:T(8,128)(2,1)S(1)} %collective-permute-done.13.refs_3_, ...), custom_call_target="tpu_custom_call" | custom-call | flops 939524096 | bytes 1835008 | tf_op jit(solution)/shard_map/pallas_call | solution.py:222
  46.6 5.8 %collective-permute-done.8.refs_1_ = bf16[448,512]{1,0:T(8,128)(2,1)S(1)} collective-permute-done((bf16[448,512]{1,0:T(8,128)(2,1)S(1)}, bf16[448,512]{1,0:T(8,128)(2,1)S(1)}, u32[]{:S(2)}, u32[]{:S(2)}) %collective-permute-start.8) | collective-permute-done | bytes 458784 | tf_op jit(solution)/shard_map/ppermute | solution.py:48
  52.4 0.1 shard_map.84
  52.5 0.9 collective-permute-done.15.refs_1_
  53.4 0.2 shard_map.91
  53.6 0.0 copy-start.5
  53.6 1.1 %collective-permute-start.16 = (bf16[448,512]{1,0:T(8,128)(2,1)S(1)}, bf16[448,512]{1,0:T(8,128)(2,1)S(1)}, u32[]{:S(2)}, u32[]{:S(2)}) collective-permute-start(bf16[448,512]{1,0:T(8,128)(2,1)S(1)} %get-tuple-element.60), channel_id=1, source_target_pairs={{0,16},{1,17},{2,18},{3,19},{4,20},{5,21},{6,22},{7,23},{8,72},{9,... | collective-permute-start | bytes 1376264 | tf_op jit(solution)/shard_map/ppermute | solution.py:48
  54.7 2.5 %collective-permute-start.9 = (bf16[224,512]{1,0:T(8,128)(2,1)S(1)}, bf16[224,512]{1,0:T(8,128)(2,1)S(1)}, u32[]{:S(2)}, u32[]{:S(2)}) collective-permute-start(bf16[224,512]{1,0:T(8,128)(2,1)S(1)} %get-tuple-element.51.refs_2_), channel_id=1, source_target_pairs={{0,48},{1,49},{2,50},{3,51},{4,52},{5,53},{6,54},{7,55},{8,73},{9,... | collective-permute-start | bytes 688136 | tf_op jit(solution)/shard_map/ppermute | solution.py:48
  57.2 4.9 %collective-permute-done.16.refs_1_ = bf16[448,512]{1,0:T(8,128)(2,1)S(1)} collective-permute-done((bf16[448,512]{1,0:T(8,128)(2,1)S(1)}, bf16[448,512]{1,0:T(8,128)(2,1)S(1)}, u32[]{:S(2)}, u32[]{:S(2)}) %collective-permute-start.16) | collective-permute-done | bytes 458784 | tf_op jit(solution)/shard_map/ppermute | solution.py:48
  62.1 0.1 shard_map.92
  62.2 2.0 %collective-permute-start.17 = (bf16[224,512]{1,0:T(8,128)(2,1)S(1)}, bf16[224,512]{1,0:T(8,128)(2,1)S(1)}, u32[]{:S(2)}, u32[]{:S(2)}) collective-permute-start(bf16[224,512]{1,0:T(8,128)(2,1)S(1)} %get-tuple-element.62), channel_id=1, source_target_pairs={{0,64},{1,65},{2,66},{3,67},{4,68},{5,69},{6,70},{7,71},{8,24},{9,... | collective-permute-start | bytes 688136 | tf_op jit(solution)/shard_map/ppermute | solution.py:48
  64.2 2.0 %collective-permute-start.10 = (bf16[112,512]{1,0:T(8,128)(2,1)S(1)}, bf16[112,512]{1,0:T(8,128)(2,1)S(1)}, u32[]{:S(2)}, u32[]{:S(2)}) collective-permute-start(bf16[112,512]{1,0:T(8,128)(2,1)S(1)} %get-tuple-element.53), channel_id=1, source_target_pairs={{0,65},{1,64},{2,67},{3,66},{4,69},{5,68},{6,71},{7,70},{8,56},{9,... | collective-permute-start | bytes 344072 | tf_op jit(solution)/shard_map/ppermute | solution.py:48
  66.2 2.1 %collective-permute-done.17.refs_1_ = bf16[224,512]{1,0:T(8,128)(2,1)S(1)} collective-permute-done((bf16[224,512]{1,0:T(8,128)(2,1)S(1)}, bf16[224,512]{1,0:T(8,128)(2,1)S(1)}, u32[]{:S(2)}, u32[]{:S(2)}) %collective-permute-start.17) | collective-permute-done | bytes 229408 | tf_op jit(solution)/shard_map/ppermute | solution.py:48
  68.4 3.1 %collective-permute-start.18 = (bf16[112,512]{1,0:T(8,128)(2,1)S(1)}, bf16[112,512]{1,0:T(8,128)(2,1)S(1)}, u32[]{:S(2)}, u32[]{:S(2)}) collective-permute-start(bf16[112,512]{1,0:T(8,128)(2,1)S(1)} %get-tuple-element.63.refs_4_), channel_id=1, source_target_pairs={{0,65},{1,64},{2,67},{3,66},{4,69},{5,68},{6,71},{7,70},{8,56},{9,... | collective-permute-start | bytes 344072 | tf_op jit(solution)/shard_map/ppermute | solution.py:48
  71.5 0.2 shard_map.94
  71.7 1.3 %collective-permute-start.21 = (bf16[112,512]{1,0:T(8,128)(2,1)S(1)}, bf16[112,512]{1,0:T(8,128)(2,1)S(1)}, u32[]{:S(2)}, u32[]{:S(2)}) collective-permute-start(bf16[112,512]{1,0:T(8,128)(2,1)S(1)} %get-tuple-element.70.own), channel_id=1, source_target_pairs={{0,2},{1,3},{2,0},{3,1},{4,6},{5,7},{6,4},{7,5},{8,14},{9,15},{10,... | collective-permute-start | bytes 344072 | tf_op jit(solution)/shard_map/ppermute | solution.py:48
  73.0 1.5 %collective-permute-done.18.refs_1_ = bf16[112,512]{1,0:T(8,128)(2,1)S(1)} collective-permute-done((bf16[112,512]{1,0:T(8,128)(2,1)S(1)}, bf16[112,512]{1,0:T(8,128)(2,1)S(1)}, u32[]{:S(2)}, u32[]{:S(2)}) %collective-permute-start.18) | collective-permute-done | bytes 114720 | tf_op jit(solution)/shard_map/ppermute | solution.py:48
  74.4 0.2 shard_map.95
  74.7 1.4 %collective-permute-start.19 = (bf16[112,512]{1,0:T(8,128)(2,1)S(1)}, bf16[112,512]{1,0:T(8,128)(2,1)S(1)}, u32[]{:S(2)}, u32[]{:S(2)}) collective-permute-start(bf16[112,512]{1,0:T(8,128)(2,1)S(1)} %get-tuple-element.69.own), channel_id=1, source_target_pairs={{0,2},{1,3},{2,0},{3,1},{4,6},{5,7},{6,4},{7,5},{8,14},{9,15},{10,... | collective-permute-start | bytes 344072 | tf_op jit(solution)/shard_map/ppermute | solution.py:48
  76.0 0.5 collective-permute-done.21.got
  76.6 2.8 %collective-permute-start.22 = (bf16[224,512]{1,0:T(8,128)(2,1)S(1)}, bf16[224,512]{1,0:T(8,128)(2,1)S(1)}, u32[]{:S(2)}, u32[]{:S(2)}) collective-permute-start(bf16[224,512]{1,0:T(8,128)(2,1)S(1)} %shard_map.97.refs_1_), channel_id=1, source_target_pairs={{0,6},{1,7},{2,4},{3,5},{4,2},{5,3},{6,0},{7,1},{8,10},{9,11},{10,... | collective-permute-start | bytes 688136 | tf_op jit(solution)/shard_map/ppermute | solution.py:48
  79.4 1.4 %collective-permute-done.19.got = bf16[112,512]{1,0:T(8,128)(2,1)S(1)} collective-permute-done((bf16[112,512]{1,0:T(8,128)(2,1)S(1)}, bf16[112,512]{1,0:T(8,128)(2,1)S(1)}, u32[]{:S(2)}, u32[]{:S(2)}) %collective-permute-start.19) | collective-permute-done | bytes 114720 | tf_op jit(solution)/shard_map/ppermute | solution.py:48
  80.8 2.8 %collective-permute-start.20 = (bf16[224,512]{1,0:T(8,128)(2,1)S(1)}, bf16[224,512]{1,0:T(8,128)(2,1)S(1)}, u32[]{:S(2)}, u32[]{:S(2)}) collective-permute-start(bf16[224,512]{1,0:T(8,128)(2,1)S(1)} %shard_map.96.refs_2_), channel_id=1, source_target_pairs={{0,6},{1,7},{2,4},{3,5},{4,2},{5,3},{6,0},{7,1},{8,10},{9,11},{10,... | collective-permute-start | bytes 688136 | tf_op jit(solution)/shard_map/ppermute | solution.py:48
  83.7 1.0 %maximum_bitcast_fusion = (f32[1,112,1024]{2,1,0:T(8,128)}, f32[1,112,1024]{2,1,0:T(8,128)}) fusion(f32[112,512]{1,0:T(8,128)S(1)} %get-tuple-element.66, f32[112,512]{1,0:T(8,128)S(1)} %get-tuple-element.64, f32[112,512]{1,0:T(8,128)S(1)} %get-tuple-element.68, f32[112,512]{1,0:T(8,128)S(1)} %get-tuple-element.67), kind=kLoop, calls=%fused_computation | loop fusion | flops 229376 | bytes 1835008 | tf_op jit(solution)/shard_map/reshape | solution.py:341
  84.7 1.2 %shard_map.98.refs_3_ = f32[448,2048]{1,0:T(8,128)S(1)} custom-call(bf16[1024,2048]{1,0:T(8,128)(2,1)S(1)} %shard_map.86.refs_0_.refs_1_, bf16[224,512]{1,0:T(8,128)(2,1)S(1)} %shard_map.97.refs_1_, bf16[224,512]{1,0:T(8,128)(2,1)S(1)} %collective-permute-done.22.refs_2_), custom_call_target="tpu_custom_call" | custom-call | flops 939524096 | bytes 5767168 | tf_op jit(solution)/shard_map/pallas_call | solution.py:222
  85.8 2.0 %shard_map.99.refs_4_ = bf16[4,112,2048]{2,1,0:T(8,128)(2,1)} custom-call(s32[4]{0:T(128)S(1)} %pad_add_fusion.refs_2_.pos.refs_0_, bf16[1024,2048]{1,0:T(8,128)(2,1)S(1)} %shard_map.86.refs_0_.refs_1_, bf16[224,512]{1,0:T(8,128)(2,1)S(1)} %shard_map.96.refs_2_, f32[448,2048]{1,0:T(8,128)S(1)} %shard_map.98.refs_3_), custom_call_target="tpu_custom_call" | custom-call | flops 469762048 | bytes 2097152 | tf_op jit(solution)/shard_map/pallas_call | solution.py:328
  87.8 0.3 collective-permute-done.20.refs_2_
  88.2 2.0 %shard_map.100 = bf16[4,112,2048]{2,1,0:T(8,128)(2,1)} custom-call(s32[4]{0:T(128)S(1)} %pad_add_fusion.refs_2_.pos.refs_0_, bf16[1024,2048]{1,0:T(8,128)(2,1)S(1)} %shard_map.86.refs_0_.refs_1_, bf16[224,512]{1,0:T(8,128)(2,1)S(1)} %collective-permute-done.20.refs_2_, f32[448,2048]{1,0:T(8,128)S(1)} %shard_map.98.refs_3_, ...), custom_call_target="tpu_custom_call", output_to_operand_aliasing={{}: (4, {})} | custom-call | flops 469762048 | bytes 2097152 | tf_op jit(solution)/shard_map/pallas_call | solution.py:328
  (21 shorter events, 0.2 us)
Async XLA Ops:
  0.7 2.2 %copy-start = (bf16[2048,1024]{1,0:T(8,128)(2,1)S(1)}, bf16[2048,1024]{1,0:T(8,128)(2,1)}, u32[]{:S(2)}) copy-start(bf16[2048,1024]{1,0:T(8,128)(2,1)} %projection.1) | copy-start | bytes 12582916
  2.9 1.6 %copy-start.2 = (bf16[512,2048]{1,0:T(8,128)(2,1)S(1)}, bf16[512,2048]{1,0:T(8,128)(2,1)}, u32[]{:S(2)}) copy-start(bf16[512,2048]{1,0:T(8,128)(2,1)} %refs_0_.3) | copy-start | bytes 6291460
  5.9 9.3 %collective-permute-start = (bf16[512,512]{1,0:T(8,128)(2,1)S(1)}, bf16[512,512]{1,0:T(8,128)(2,1)S(1)}, u32[]{:S(2)}, u32[]{:S(2)}) collective-permute-start(bf16[512,512]{1,0:T(8,128)(2,1)S(1)} %get-tuple-element.40), channel_id=1, source_target_pairs={{0,2},{1,3},{2,0},{3,1},{4,6},{5,7},{6,4},{7,5},{8,14},{9,15},{10,... | collective-permute-start | bytes 1572872 | tf_op jit(solution)/shard_map/ppermute | solution.py:48
  7.6 2.0 %copy-start.3 = (bf16[512,3584]{1,0:T(8,128)(2,1)S(1)}, bf16[512,3584]{1,0:T(8,128)(2,1)}, u32[]{:S(2)}) copy-start(bf16[512,3584]{1,0:T(8,128)(2,1)} %hidden.1) | copy-start | bytes 11010052
  8.9 14.2 %collective-permute-start.11 = (bf16[512,512]{1,0:T(8,128)(2,1)S(1)}, bf16[512,512]{1,0:T(8,128)(2,1)S(1)}, u32[]{:S(2)}, u32[]{:S(2)}) collective-permute-start(bf16[512,512]{1,0:T(8,128)(2,1)S(1)} %get-tuple-element.54), channel_id=1, source_target_pairs={{0,2},{1,3},{2,0},{3,1},{4,6},{5,7},{6,4},{7,5},{8,14},{9,15},{10,... | collective-permute-start | bytes 1572872 | tf_op jit(solution)/shard_map/ppermute | solution.py:48
  9.6 9.7 %copy-start.1 = (bf16[2048,1024]{1,0:T(8,128)(2,1)S(1)}, bf16[2048,1024]{1,0:T(8,128)(2,1)}, u32[]{:S(2)}) copy-start(bf16[2048,1024]{1,0:T(8,128)(2,1)} %projection.1) | copy-start | bytes 12582916
  11.4 15.8 %collective-permute-start.5 = (bf16[560,512]{1,0:T(8,128)(2,1)S(1)}, bf16[560,512]{1,0:T(8,128)(2,1)S(1)}, u32[]{:S(2)}, u32[]{:S(2)}) collective-permute-start(bf16[560,512]{1,0:T(8,128)(2,1)S(1)} %get-tuple-element.46), channel_id=1, source_target_pairs={{0,8},{1,9},{2,10},{3,11},{4,12},{5,13},{6,14},{7,15},{8,0},{9,1},... | collective-permute-start | bytes 1720328 | tf_op jit(solution)/shard_map/ppermute | solution.py:48
  15.9 10.8 %collective-permute-start.1 = (bf16[512,512]{1,0:T(8,128)(2,1)S(1)}, bf16[512,512]{1,0:T(8,128)(2,1)S(1)}, u32[]{:S(2)}, u32[]{:S(2)}) collective-permute-start(bf16[512,512]{1,0:T(8,128)(2,1)S(1)} %get-tuple-element.42._), channel_id=1, source_target_pairs={{0,6},{1,7},{2,4},{3,5},{4,2},{5,3},{6,0},{7,1},{8,10},{9,11},{10,... | collective-permute-start | bytes 1572872 | tf_op jit(solution)/shard_map/ppermute | solution.py:48
  18.8 8.9 %collective-permute-start.4 = (bf16[672,512]{1,0:T(8,128)(2,1)S(1)}, bf16[672,512]{1,0:T(8,128)(2,1)S(1)}, u32[]{:S(2)}, u32[]{:S(2)}) collective-permute-start(bf16[672,512]{1,0:T(8,128)(2,1)S(1)} %get-tuple-element.45), channel_id=1, source_target_pairs={{0,8},{1,9},{2,10},{3,11},{4,12},{5,13},{6,14},{7,15},{8,0},{9,1},... | collective-permute-start | bytes 2064392 | tf_op jit(solution)/shard_map/ppermute | solution.py:48
  18.8 8.9 %collective-permute-start.6 = (bf16[560,512]{1,0:T(8,128)(2,1)S(1)}, bf16[560,512]{1,0:T(8,128)(2,1)S(1)}, u32[]{:S(2)}, u32[]{:S(2)}) collective-permute-start(bf16[560,512]{1,0:T(8,128)(2,1)S(1)} %get-tuple-element.47), channel_id=1, source_target_pairs={{0,8},{1,9},{2,10},{3,11},{4,12},{5,13},{6,14},{7,15},{8,0},{9,1},... | collective-permute-start | bytes 1720328 | tf_op jit(solution)/shard_map/ppermute | solution.py:48
  23.9 10.5 %collective-permute-start.12 = (bf16[512,512]{1,0:T(8,128)(2,1)S(1)}, bf16[512,512]{1,0:T(8,128)(2,1)S(1)}, u32[]{:S(2)}, u32[]{:S(2)}) collective-permute-start(bf16[512,512]{1,0:T(8,128)(2,1)S(1)} %get-tuple-element.56), channel_id=1, source_target_pairs={{0,6},{1,7},{2,4},{3,5},{4,2},{5,3},{6,0},{7,1},{8,10},{9,11},{10,... | collective-permute-start | bytes 1572872 | tf_op jit(solution)/shard_map/ppermute | solution.py:48
  27.1 1.6 %collective-permute-start.2 = (bf16[256,512]{1,0:T(8,128)(2,1)S(1)}, bf16[256,512]{1,0:T(8,128)(2,1)S(1)}, u32[]{:S(2)}, u32[]{:S(2)}) collective-permute-start(bf16[256,512]{1,0:T(8,128)(2,1)S(1)} %get-tuple-element.43.refs_1_), channel_id=1, source_target_pairs={{0,8},{1,9},{2,10},{3,11},{4,12},{5,13},{6,14},{7,15},{8,0},{9,1},... | collective-permute-start | bytes 786440 | tf_op jit(solution)/shard_map/ppermute | solution.py:48
  27.2 1.9 %collective-permute-start.3 = (bf16[256,512]{1,0:T(8,128)(2,1)S(1)}, bf16[256,512]{1,0:T(8,128)(2,1)S(1)}, u32[]{:S(2)}, u32[]{:S(2)}) collective-permute-start(bf16[256,512]{1,0:T(8,128)(2,1)S(1)} %get-tuple-element.44.refs_2_), channel_id=1, source_target_pairs={{0,8},{1,9},{2,10},{3,11},{4,12},{5,13},{6,14},{7,15},{8,0},{9,1},... | collective-permute-start | bytes 786440 | tf_op jit(solution)/shard_map/ppermute | solution.py:48
  30.2 13.5 %collective-permute-start.7 = (bf16[896,512]{1,0:T(8,128)(2,1)S(1)}, bf16[896,512]{1,0:T(8,128)(2,1)S(1)}, u32[]{:S(2)}, u32[]{:S(2)}) collective-permute-start(bf16[896,512]{1,0:T(8,128)(2,1)S(1)} %shard_map.82.refs_0_), channel_id=1, source_target_pairs={{0,16},{1,17},{2,18},{3,19},{4,20},{5,21},{6,22},{7,23},{8,72},{9,... | collective-permute-start | bytes 2752520 | tf_op jit(solution)/shard_map/ppermute | solution.py:48
  34.8 1.7 %collective-permute-start.13 = (bf16[256,512]{1,0:T(8,128)(2,1)S(1)}, bf16[256,512]{1,0:T(8,128)(2,1)S(1)}, u32[]{:S(2)}, u32[]{:S(2)}) collective-permute-start(bf16[256,512]{1,0:T(8,128)(2,1)S(1)} %get-tuple-element.57.refs_1_), channel_id=1, source_target_pairs={{0,8},{1,9},{2,10},{3,11},{4,12},{5,13},{6,14},{7,15},{8,0},{9,1},... | collective-permute-start | bytes 786440 | tf_op jit(solution)/shard_map/ppermute | solution.py:48
  34.9 1.9 %collective-permute-start.14 = (bf16[256,512]{1,0:T(8,128)(2,1)S(1)}, bf16[256,512]{1,0:T(8,128)(2,1)S(1)}, u32[]{:S(2)}, u32[]{:S(2)}) collective-permute-start(bf16[256,512]{1,0:T(8,128)(2,1)S(1)} %get-tuple-element.58.refs_2_), channel_id=1, source_target_pairs={{0,8},{1,9},{2,10},{3,11},{4,12},{5,13},{6,14},{7,15},{8,0},{9,1},... | collective-permute-start | bytes 786440 | tf_op jit(solution)/shard_map/ppermute | solution.py:48
  37.9 15.5 %collective-permute-start.15 = (bf16[896,512]{1,0:T(8,128)(2,1)S(1)}, bf16[896,512]{1,0:T(8,128)(2,1)S(1)}, u32[]{:S(2)}, u32[]{:S(2)}) collective-permute-start(bf16[896,512]{1,0:T(8,128)(2,1)S(1)} %shard_map.90), channel_id=1, source_target_pairs={{0,48},{1,49},{2,50},{3,51},{4,52},{5,53},{6,54},{7,55},{8,73},{9,... | collective-permute-start | bytes 2752520 | tf_op jit(solution)/shard_map/ppermute | solution.py:48
  43.9 8.6 %collective-permute-start.8 = (bf16[448,512]{1,0:T(8,128)(2,1)S(1)}, bf16[448,512]{1,0:T(8,128)(2,1)S(1)}, u32[]{:S(2)}, u32[]{:S(2)}) collective-permute-start(bf16[448,512]{1,0:T(8,128)(2,1)S(1)} %get-tuple-element.49), channel_id=1, source_target_pairs={{0,64},{1,65},{2,66},{3,67},{4,68},{5,69},{6,70},{7,71},{8,24},{9,... | collective-permute-start | bytes 1376264 | tf_op jit(solution)/shard_map/ppermute | solution.py:48
  53.6 17.9 %copy-start.4 = (f32[1,112,1024]{2,1,0:T(8,128)S(1)}, f32[1,112,1024]{2,1,0:T(8,128)}, u32[]{:S(2)}) copy-start(f32[1,112,1024]{2,1,0:T(8,128)} %refs_2_.3) | copy-start | bytes 1376260
  53.6 17.9 %copy-start.5 = (f32[1,112,1024]{2,1,0:T(8,128)S(1)}, f32[1,112,1024]{2,1,0:T(8,128)}, u32[]{:S(2)}) copy-start(f32[1,112,1024]{2,1,0:T(8,128)} %refs_3_.3) | copy-start | bytes 1376260
  53.6 8.6 %collective-permute-start.16 = (bf16[448,512]{1,0:T(8,128)(2,1)S(1)}, bf16[448,512]{1,0:T(8,128)(2,1)S(1)}, u32[]{:S(2)}, u32[]{:S(2)}) collective-permute-start(bf16[448,512]{1,0:T(8,128)(2,1)S(1)} %get-tuple-element.60), channel_id=1, source_target_pairs={{0,16},{1,17},{2,18},{3,19},{4,20},{5,21},{6,22},{7,23},{8,72},{9,... | collective-permute-start | bytes 1376264 | tf_op jit(solution)/shard_map/ppermute | solution.py:48
  54.7 9.5 %collective-permute-start.9 = (bf16[224,512]{1,0:T(8,128)(2,1)S(1)}, bf16[224,512]{1,0:T(8,128)(2,1)S(1)}, u32[]{:S(2)}, u32[]{:S(2)}) collective-permute-start(bf16[224,512]{1,0:T(8,128)(2,1)S(1)} %get-tuple-element.51.refs_2_), channel_id=1, source_target_pairs={{0,48},{1,49},{2,50},{3,51},{4,52},{5,53},{6,54},{7,55},{8,73},{9,... | collective-permute-start | bytes 688136 | tf_op jit(solution)/shard_map/ppermute | solution.py:48
  62.2 6.1 %collective-permute-start.17 = (bf16[224,512]{1,0:T(8,128)(2,1)S(1)}, bf16[224,512]{1,0:T(8,128)(2,1)S(1)}, u32[]{:S(2)}, u32[]{:S(2)}) collective-permute-start(bf16[224,512]{1,0:T(8,128)(2,1)S(1)} %get-tuple-element.62), channel_id=1, source_target_pairs={{0,64},{1,65},{2,66},{3,67},{4,68},{5,69},{6,70},{7,71},{8,24},{9,... | collective-permute-start | bytes 688136 | tf_op jit(solution)/shard_map/ppermute | solution.py:48
  64.2 7.2 %collective-permute-start.10 = (bf16[112,512]{1,0:T(8,128)(2,1)S(1)}, bf16[112,512]{1,0:T(8,128)(2,1)S(1)}, u32[]{:S(2)}, u32[]{:S(2)}) collective-permute-start(bf16[112,512]{1,0:T(8,128)(2,1)S(1)} %get-tuple-element.53), channel_id=1, source_target_pairs={{0,65},{1,64},{2,67},{3,66},{4,69},{5,68},{6,71},{7,70},{8,56},{9,... | collective-permute-start | bytes 344072 | tf_op jit(solution)/shard_map/ppermute | solution.py:48
  68.4 6.1 %collective-permute-start.18 = (bf16[112,512]{1,0:T(8,128)(2,1)S(1)}, bf16[112,512]{1,0:T(8,128)(2,1)S(1)}, u32[]{:S(2)}, u32[]{:S(2)}) collective-permute-start(bf16[112,512]{1,0:T(8,128)(2,1)S(1)} %get-tuple-element.63.refs_4_), channel_id=1, source_target_pairs={{0,65},{1,64},{2,67},{3,66},{4,69},{5,68},{6,71},{7,70},{8,56},{9,... | collective-permute-start | bytes 344072 | tf_op jit(solution)/shard_map/ppermute | solution.py:48
  71.7 4.9 %collective-permute-start.21 = (bf16[112,512]{1,0:T(8,128)(2,1)S(1)}, bf16[112,512]{1,0:T(8,128)(2,1)S(1)}, u32[]{:S(2)}, u32[]{:S(2)}) collective-permute-start(bf16[112,512]{1,0:T(8,128)(2,1)S(1)} %get-tuple-element.70.own), channel_id=1, source_target_pairs={{0,2},{1,3},{2,0},{3,1},{4,6},{5,7},{6,4},{7,5},{8,14},{9,15},{10,... | collective-permute-start | bytes 344072 | tf_op jit(solution)/shard_map/ppermute | solution.py:48
  74.7 6.2 %collective-permute-start.19 = (bf16[112,512]{1,0:T(8,128)(2,1)S(1)}, bf16[112,512]{1,0:T(8,128)(2,1)S(1)}, u32[]{:S(2)}, u32[]{:S(2)}) collective-permute-start(bf16[112,512]{1,0:T(8,128)(2,1)S(1)} %get-tuple-element.69.own), channel_id=1, source_target_pairs={{0,2},{1,3},{2,0},{3,1},{4,6},{5,7},{6,4},{7,5},{8,14},{9,15},{10,... | collective-permute-start | bytes 344072 | tf_op jit(solution)/shard_map/ppermute | solution.py:48
  76.6 8.1 %collective-permute-start.22 = (bf16[224,512]{1,0:T(8,128)(2,1)S(1)}, bf16[224,512]{1,0:T(8,128)(2,1)S(1)}, u32[]{:S(2)}, u32[]{:S(2)}) collective-permute-start(bf16[224,512]{1,0:T(8,128)(2,1)S(1)} %shard_map.97.refs_1_), channel_id=1, source_target_pairs={{0,6},{1,7},{2,4},{3,5},{4,2},{5,3},{6,0},{7,1},{8,10},{9,11},{10,... | collective-permute-start | bytes 688136 | tf_op jit(solution)/shard_map/ppermute | solution.py:48
  80.8 7.3 %collective-permute-start.20 = (bf16[224,512]{1,0:T(8,128)(2,1)S(1)}, bf16[224,512]{1,0:T(8,128)(2,1)S(1)}, u32[]{:S(2)}, u32[]{:S(2)}) collective-permute-start(bf16[224,512]{1,0:T(8,128)(2,1)S(1)} %shard_map.96.refs_2_), channel_id=1, source_target_pairs={{0,6},{1,7},{2,4},{3,5},{4,2},{5,3},{6,0},{7,1},{8,10},{9,11},{10,... | collective-permute-start | bytes 688136 | tf_op jit(solution)/shard_map/ppermute | solution.py:48

commit v3 on v2

--- a/solution.py
+++ b/solution.py
@@ -241,14 +241,17 @@
     depth = grad_out.shape[1]
     half = units // 2
 
+    pos, first_columns = lax.optimization_barrier((pos, projection))
+    first_columns = first_columns[:, : WIDTHS[0]]
+
     def project(c, after=None):
         width = WIDTHS[c]
         return call(
-            lambda *refs: project_kernel(STARTS[c], *refs),
+            lambda *refs: project_kernel(STARTS[c] if c else 0, *refs),
             [((tokens, width), F32), ((tokens, width), BF16)],
             flops=2 * tokens * depth * width,
             nbytes=2 * tokens * depth + 2 * depth * width,
-        )(grad_out, projection, after=after)
+        )(grad_out, projection if c else first_columns, after=after)
 
     partials = [project(0, pos)]
     partials.append(project(1, partials[0][0]))

time: 90.5 us -> 88.8 us (0.981)
  local copies, waits for them, and re-layouts: 3.93 us -> 2.24 us
    unnamed x12 -> x10, local copies, waits for them, and re-layouts: 3.93 us -> 0.36 us
    slice x0 -> x1, local copies, waits for them, and re-layouts: none -> 1.88 us  [local(): first_columns = first_columns[:, :WIDTHS[0]]]
where the time goes in v3:
time: 88.8 us; the launch traced here: 88.7 us
  starting transfers between devices  37.5 us (42%)
  waiting for transfers between devices  28.4 us (32%)
  Pallas kernels  18.5 us (21%)
  local copies, waits for them, and re-layouts  2.24 us (3%)
  other arithmetic  1.07 us (1%)
  between operations  1.03 us (1%)
    ppermute x23, starting transfers between devices, exchange(): return lax.ppermute(array, AXES, pairs)  37.5 us
    ppermute x23, waiting for transfers between devices, exchange(): return lax.ppermute(array, AXES, pairs)  28.4 us
    pallas_call x23, Pallas kernels, run(): pl.pallas_call(kernel, out_shape=[jax.ShapeDtypeStruct(s, t) for s, t in...  14.6 us
    pallas_call x2, Pallas kernels, local(): pl.pallas_call(lambda *refs, far=far: finish_kernel(STARTS[1], far, *refs...  3.89 us
    slice x1, local copies, waits for them, and re-layouts, local(): first_columns = first_columns[:, :WIDTHS[0]]  1.88 us
  transfers between devices with their start and end apart: 23, of which 15 were waited for; matrix products, arithmetic and copies ran while one was open for 1% of the time, Pallas kernels for 17%

profile of v3, /device:TPU:0, one launch (start us, length us, event | category | flops | bytes accessed | tf_op | source)
XLA Modules:
  0.0 88.7 jit_solution(3422170664569782748)
XLA Ops:
  0.7 0.1 pad_add_fusion.refs_2_.pos.refs_0_
  0.8 1.9 %slice.3.refs_1_ = bf16[2048,512]{1,0:T(8,128)(2,1)S(1)} slice(bf16[2048,1024]{1,0:T(8,128)(2,1)} %projection.1), slice={[0:2048], [0:512]} | slice | bytes 4194304 | tf_op jit(solution)/shard_map/slice | solution.py:245
  2.6 0.3 copy-done.1
  3.0 1.4 %shard_map.76 = (f32[512,512]{1,0:T(8,128)S(1)}, bf16[512,512]{1,0:T(8,128)(2,1)S(1)}) custom-call(bf16[512,2048]{1,0:T(8,128)(2,1)S(1)} %copy-done.1, bf16[2048,512]{1,0:T(8,128)(2,1)S(1)} %slice.3.refs_1_, s32[4]{0:T(128)S(1)} %pad_add_fusion.refs_2_.pos.refs_0_), custom_call_target="tpu_custom_call" | custom-call | flops 1073741824 | bytes 4194304 | tf_op jit(solution)/shard_map/pallas_call | solution.py:222
  4.4 1.7 %collective-permute-start = (bf16[512,512]{1,0:T(8,128)(2,1)S(1)}, bf16[512,512]{1,0:T(8,128)(2,1)S(1)}, u32[]{:S(2)}, u32[]{:S(2)}) collective-permute-start(bf16[512,512]{1,0:T(8,128)(2,1)S(1)} %get-tuple-element.44), channel_id=1, source_target_pairs={{0,2},{1,3},{2,0},{3,1},{4,6},{5,7},{6,4},{7,5},{8,14},{9,15},{10,... | collective-permute-start | bytes 1572872 | tf_op jit(solution)/shard_map/ppermute | solution.py:48
  6.0 1.4 %shard_map.77 = (f32[512,512]{1,0:T(8,128)S(1)}, bf16[512,512]{1,0:T(8,128)(2,1)S(1)}) custom-call(bf16[512,2048]{1,0:T(8,128)(2,1)S(1)} %copy-done.1, bf16[2048,1024]{1,0:T(8,128)(2,1)S(1)} %copy-done, f32[512,512]{1,0:T(8,128)S(1)} %get-tuple-element.41.refs_2_.total), custom_call_target="tpu_custom_call" | custom-call | flops 1073741824 | bytes 4194304 | tf_op jit(solution)/shard_map/pallas_call | solution.py:222
  7.4 0.8 collective-permute-start.11
  8.2 1.8 %shard_map.78 = (bf16[1792,512]{1,0:T(8,128)(2,1)S(1)}, bf16[672,512]{1,0:T(8,128)(2,1)S(1)}, bf16[560,512]{1,0:T(8,128)(2,1)S(1)}, bf16[560,512]{1,0:T(8,128)(2,1)S(1)}) custom-call(s32[4]{0:T(128)S(1)} %pad_add_fusion.refs_2_.pos.refs_0_, bf16[512,3584]{1,0:T(8,128)(2,1)S(1)} %copy-done.2, f32[512,512]{1,0:T(8,128)S(1)} %get-tuple-element.42._.total), custom_call_target="tpu_custom_call" | custom-call | bytes 7340032 | tf_op jit(solution)/shard_map/pallas_call | solution.py:222
  10.0 0.9 %collective-permute-start.5 = (bf16[560,512]{1,0:T(8,128)(2,1)S(1)}, bf16[560,512]{1,0:T(8,128)(2,1)S(1)}, u32[]{:S(2)}, u32[]{:S(2)}) collective-permute-start(bf16[560,512]{1,0:T(8,128)(2,1)S(1)} %get-tuple-element.50), channel_id=1, source_target_pairs={{0,8},{1,9},{2,10},{3,11},{4,12},{5,13},{6,14},{7,15},{8,0},{9,1},... | collective-permute-start | bytes 1720328 | tf_op jit(solution)/shard_map/ppermute | solution.py:48
  10.9 2.7 %collective-permute-done.got = bf16[512,512]{1,0:T(8,128)(2,1)S(1)} collective-permute-done((bf16[512,512]{1,0:T(8,128)(2,1)S(1)}, bf16[512,512]{1,0:T(8,128)(2,1)S(1)}, u32[]{:S(2)}, u32[]{:S(2)}) %collective-permute-start) | collective-permute-done | bytes 524320 | tf_op jit(solution)/shard_map/ppermute | solution.py:48
  13.6 0.7 shard_map.79
  14.3 2.9 %collective-permute-start.1 = (bf16[512,512]{1,0:T(8,128)(2,1)S(1)}, bf16[512,512]{1,0:T(8,128)(2,1)S(1)}, u32[]{:S(2)}, u32[]{:S(2)}) collective-permute-start(bf16[512,512]{1,0:T(8,128)(2,1)S(1)} %get-tuple-element.46._), channel_id=1, source_target_pairs={{0,6},{1,7},{2,4},{3,5},{4,2},{5,3},{6,0},{7,1},{8,10},{9,11},{10,... | collective-permute-start | bytes 1572872 | tf_op jit(solution)/shard_map/ppermute | solution.py:48
  17.2 0.5 collective-permute-start.6
  17.8 1.2 %shard_map.86.refs_0_.refs_1_ = bf16[1024,2048]{1,0:T(8,128)(2,1)S(1)} custom-call(bf16[2048,1024]{1,0:T(8,128)(2,1)S(1)} %copy-done, bf16[512,512]{1,0:T(8,128)(2,1)S(1)} %get-tuple-element.46._), custom_call_target="tpu_custom_call" | custom-call | bytes 8388608 | tf_op jit(solution)/shard_map/pallas_call | solution.py:222
  19.0 2.6 %collective-permute-done.11.got = bf16[512,512]{1,0:T(8,128)(2,1)S(1)} collective-permute-done((bf16[512,512]{1,0:T(8,128)(2,1)S(1)}, bf16[512,512]{1,0:T(8,128)(2,1)S(1)}, u32[]{:S(2)}, u32[]{:S(2)}) %collective-permute-start.11) | collective-permute-done | bytes 524320 | tf_op jit(solution)/shard_map/ppermute | solution.py:48
  21.6 0.7 shard_map.87
  22.3 2.8 %collective-permute-start.12 = (bf16[512,512]{1,0:T(8,128)(2,1)S(1)}, bf16[512,512]{1,0:T(8,128)(2,1)S(1)}, u32[]{:S(2)}, u32[]{:S(2)}) collective-permute-start(bf16[512,512]{1,0:T(8,128)(2,1)S(1)} %get-tuple-element.60), channel_id=1, source_target_pairs={{0,6},{1,7},{2,4},{3,5},{4,2},{5,3},{6,0},{7,1},{8,10},{9,11},{10,... | collective-permute-start | bytes 1572872 | tf_op jit(solution)/shard_map/ppermute | solution.py:48
  25.1 0.4 shard_map.80
  25.6 0.1 collective-permute-start.2
  25.7 0.5 collective-permute-start.3
  26.2 1.0 %collective-permute-done.2.refs_3_ = bf16[256,512]{1,0:T(8,128)(2,1)S(1)} collective-permute-done((bf16[256,512]{1,0:T(8,128)(2,1)S(1)}, bf16[256,512]{1,0:T(8,128)(2,1)S(1)}, u32[]{:S(2)}, u32[]{:S(2)}) %collective-permute-start.2) | collective-permute-done | bytes 262176 | tf_op jit(solution)/shard_map/ppermute | solution.py:48
  27.2 0.4 collective-permute-done.3.refs_4_
  27.6 1.1 %shard_map.82.refs_0_ = bf16[896,512]{1,0:T(8,128)(2,1)S(1)} custom-call(bf16[1792,512]{1,0:T(8,128)(2,1)S(1)} %get-tuple-element.43.refs_0_, bf16[256,512]{1,0:T(8,128)(2,1)S(1)} %get-tuple-element.47.refs_1_, bf16[256,512]{1,0:T(8,128)(2,1)S(1)} %get-tuple-element.48.refs_2_, bf16[256,512]{1,0:T(8,128)(2,1)S(1)} %collective-permute-done.2.refs_3_, ...), custom_call_target="tpu_custom_call" | custom-call | flops 939524096 | bytes 1835008 | tf_op jit(solution)/shard_map/pallas_call | solution.py:222
  28.7 2.0 %collective-permute-start.7 = (bf16[896,512]{1,0:T(8,128)(2,1)S(1)}, bf16[896,512]{1,0:T(8,128)(2,1)S(1)}, u32[]{:S(2)}, u32[]{:S(2)}) collective-permute-start(bf16[896,512]{1,0:T(8,128)(2,1)S(1)} %shard_map.82.refs_0_), channel_id=1, source_target_pairs={{0,16},{1,17},{2,18},{3,19},{4,20},{5,21},{6,22},{7,23},{8,72},{9,... | collective-permute-start | bytes 2752520 | tf_op jit(solution)/shard_map/ppermute | solution.py:48
  30.7 2.1 %collective-permute-done.12.got = bf16[512,512]{1,0:T(8,128)(2,1)S(1)} collective-permute-done((bf16[512,512]{1,0:T(8,128)(2,1)S(1)}, bf16[512,512]{1,0:T(8,128)(2,1)S(1)}, u32[]{:S(2)}, u32[]{:S(2)}) %collective-permute-start.12) | collective-permute-done | bytes 524320 | tf_op jit(solution)/shard_map/ppermute | solution.py:48
  32.8 0.4 shard_map.88
  33.2 0.1 collective-permute-start.13
  33.3 0.5 collective-permute-start.14
  33.8 1.1 %shard_map.81.refs_0_.refs_8_ = f32[896,512]{1,0:T(8,128)S(1)} custom-call(bf16[1792,512]{1,0:T(8,128)(2,1)S(1)} %get-tuple-element.43.refs_0_, bf16[256,512]{1,0:T(8,128)(2,1)S(1)} %get-tuple-element.47.refs_1_, bf16[256,512]{1,0:T(8,128)(2,1)S(1)} %get-tuple-element.48.refs_2_, bf16[256,512]{1,0:T(8,128)(2,1)S(1)} %collective-permute-done.2.refs_3_, ...), custom_call_target="tpu_custom_call" | custom-call | flops 939524096 | bytes 1835008 | tf_op jit(solution)/shard_map/pallas_call | solution.py:222
  34.9 0.3 collective-permute-done.14.refs_4_
  35.2 1.2 %shard_map.90 = bf16[896,512]{1,0:T(8,128)(2,1)S(1)} custom-call(bf16[1792,512]{1,0:T(8,128)(2,1)S(1)} %get-tuple-element.43.refs_0_, bf16[256,512]{1,0:T(8,128)(2,1)S(1)} %get-tuple-element.61.refs_1_, bf16[256,512]{1,0:T(8,128)(2,1)S(1)} %get-tuple-element.62.refs_2_, bf16[256,512]{1,0:T(8,128)(2,1)S(1)} %collective-permute-done.13.refs_3_, ...), custom_call_target="tpu_custom_call" | custom-call | flops 939524096 | bytes 1835008 | tf_op jit(solution)/shard_map/pallas_call | solution.py:222
  36.4 4.1 %collective-permute-start.15 = (bf16[896,512]{1,0:T(8,128)(2,1)S(1)}, bf16[896,512]{1,0:T(8,128)(2,1)S(1)}, u32[]{:S(2)}, u32[]{:S(2)}) collective-permute-start(bf16[896,512]{1,0:T(8,128)(2,1)S(1)} %shard_map.90), channel_id=1, source_target_pairs={{0,48},{1,49},{2,50},{3,51},{4,52},{5,53},{6,54},{7,55},{8,73},{9,... | collective-permute-start | bytes 2752520 | tf_op jit(solution)/shard_map/ppermute | solution.py:48
  40.5 1.7 %collective-permute-done.7.refs_1_ = bf16[896,512]{1,0:T(8,128)(2,1)S(1)} collective-permute-done((bf16[896,512]{1,0:T(8,128)(2,1)S(1)}, bf16[896,512]{1,0:T(8,128)(2,1)S(1)}, u32[]{:S(2)}, u32[]{:S(2)}) %collective-permute-start.7) | collective-permute-done | bytes 917536 | tf_op jit(solution)/shard_map/ppermute | solution.py:48
  42.2 0.2 shard_map.83
  42.3 1.7 %collective-permute-start.8 = (bf16[448,512]{1,0:T(8,128)(2,1)S(1)}, bf16[448,512]{1,0:T(8,128)(2,1)S(1)}, u32[]{:S(2)}, u32[]{:S(2)}) collective-permute-start(bf16[448,512]{1,0:T(8,128)(2,1)S(1)} %get-tuple-element.53), channel_id=1, source_target_pairs={{0,64},{1,65},{2,66},{3,67},{4,68},{5,69},{6,70},{7,71},{8,24},{9,... | collective-permute-start | bytes 1376264 | tf_op jit(solution)/shard_map/ppermute | solution.py:48
  44.0 1.1 %shard_map.89.refs_0_ = f32[896,512]{1,0:T(8,128)S(1)} custom-call(bf16[1792,512]{1,0:T(8,128)(2,1)S(1)} %get-tuple-element.43.refs_0_, bf16[256,512]{1,0:T(8,128)(2,1)S(1)} %get-tuple-element.61.refs_1_, bf16[256,512]{1,0:T(8,128)(2,1)S(1)} %get-tuple-element.62.refs_2_, bf16[256,512]{1,0:T(8,128)(2,1)S(1)} %collective-permute-done.13.refs_3_, ...), custom_call_target="tpu_custom_call" | custom-call | flops 939524096 | bytes 1835008 | tf_op jit(solution)/shard_map/pallas_call | solution.py:222
  45.1 5.8 %collective-permute-done.8.refs_1_ = bf16[448,512]{1,0:T(8,128)(2,1)S(1)} collective-permute-done((bf16[448,512]{1,0:T(8,128)(2,1)S(1)}, bf16[448,512]{1,0:T(8,128)(2,1)S(1)}, u32[]{:S(2)}, u32[]{:S(2)}) %collective-permute-start.8) | collective-permute-done | bytes 458784 | tf_op jit(solution)/shard_map/ppermute | solution.py:48
  50.9 0.1 shard_map.84
  51.0 0.9 %collective-permute-done.15.refs_1_ = bf16[896,512]{1,0:T(8,128)(2,1)S(1)} collective-permute-done((bf16[896,512]{1,0:T(8,128)(2,1)S(1)}, bf16[896,512]{1,0:T(8,128)(2,1)S(1)}, u32[]{:S(2)}, u32[]{:S(2)}) %collective-permute-start.15) | collective-permute-done | bytes 917536 | tf_op jit(solution)/shard_map/ppermute | solution.py:48
  51.8 0.2 shard_map.91
  52.0 0.0 copy-start.3
  52.0 0.0 copy-start.4
  52.0 1.1 %collective-permute-start.16 = (bf16[448,512]{1,0:T(8,128)(2,1)S(1)}, bf16[448,512]{1,0:T(8,128)(2,1)S(1)}, u32[]{:S(2)}, u32[]{:S(2)}) collective-permute-start(bf16[448,512]{1,0:T(8,128)(2,1)S(1)} %get-tuple-element.64), channel_id=1, source_target_pairs={{0,16},{1,17},{2,18},{3,19},{4,20},{5,21},{6,22},{7,23},{8,72},{9,... | collective-permute-start | bytes 1376264 | tf_op jit(solution)/shard_map/ppermute | solution.py:48
  53.2 2.5 %collective-permute-start.9 = (bf16[224,512]{1,0:T(8,128)(2,1)S(1)}, bf16[224,512]{1,0:T(8,128)(2,1)S(1)}, u32[]{:S(2)}, u32[]{:S(2)}) collective-permute-start(bf16[224,512]{1,0:T(8,128)(2,1)S(1)} %get-tuple-element.55.refs_2_), channel_id=1, source_target_pairs={{0,48},{1,49},{2,50},{3,51},{4,52},{5,53},{6,54},{7,55},{8,73},{9,... | collective-permute-start | bytes 688136 | tf_op jit(solution)/shard_map/ppermute | solution.py:48
  55.7 4.9 %collective-permute-done.16.refs_1_ = bf16[448,512]{1,0:T(8,128)(2,1)S(1)} collective-permute-done((bf16[448,512]{1,0:T(8,128)(2,1)S(1)}, bf16[448,512]{1,0:T(8,128)(2,1)S(1)}, u32[]{:S(2)}, u32[]{:S(2)}) %collective-permute-start.16) | collective-permute-done | bytes 458784 | tf_op jit(solution)/shard_map/ppermute | solution.py:48
  60.6 0.1 shard_map.92
  60.7 2.0 %collective-permute-start.17 = (bf16[224,512]{1,0:T(8,128)(2,1)S(1)}, bf16[224,512]{1,0:T(8,128)(2,1)S(1)}, u32[]{:S(2)}, u32[]{:S(2)}) collective-permute-start(bf16[224,512]{1,0:T(8,128)(2,1)S(1)} %get-tuple-element.66), channel_id=1, source_target_pairs={{0,64},{1,65},{2,66},{3,67},{4,68},{5,69},{6,70},{7,71},{8,24},{9,... | collective-permute-start | bytes 688136 | tf_op jit(solution)/shard_map/ppermute | solution.py:48
  62.7 2.0 %collective-permute-start.10 = (bf16[112,512]{1,0:T(8,128)(2,1)S(1)}, bf16[112,512]{1,0:T(8,128)(2,1)S(1)}, u32[]{:S(2)}, u32[]{:S(2)}) collective-permute-start(bf16[112,512]{1,0:T(8,128)(2,1)S(1)} %get-tuple-element.57), channel_id=1, source_target_pairs={{0,65},{1,64},{2,67},{3,66},{4,69},{5,68},{6,71},{7,70},{8,56},{9,... | collective-permute-start | bytes 344072 | tf_op jit(solution)/shard_map/ppermute | solution.py:48
  64.6 2.1 %collective-permute-done.17.refs_1_ = bf16[224,512]{1,0:T(8,128)(2,1)S(1)} collective-permute-done((bf16[224,512]{1,0:T(8,128)(2,1)S(1)}, bf16[224,512]{1,0:T(8,128)(2,1)S(1)}, u32[]{:S(2)}, u32[]{:S(2)}) %collective-permute-start.17) | collective-permute-done | bytes 229408 | tf_op jit(solution)/shard_map/ppermute | solution.py:48
  66.8 3.1 %collective-permute-start.18 = (bf16[112,512]{1,0:T(8,128)(2,1)S(1)}, bf16[112,512]{1,0:T(8,128)(2,1)S(1)}, u32[]{:S(2)}, u32[]{:S(2)}) collective-permute-start(bf16[112,512]{1,0:T(8,128)(2,1)S(1)} %get-tuple-element.67.refs_4_), channel_id=1, source_target_pairs={{0,65},{1,64},{2,67},{3,66},{4,69},{5,68},{6,71},{7,70},{8,56},{9,... | collective-permute-start | bytes 344072 | tf_op jit(solution)/shard_map/ppermute | solution.py:48
  69.9 0.2 shard_map.94
  70.1 1.3 %collective-permute-start.21 = (bf16[112,512]{1,0:T(8,128)(2,1)S(1)}, bf16[112,512]{1,0:T(8,128)(2,1)S(1)}, u32[]{:S(2)}, u32[]{:S(2)}) collective-permute-start(bf16[112,512]{1,0:T(8,128)(2,1)S(1)} %get-tuple-element.74.own), channel_id=1, source_target_pairs={{0,2},{1,3},{2,0},{3,1},{4,6},{5,7},{6,4},{7,5},{8,14},{9,15},{10,... | collective-permute-start | bytes 344072 | tf_op jit(solution)/shard_map/ppermute | solution.py:48
  71.4 1.5 %collective-permute-done.18.refs_1_ = bf16[112,512]{1,0:T(8,128)(2,1)S(1)} collective-permute-done((bf16[112,512]{1,0:T(8,128)(2,1)S(1)}, bf16[112,512]{1,0:T(8,128)(2,1)S(1)}, u32[]{:S(2)}, u32[]{:S(2)}) %collective-permute-start.18) | collective-permute-done | bytes 114720 | tf_op jit(solution)/shard_map/ppermute | solution.py:48
  72.9 0.2 shard_map.95
  73.1 1.4 %collective-permute-start.19 = (bf16[112,512]{1,0:T(8,128)(2,1)S(1)}, bf16[112,512]{1,0:T(8,128)(2,1)S(1)}, u32[]{:S(2)}, u32[]{:S(2)}) collective-permute-start(bf16[112,512]{1,0:T(8,128)(2,1)S(1)} %get-tuple-element.73.own), channel_id=1, source_target_pairs={{0,2},{1,3},{2,0},{3,1},{4,6},{5,7},{6,4},{7,5},{8,14},{9,15},{10,... | collective-permute-start | bytes 344072 | tf_op jit(solution)/shard_map/ppermute | solution.py:48
  74.5 0.5 collective-permute-done.21.got
  75.0 2.8 %collective-permute-start.22 = (bf16[224,512]{1,0:T(8,128)(2,1)S(1)}, bf16[224,512]{1,0:T(8,128)(2,1)S(1)}, u32[]{:S(2)}, u32[]{:S(2)}) collective-permute-start(bf16[224,512]{1,0:T(8,128)(2,1)S(1)} %shard_map.97.refs_1_), channel_id=1, source_target_pairs={{0,6},{1,7},{2,4},{3,5},{4,2},{5,3},{6,0},{7,1},{8,10},{9,11},{10,... | collective-permute-start | bytes 688136 | tf_op jit(solution)/shard_map/ppermute | solution.py:48
  77.9 1.4 %collective-permute-done.19.got = bf16[112,512]{1,0:T(8,128)(2,1)S(1)} collective-permute-done((bf16[112,512]{1,0:T(8,128)(2,1)S(1)}, bf16[112,512]{1,0:T(8,128)(2,1)S(1)}, u32[]{:S(2)}, u32[]{:S(2)}) %collective-permute-start.19) | collective-permute-done | bytes 114720 | tf_op jit(solution)/shard_map/ppermute | solution.py:48
  79.3 2.8 %collective-permute-start.20 = (bf16[224,512]{1,0:T(8,128)(2,1)S(1)}, bf16[224,512]{1,0:T(8,128)(2,1)S(1)}, u32[]{:S(2)}, u32[]{:S(2)}) collective-permute-start(bf16[224,512]{1,0:T(8,128)(2,1)S(1)} %shard_map.96.refs_2_), channel_id=1, source_target_pairs={{0,6},{1,7},{2,4},{3,5},{4,2},{5,3},{6,0},{7,1},{8,10},{9,11},{10,... | collective-permute-start | bytes 688136 | tf_op jit(solution)/shard_map/ppermute | solution.py:48
  82.1 1.0 %maximum_bitcast_fusion = (f32[1,112,1024]{2,1,0:T(8,128)}, f32[1,112,1024]{2,1,0:T(8,128)}) fusion(f32[112,512]{1,0:T(8,128)S(1)} %get-tuple-element.70, f32[112,512]{1,0:T(8,128)S(1)} %get-tuple-element.68, f32[112,512]{1,0:T(8,128)S(1)} %get-tuple-element.72, f32[112,512]{1,0:T(8,128)S(1)} %get-tuple-element.71), kind=kLoop, calls=%fused_computation | loop fusion | flops 229376 | bytes 1835008 | tf_op jit(solution)/shard_map/reshape | solution.py:344
  83.1 1.1 %shard_map.98.refs_3_ = f32[448,2048]{1,0:T(8,128)S(1)} custom-call(bf16[1024,2048]{1,0:T(8,128)(2,1)S(1)} %shard_map.86.refs_0_.refs_1_, bf16[224,512]{1,0:T(8,128)(2,1)S(1)} %shard_map.97.refs_1_, bf16[224,512]{1,0:T(8,128)(2,1)S(1)} %collective-permute-done.22.refs_2_), custom_call_target="tpu_custom_call" | custom-call | flops 939524096 | bytes 5767168 | tf_op jit(solution)/shard_map/pallas_call | solution.py:222
  84.3 1.9 %shard_map.99.refs_4_ = bf16[4,112,2048]{2,1,0:T(8,128)(2,1)} custom-call(s32[4]{0:T(128)S(1)} %pad_add_fusion.refs_2_.pos.refs_0_, bf16[1024,2048]{1,0:T(8,128)(2,1)S(1)} %shard_map.86.refs_0_.refs_1_, bf16[224,512]{1,0:T(8,128)(2,1)S(1)} %shard_map.96.refs_2_, f32[448,2048]{1,0:T(8,128)S(1)} %shard_map.98.refs_3_), custom_call_target="tpu_custom_call" | custom-call | flops 469762048 | bytes 2097152 | tf_op jit(solution)/shard_map/pallas_call | solution.py:331
  86.2 0.4 collective-permute-done.20.refs_2_
  86.6 1.9 %shard_map.100 = bf16[4,112,2048]{2,1,0:T(8,128)(2,1)} custom-call(s32[4]{0:T(128)S(1)} %pad_add_fusion.refs_2_.pos.refs_0_, bf16[1024,2048]{1,0:T(8,128)(2,1)S(1)} %shard_map.86.refs_0_.refs_1_, bf16[224,512]{1,0:T(8,128)(2,1)S(1)} %collective-permute-done.20.refs_2_, f32[448,2048]{1,0:T(8,128)S(1)} %shard_map.98.refs_3_, ...), custom_call_target="tpu_custom_call", output_to_operand_aliasing={{}: (4, {})} | custom-call | flops 469762048 | bytes 2097152 | tf_op jit(solution)/shard_map/pallas_call | solution.py:331
  (20 shorter events, 0.2 us)
Async XLA Ops:
  0.7 2.2 %copy-start.1 = (bf16[512,2048]{1,0:T(8,128)(2,1)S(1)}, bf16[512,2048]{1,0:T(8,128)(2,1)}, u32[]{:S(2)}) copy-start(bf16[512,2048]{1,0:T(8,128)(2,1)} %refs_0_.3) | copy-start | bytes 6291460
  3.0 3.0 %copy-start = (bf16[2048,1024]{1,0:T(8,128)(2,1)S(1)}, bf16[2048,1024]{1,0:T(8,128)(2,1)}, u32[]{:S(2)}) copy-start(bf16[2048,1024]{1,0:T(8,128)(2,1)} %projection.1) | copy-start | bytes 12582916
  4.4 9.3 %collective-permute-start = (bf16[512,512]{1,0:T(8,128)(2,1)S(1)}, bf16[512,512]{1,0:T(8,128)(2,1)S(1)}, u32[]{:S(2)}, u32[]{:S(2)}) collective-permute-start(bf16[512,512]{1,0:T(8,128)(2,1)S(1)} %get-tuple-element.44), channel_id=1, source_target_pairs={{0,2},{1,3},{2,0},{3,1},{4,6},{5,7},{6,4},{7,5},{8,14},{9,15},{10,... | collective-permute-start | bytes 1572872 | tf_op jit(solution)/shard_map/ppermute | solution.py:48
  6.0 2.2 %copy-start.2 = (bf16[512,3584]{1,0:T(8,128)(2,1)S(1)}, bf16[512,3584]{1,0:T(8,128)(2,1)}, u32[]{:S(2)}) copy-start(bf16[512,3584]{1,0:T(8,128)(2,1)} %hidden.1) | copy-start | bytes 11010052
  7.4 14.2 %collective-permute-start.11 = (bf16[512,512]{1,0:T(8,128)(2,1)S(1)}, bf16[512,512]{1,0:T(8,128)(2,1)S(1)}, u32[]{:S(2)}, u32[]{:S(2)}) collective-permute-start(bf16[512,512]{1,0:T(8,128)(2,1)S(1)} %get-tuple-element.58), channel_id=1, source_target_pairs={{0,2},{1,3},{2,0},{3,1},{4,6},{5,7},{6,4},{7,5},{8,14},{9,15},{10,... | collective-permute-start | bytes 1572872 | tf_op jit(solution)/shard_map/ppermute | solution.py:48
  10.0 15.7 %collective-permute-start.5 = (bf16[560,512]{1,0:T(8,128)(2,1)S(1)}, bf16[560,512]{1,0:T(8,128)(2,1)S(1)}, u32[]{:S(2)}, u32[]{:S(2)}) collective-permute-start(bf16[560,512]{1,0:T(8,128)(2,1)S(1)} %get-tuple-element.50), channel_id=1, source_target_pairs={{0,8},{1,9},{2,10},{3,11},{4,12},{5,13},{6,14},{7,15},{8,0},{9,1},... | collective-permute-start | bytes 1720328 | tf_op jit(solution)/shard_map/ppermute | solution.py:48
  14.3 10.8 %collective-permute-start.1 = (bf16[512,512]{1,0:T(8,128)(2,1)S(1)}, bf16[512,512]{1,0:T(8,128)(2,1)S(1)}, u32[]{:S(2)}, u32[]{:S(2)}) collective-permute-start(bf16[512,512]{1,0:T(8,128)(2,1)S(1)} %get-tuple-element.46._), channel_id=1, source_target_pairs={{0,6},{1,7},{2,4},{3,5},{4,2},{5,3},{6,0},{7,1},{8,10},{9,11},{10,... | collective-permute-start | bytes 1572872 | tf_op jit(solution)/shard_map/ppermute | solution.py:48
  17.2 8.9 %collective-permute-start.4 = (bf16[672,512]{1,0:T(8,128)(2,1)S(1)}, bf16[672,512]{1,0:T(8,128)(2,1)S(1)}, u32[]{:S(2)}, u32[]{:S(2)}) collective-permute-start(bf16[672,512]{1,0:T(8,128)(2,1)S(1)} %get-tuple-element.49), channel_id=1, source_target_pairs={{0,8},{1,9},{2,10},{3,11},{4,12},{5,13},{6,14},{7,15},{8,0},{9,1},... | collective-permute-start | bytes 2064392 | tf_op jit(solution)/shard_map/ppermute | solution.py:48
  17.2 8.9 %collective-permute-start.6 = (bf16[560,512]{1,0:T(8,128)(2,1)S(1)}, bf16[560,512]{1,0:T(8,128)(2,1)S(1)}, u32[]{:S(2)}, u32[]{:S(2)}) collective-permute-start(bf16[560,512]{1,0:T(8,128)(2,1)S(1)} %get-tuple-element.51), channel_id=1, source_target_pairs={{0,8},{1,9},{2,10},{3,11},{4,12},{5,13},{6,14},{7,15},{8,0},{9,1},... | collective-permute-start | bytes 1720328 | tf_op jit(solution)/shard_map/ppermute | solution.py:48
  22.3 10.5 %collective-permute-start.12 = (bf16[512,512]{1,0:T(8,128)(2,1)S(1)}, bf16[512,512]{1,0:T(8,128)(2,1)S(1)}, u32[]{:S(2)}, u32[]{:S(2)}) collective-permute-start(bf16[512,512]{1,0:T(8,128)(2,1)S(1)} %get-tuple-element.60), channel_id=1, source_target_pairs={{0,6},{1,7},{2,4},{3,5},{4,2},{5,3},{6,0},{7,1},{8,10},{9,11},{10,... | collective-permute-start | bytes 1572872 | tf_op jit(solution)/shard_map/ppermute | solution.py:48
  25.6 1.6 %collective-permute-start.2 = (bf16[256,512]{1,0:T(8,128)(2,1)S(1)}, bf16[256,512]{1,0:T(8,128)(2,1)S(1)}, u32[]{:S(2)}, u32[]{:S(2)}) collective-permute-start(bf16[256,512]{1,0:T(8,128)(2,1)S(1)} %get-tuple-element.47.refs_1_), channel_id=1, source_target_pairs={{0,8},{1,9},{2,10},{3,11},{4,12},{5,13},{6,14},{7,15},{8,0},{9,1},... | collective-permute-start | bytes 786440 | tf_op jit(solution)/shard_map/ppermute | solution.py:48
  25.7 1.9 %collective-permute-start.3 = (bf16[256,512]{1,0:T(8,128)(2,1)S(1)}, bf16[256,512]{1,0:T(8,128)(2,1)S(1)}, u32[]{:S(2)}, u32[]{:S(2)}) collective-permute-start(bf16[256,512]{1,0:T(8,128)(2,1)S(1)} %get-tuple-element.48.refs_2_), channel_id=1, source_target_pairs={{0,8},{1,9},{2,10},{3,11},{4,12},{5,13},{6,14},{7,15},{8,0},{9,1},... | collective-permute-start | bytes 786440 | tf_op jit(solution)/shard_map/ppermute | solution.py:48
  28.7 13.5 %collective-permute-start.7 = (bf16[896,512]{1,0:T(8,128)(2,1)S(1)}, bf16[896,512]{1,0:T(8,128)(2,1)S(1)}, u32[]{:S(2)}, u32[]{:S(2)}) collective-permute-start(bf16[896,512]{1,0:T(8,128)(2,1)S(1)} %shard_map.82.refs_0_), channel_id=1, source_target_pairs={{0,16},{1,17},{2,18},{3,19},{4,20},{5,21},{6,22},{7,23},{8,72},{9,... | collective-permute-start | bytes 2752520 | tf_op jit(solution)/shard_map/ppermute | solution.py:48
  33.2 1.7 %collective-permute-start.13 = (bf16[256,512]{1,0:T(8,128)(2,1)S(1)}, bf16[256,512]{1,0:T(8,128)(2,1)S(1)}, u32[]{:S(2)}, u32[]{:S(2)}) collective-permute-start(bf16[256,512]{1,0:T(8,128)(2,1)S(1)} %get-tuple-element.61.refs_1_), channel_id=1, source_target_pairs={{0,8},{1,9},{2,10},{3,11},{4,12},{5,13},{6,14},{7,15},{8,0},{9,1},... | collective-permute-start | bytes 786440 | tf_op jit(solution)/shard_map/ppermute | solution.py:48
  33.3 1.9 %collective-permute-start.14 = (bf16[256,512]{1,0:T(8,128)(2,1)S(1)}, bf16[256,512]{1,0:T(8,128)(2,1)S(1)}, u32[]{:S(2)}, u32[]{:S(2)}) collective-permute-start(bf16[256,512]{1,0:T(8,128)(2,1)S(1)} %get-tuple-element.62.refs_2_), channel_id=1, source_target_pairs={{0,8},{1,9},{2,10},{3,11},{4,12},{5,13},{6,14},{7,15},{8,0},{9,1},... | collective-permute-start | bytes 786440 | tf_op jit(solution)/shard_map/ppermute | solution.py:48
  36.4 15.5 %collective-permute-start.15 = (bf16[896,512]{1,0:T(8,128)(2,1)S(1)}, bf16[896,512]{1,0:T(8,128)(2,1)S(1)}, u32[]{:S(2)}, u32[]{:S(2)}) collective-permute-start(bf16[896,512]{1,0:T(8,128)(2,1)S(1)} %shard_map.90), channel_id=1, source_target_pairs={{0,48},{1,49},{2,50},{3,51},{4,52},{5,53},{6,54},{7,55},{8,73},{9,... | collective-permute-start | bytes 2752520 | tf_op jit(solution)/shard_map/ppermute | solution.py:48
  42.3 8.6 %collective-permute-start.8 = (bf16[448,512]{1,0:T(8,128)(2,1)S(1)}, bf16[448,512]{1,0:T(8,128)(2,1)S(1)}, u32[]{:S(2)}, u32[]{:S(2)}) collective-permute-start(bf16[448,512]{1,0:T(8,128)(2,1)S(1)} %get-tuple-element.53), channel_id=1, source_target_pairs={{0,64},{1,65},{2,66},{3,67},{4,68},{5,69},{6,70},{7,71},{8,24},{9,... | collective-permute-start | bytes 1376264 | tf_op jit(solution)/shard_map/ppermute | solution.py:48
  52.0 17.9 %copy-start.3 = (f32[1,112,1024]{2,1,0:T(8,128)S(1)}, f32[1,112,1024]{2,1,0:T(8,128)}, u32[]{:S(2)}) copy-start(f32[1,112,1024]{2,1,0:T(8,128)} %refs_2_.3) | copy-start | bytes 1376260
  52.0 17.9 %copy-start.4 = (f32[1,112,1024]{2,1,0:T(8,128)S(1)}, f32[1,112,1024]{2,1,0:T(8,128)}, u32[]{:S(2)}) copy-start(f32[1,112,1024]{2,1,0:T(8,128)} %refs_3_.3) | copy-start | bytes 1376260
  52.0 8.6 %collective-permute-start.16 = (bf16[448,512]{1,0:T(8,128)(2,1)S(1)}, bf16[448,512]{1,0:T(8,128)(2,1)S(1)}, u32[]{:S(2)}, u32[]{:S(2)}) collective-permute-start(bf16[448,512]{1,0:T(8,128)(2,1)S(1)} %get-tuple-element.64), channel_id=1, source_target_pairs={{0,16},{1,17},{2,18},{3,19},{4,20},{5,21},{6,22},{7,23},{8,72},{9,... | collective-permute-start | bytes 1376264 | tf_op jit(solution)/shard_map/ppermute | solution.py:48
  53.2 9.5 %collective-permute-start.9 = (bf16[224,512]{1,0:T(8,128)(2,1)S(1)}, bf16[224,512]{1,0:T(8,128)(2,1)S(1)}, u32[]{:S(2)}, u32[]{:S(2)}) collective-permute-start(bf16[224,512]{1,0:T(8,128)(2,1)S(1)} %get-tuple-element.55.refs_2_), channel_id=1, source_target_pairs={{0,48},{1,49},{2,50},{3,51},{4,52},{5,53},{6,54},{7,55},{8,73},{9,... | collective-permute-start | bytes 688136 | tf_op jit(solution)/shard_map/ppermute | solution.py:48
  60.7 6.1 %collective-permute-start.17 = (bf16[224,512]{1,0:T(8,128)(2,1)S(1)}, bf16[224,512]{1,0:T(8,128)(2,1)S(1)}, u32[]{:S(2)}, u32[]{:S(2)}) collective-permute-start(bf16[224,512]{1,0:T(8,128)(2,1)S(1)} %get-tuple-element.66), channel_id=1, source_target_pairs={{0,64},{1,65},{2,66},{3,67},{4,68},{5,69},{6,70},{7,71},{8,24},{9,... | collective-permute-start | bytes 688136 | tf_op jit(solution)/shard_map/ppermute | solution.py:48
  62.7 7.2 %collective-permute-start.10 = (bf16[112,512]{1,0:T(8,128)(2,1)S(1)}, bf16[112,512]{1,0:T(8,128)(2,1)S(1)}, u32[]{:S(2)}, u32[]{:S(2)}) collective-permute-start(bf16[112,512]{1,0:T(8,128)(2,1)S(1)} %get-tuple-element.57), channel_id=1, source_target_pairs={{0,65},{1,64},{2,67},{3,66},{4,69},{5,68},{6,71},{7,70},{8,56},{9,... | collective-permute-start | bytes 344072 | tf_op jit(solution)/shard_map/ppermute | solution.py:48
  66.8 6.1 %collective-permute-start.18 = (bf16[112,512]{1,0:T(8,128)(2,1)S(1)}, bf16[112,512]{1,0:T(8,128)(2,1)S(1)}, u32[]{:S(2)}, u32[]{:S(2)}) collective-permute-start(bf16[112,512]{1,0:T(8,128)(2,1)S(1)} %get-tuple-element.67.refs_4_), channel_id=1, source_target_pairs={{0,65},{1,64},{2,67},{3,66},{4,69},{5,68},{6,71},{7,70},{8,56},{9,... | collective-permute-start | bytes 344072 | tf_op jit(solution)/shard_map/ppermute | solution.py:48
  70.1 4.9 %collective-permute-start.21 = (bf16[112,512]{1,0:T(8,128)(2,1)S(1)}, bf16[112,512]{1,0:T(8,128)(2,1)S(1)}, u32[]{:S(2)}, u32[]{:S(2)}) collective-permute-start(bf16[112,512]{1,0:T(8,128)(2,1)S(1)} %get-tuple-element.74.own), channel_id=1, source_target_pairs={{0,2},{1,3},{2,0},{3,1},{4,6},{5,7},{6,4},{7,5},{8,14},{9,15},{10,... | collective-permute-start | bytes 344072 | tf_op jit(solution)/shard_map/ppermute | solution.py:48
  73.1 6.2 %collective-permute-start.19 = (bf16[112,512]{1,0:T(8,128)(2,1)S(1)}, bf16[112,512]{1,0:T(8,128)(2,1)S(1)}, u32[]{:S(2)}, u32[]{:S(2)}) collective-permute-start(bf16[112,512]{1,0:T(8,128)(2,1)S(1)} %get-tuple-element.73.own), channel_id=1, source_target_pairs={{0,2},{1,3},{2,0},{3,1},{4,6},{5,7},{6,4},{7,5},{8,14},{9,15},{10,... | collective-permute-start | bytes 344072 | tf_op jit(solution)/shard_map/ppermute | solution.py:48
  75.0 8.1 %collective-permute-start.22 = (bf16[224,512]{1,0:T(8,128)(2,1)S(1)}, bf16[224,512]{1,0:T(8,128)(2,1)S(1)}, u32[]{:S(2)}, u32[]{:S(2)}) collective-permute-start(bf16[224,512]{1,0:T(8,128)(2,1)S(1)} %shard_map.97.refs_1_), channel_id=1, source_target_pairs={{0,6},{1,7},{2,4},{3,5},{4,2},{5,3},{6,0},{7,1},{8,10},{9,11},{10,... | collective-permute-start | bytes 688136 | tf_op jit(solution)/shard_map/ppermute | solution.py:48
  79.3 7.3 %collective-permute-start.20 = (bf16[224,512]{1,0:T(8,128)(2,1)S(1)}, bf16[224,512]{1,0:T(8,128)(2,1)S(1)}, u32[]{:S(2)}, u32[]{:S(2)}) collective-permute-start(bf16[224,512]{1,0:T(8,128)(2,1)S(1)} %shard_map.96.refs_2_), channel_id=1, source_target_pairs={{0,6},{1,7},{2,4},{3,5},{4,2},{5,3},{6,0},{7,1},{8,10},{9,11},{10,... | collective-permute-start | bytes 688136 | tf_op jit(solution)/shard_map/ppermute | solution.py:48

commit v4 on v3

--- a/solution.py
+++ b/solution.py
@@ -19,7 +19,7 @@
 SHARES = 2
 N = 4
 ROWS = 112
-SCALE = 2.0**22
+SCALE = 2.0**50
 LEAST = 2.0**-126
 VMEM = pl.BlockSpec(memory_space=pltpu.VMEM)
 SMEM = pl.BlockSpec(memory_space=pltpu.SMEM)
@@ -67,14 +67,12 @@
 
 def encode(value):
     value = value * SCALE
-    square = value * value
-    return jnp.where(value < 0, -square * square, square * square).astype(BF16)
+    return (value * jnp.abs(value)).astype(BF16)
 
 
 def decode(code):
     code = code.astype(F32)
-    root = lax.rsqrt(lax.rsqrt(jnp.maximum(jnp.abs(code), LEAST))) * (1.0 / SCALE)
-    return jnp.where(code < 0, -root, jnp.where(code > 0, root, 0.0))
+    return code * lax.rsqrt(jnp.maximum(jnp.abs(code), LEAST)) * (1.0 / SCALE)
 
 
 def turn_kernel(pos, hidden, _, mine, *refs):

time: 88.8 us -> 88.6 us (level)
  Pallas kernels: 18.5 us -> 17.4 us
    pallas_call x23, Pallas kernels: 14.6 us -> 13.5 us  [run(): pl.pallas_call(kernel, out_shape=[jax.ShapeDtypeStruct(s, t) for s, t in...]
  transfers between devices with their start and end apart: 23 -> 23, of which waited for: 15 -> 15; matrix products, arithmetic and copies ran while one was open for 1% -> 1% of each run, Pallas kernels for 17% -> 16%
where the time goes in v4:
time: 88.6 us; the launch traced here: 88.4 us
  starting transfers between devices  37.9 us (43%)
  waiting for transfers between devices  28.8 us (33%)
  Pallas kernels  17.4 us (20%)
  local copies, waits for them, and re-layouts  2.24 us (3%)
  other arithmetic  1.07 us (1%)
  between operations  1.03 us (1%)
    ppermute x23, starting transfers between devices, exchange(): return lax.ppermute(array, AXES, pairs)  37.9 us
    ppermute x23, waiting for transfers between devices, exchange(): return lax.ppermute(array, AXES, pairs)  28.8 us
    pallas_call x23, Pallas kernels, run(): pl.pallas_call(kernel, out_shape=[jax.ShapeDtypeStruct(s, t) for s, t in...  13.5 us
    pallas_call x2, Pallas kernels, local(): pl.pallas_call(lambda *refs, far=far: finish_kernel(STARTS[1], far, *refs...  3.89 us
    slice x1, local copies, waits for them, and re-layouts, local(): first_columns = first_columns[:, :WIDTHS[0]]  1.88 us
  transfers between devices with their start and end apart: 23, of which 15 were waited for; matrix products, arithmetic and copies ran while one was open for 1% of the time, Pallas kernels for 16%

profile of v4, /device:TPU:0, one launch (start us, length us, event | category | flops | bytes accessed | tf_op | source)
XLA Modules:
  0.0 88.4 jit_solution(12405575732268621386)
XLA Ops:
  0.7 0.1 pad_add_fusion.refs_2_.pos.refs_0_
  0.8 1.9 %slice.3.refs_1_ = bf16[2048,512]{1,0:T(8,128)(2,1)S(1)} slice(bf16[2048,1024]{1,0:T(8,128)(2,1)} %projection.1), slice={[0:2048], [0:512]} | slice | bytes 4194304 | tf_op jit(solution)/shard_map/slice | solution.py:243
  2.6 0.3 copy-done.1
  3.0 1.3 %shard_map.76 = (f32[512,512]{1,0:T(8,128)S(1)}, bf16[512,512]{1,0:T(8,128)(2,1)S(1)}) custom-call(bf16[512,2048]{1,0:T(8,128)(2,1)S(1)} %copy-done.1, bf16[2048,512]{1,0:T(8,128)(2,1)S(1)} %slice.3.refs_1_, s32[4]{0:T(128)S(1)} %pad_add_fusion.refs_2_.pos.refs_0_), custom_call_target="tpu_custom_call" | custom-call | flops 1073741824 | bytes 4194304 | tf_op jit(solution)/shard_map/pallas_call | solution.py:220
  4.2 1.7 %collective-permute-start = (bf16[512,512]{1,0:T(8,128)(2,1)S(1)}, bf16[512,512]{1,0:T(8,128)(2,1)S(1)}, u32[]{:S(2)}, u32[]{:S(2)}) collective-permute-start(bf16[512,512]{1,0:T(8,128)(2,1)S(1)} %get-tuple-element.44), channel_id=1, source_target_pairs={{0,2},{1,3},{2,0},{3,1},{4,6},{5,7},{6,4},{7,5},{8,14},{9,15},{10,... | collective-permute-start | bytes 1572872 | tf_op jit(solution)/shard_map/ppermute | solution.py:48
  5.9 1.2 %shard_map.77 = (f32[512,512]{1,0:T(8,128)S(1)}, bf16[512,512]{1,0:T(8,128)(2,1)S(1)}) custom-call(bf16[512,2048]{1,0:T(8,128)(2,1)S(1)} %copy-done.1, bf16[2048,1024]{1,0:T(8,128)(2,1)S(1)} %copy-done, f32[512,512]{1,0:T(8,128)S(1)} %get-tuple-element.41.refs_2_.total), custom_call_target="tpu_custom_call" | custom-call | flops 1073741824 | bytes 4194304 | tf_op jit(solution)/shard_map/pallas_call | solution.py:220
  7.2 0.9 %collective-permute-start.11 = (bf16[512,512]{1,0:T(8,128)(2,1)S(1)}, bf16[512,512]{1,0:T(8,128)(2,1)S(1)}, u32[]{:S(2)}, u32[]{:S(2)}) collective-permute-start(bf16[512,512]{1,0:T(8,128)(2,1)S(1)} %get-tuple-element.58), channel_id=1, source_target_pairs={{0,2},{1,3},{2,0},{3,1},{4,6},{5,7},{6,4},{7,5},{8,14},{9,15},{10,... | collective-permute-start | bytes 1572872 | tf_op jit(solution)/shard_map/ppermute | solution.py:48
  8.1 1.8 %shard_map.78 = (bf16[1792,512]{1,0:T(8,128)(2,1)S(1)}, bf16[672,512]{1,0:T(8,128)(2,1)S(1)}, bf16[560,512]{1,0:T(8,128)(2,1)S(1)}, bf16[560,512]{1,0:T(8,128)(2,1)S(1)}) custom-call(s32[4]{0:T(128)S(1)} %pad_add_fusion.refs_2_.pos.refs_0_, bf16[512,3584]{1,0:T(8,128)(2,1)S(1)} %copy-done.2, f32[512,512]{1,0:T(8,128)S(1)} %get-tuple-element.42._.total), custom_call_target="tpu_custom_call" | custom-call | bytes 7340032 | tf_op jit(solution)/shard_map/pallas_call | solution.py:220
  9.9 0.9 %collective-permute-start.5 = (bf16[560,512]{1,0:T(8,128)(2,1)S(1)}, bf16[560,512]{1,0:T(8,128)(2,1)S(1)}, u32[]{:S(2)}, u32[]{:S(2)}) collective-permute-start(bf16[560,512]{1,0:T(8,128)(2,1)S(1)} %get-tuple-element.50), channel_id=1, source_target_pairs={{0,8},{1,9},{2,10},{3,11},{4,12},{5,13},{6,14},{7,15},{8,0},{9,1},... | collective-permute-start | bytes 1720328 | tf_op jit(solution)/shard_map/ppermute | solution.py:48
  10.8 2.7 %collective-permute-done.got = bf16[512,512]{1,0:T(8,128)(2,1)S(1)} collective-permute-done((bf16[512,512]{1,0:T(8,128)(2,1)S(1)}, bf16[512,512]{1,0:T(8,128)(2,1)S(1)}, u32[]{:S(2)}, u32[]{:S(2)}) %collective-permute-start) | collective-permute-done | bytes 524320 | tf_op jit(solution)/shard_map/ppermute | solution.py:48
  13.5 0.4 shard_map.79
  13.9 2.9 %collective-permute-start.1 = (bf16[512,512]{1,0:T(8,128)(2,1)S(1)}, bf16[512,512]{1,0:T(8,128)(2,1)S(1)}, u32[]{:S(2)}, u32[]{:S(2)}) collective-permute-start(bf16[512,512]{1,0:T(8,128)(2,1)S(1)} %get-tuple-element.46._), channel_id=1, source_target_pairs={{0,6},{1,7},{2,4},{3,5},{4,2},{5,3},{6,0},{7,1},{8,10},{9,11},{10,... | collective-permute-start | bytes 1572872 | tf_op jit(solution)/shard_map/ppermute | solution.py:48
  16.9 0.5 collective-permute-start.6
  17.4 1.2 %shard_map.86.refs_0_.refs_1_ = bf16[1024,2048]{1,0:T(8,128)(2,1)S(1)} custom-call(bf16[2048,1024]{1,0:T(8,128)(2,1)S(1)} %copy-done, bf16[512,512]{1,0:T(8,128)(2,1)S(1)} %get-tuple-element.46._), custom_call_target="tpu_custom_call" | custom-call | bytes 8388608 | tf_op jit(solution)/shard_map/pallas_call | solution.py:220
  18.6 3.2 %collective-permute-done.11.got = bf16[512,512]{1,0:T(8,128)(2,1)S(1)} collective-permute-done((bf16[512,512]{1,0:T(8,128)(2,1)S(1)}, bf16[512,512]{1,0:T(8,128)(2,1)S(1)}, u32[]{:S(2)}, u32[]{:S(2)}) %collective-permute-start.11) | collective-permute-done | bytes 524320 | tf_op jit(solution)/shard_map/ppermute | solution.py:48
  21.8 0.4 shard_map.87
  22.2 2.8 %collective-permute-start.12 = (bf16[512,512]{1,0:T(8,128)(2,1)S(1)}, bf16[512,512]{1,0:T(8,128)(2,1)S(1)}, u32[]{:S(2)}, u32[]{:S(2)}) collective-permute-start(bf16[512,512]{1,0:T(8,128)(2,1)S(1)} %get-tuple-element.60), channel_id=1, source_target_pairs={{0,6},{1,7},{2,4},{3,5},{4,2},{5,3},{6,0},{7,1},{8,10},{9,11},{10,... | collective-permute-start | bytes 1572872 | tf_op jit(solution)/shard_map/ppermute | solution.py:48
  25.0 0.3 shard_map.80
  25.3 0.1 collective-permute-start.2
  25.4 0.5 collective-permute-start.3
  25.9 1.0 %collective-permute-done.2.refs_3_ = bf16[256,512]{1,0:T(8,128)(2,1)S(1)} collective-permute-done((bf16[256,512]{1,0:T(8,128)(2,1)S(1)}, bf16[256,512]{1,0:T(8,128)(2,1)S(1)}, u32[]{:S(2)}, u32[]{:S(2)}) %collective-permute-start.2) | collective-permute-done | bytes 262176 | tf_op jit(solution)/shard_map/ppermute | solution.py:48
  26.9 0.4 collective-permute-done.3.refs_4_
  27.3 1.1 %shard_map.82.refs_0_ = bf16[896,512]{1,0:T(8,128)(2,1)S(1)} custom-call(bf16[1792,512]{1,0:T(8,128)(2,1)S(1)} %get-tuple-element.43.refs_0_, bf16[256,512]{1,0:T(8,128)(2,1)S(1)} %get-tuple-element.47.refs_1_, bf16[256,512]{1,0:T(8,128)(2,1)S(1)} %get-tuple-element.48.refs_2_, bf16[256,512]{1,0:T(8,128)(2,1)S(1)} %collective-permute-done.2.refs_3_, ...), custom_call_target="tpu_custom_call" | custom-call | flops 939524096 | bytes 1835008 | tf_op jit(solution)/shard_map/pallas_call | solution.py:220
  28.4 2.0 %collective-permute-start.7 = (bf16[896,512]{1,0:T(8,128)(2,1)S(1)}, bf16[896,512]{1,0:T(8,128)(2,1)S(1)}, u32[]{:S(2)}, u32[]{:S(2)}) collective-permute-start(bf16[896,512]{1,0:T(8,128)(2,1)S(1)} %shard_map.82.refs_0_), channel_id=1, source_target_pairs={{0,16},{1,17},{2,18},{3,19},{4,20},{5,21},{6,22},{7,23},{8,72},{9,... | collective-permute-start | bytes 2752520 | tf_op jit(solution)/shard_map/ppermute | solution.py:48
  30.4 2.3 %collective-permute-done.12.got = bf16[512,512]{1,0:T(8,128)(2,1)S(1)} collective-permute-done((bf16[512,512]{1,0:T(8,128)(2,1)S(1)}, bf16[512,512]{1,0:T(8,128)(2,1)S(1)}, u32[]{:S(2)}, u32[]{:S(2)}) %collective-permute-start.12) | collective-permute-done | bytes 524320 | tf_op jit(solution)/shard_map/ppermute | solution.py:48
  32.7 0.3 shard_map.88
  32.9 0.1 collective-permute-start.13
  33.0 0.5 collective-permute-start.14
  33.5 1.1 %shard_map.81.refs_0_.refs_8_ = f32[896,512]{1,0:T(8,128)S(1)} custom-call(bf16[1792,512]{1,0:T(8,128)(2,1)S(1)} %get-tuple-element.43.refs_0_, bf16[256,512]{1,0:T(8,128)(2,1)S(1)} %get-tuple-element.47.refs_1_, bf16[256,512]{1,0:T(8,128)(2,1)S(1)} %get-tuple-element.48.refs_2_, bf16[256,512]{1,0:T(8,128)(2,1)S(1)} %collective-permute-done.2.refs_3_, ...), custom_call_target="tpu_custom_call" | custom-call | flops 939524096 | bytes 1835008 | tf_op jit(solution)/shard_map/pallas_call | solution.py:220
  34.7 0.3 collective-permute-done.14.refs_4_
  34.9 1.2 %shard_map.90 = bf16[896,512]{1,0:T(8,128)(2,1)S(1)} custom-call(bf16[1792,512]{1,0:T(8,128)(2,1)S(1)} %get-tuple-element.43.refs_0_, bf16[256,512]{1,0:T(8,128)(2,1)S(1)} %get-tuple-element.61.refs_1_, bf16[256,512]{1,0:T(8,128)(2,1)S(1)} %get-tuple-element.62.refs_2_, bf16[256,512]{1,0:T(8,128)(2,1)S(1)} %collective-permute-done.13.refs_3_, ...), custom_call_target="tpu_custom_call" | custom-call | flops 939524096 | bytes 1835008 | tf_op jit(solution)/shard_map/pallas_call | solution.py:220
  36.1 4.1 %collective-permute-start.15 = (bf16[896,512]{1,0:T(8,128)(2,1)S(1)}, bf16[896,512]{1,0:T(8,128)(2,1)S(1)}, u32[]{:S(2)}, u32[]{:S(2)}) collective-permute-start(bf16[896,512]{1,0:T(8,128)(2,1)S(1)} %shard_map.90), channel_id=1, source_target_pairs={{0,48},{1,49},{2,50},{3,51},{4,52},{5,53},{6,54},{7,55},{8,73},{9,... | collective-permute-start | bytes 2752520 | tf_op jit(solution)/shard_map/ppermute | solution.py:48
  40.2 1.7 %collective-permute-done.7.refs_1_ = bf16[896,512]{1,0:T(8,128)(2,1)S(1)} collective-permute-done((bf16[896,512]{1,0:T(8,128)(2,1)S(1)}, bf16[896,512]{1,0:T(8,128)(2,1)S(1)}, u32[]{:S(2)}, u32[]{:S(2)}) %collective-permute-start.7) | collective-permute-done | bytes 917536 | tf_op jit(solution)/shard_map/ppermute | solution.py:48
  41.9 0.2 shard_map.83
  42.0 1.8 %collective-permute-start.8 = (bf16[448,512]{1,0:T(8,128)(2,1)S(1)}, bf16[448,512]{1,0:T(8,128)(2,1)S(1)}, u32[]{:S(2)}, u32[]{:S(2)}) collective-permute-start(bf16[448,512]{1,0:T(8,128)(2,1)S(1)} %get-tuple-element.53), channel_id=1, source_target_pairs={{0,64},{1,65},{2,66},{3,67},{4,68},{5,69},{6,70},{7,71},{8,24},{9,... | collective-permute-start | bytes 1376264 | tf_op jit(solution)/shard_map/ppermute | solution.py:48
  43.9 1.1 %shard_map.89.refs_0_ = f32[896,512]{1,0:T(8,128)S(1)} custom-call(bf16[1792,512]{1,0:T(8,128)(2,1)S(1)} %get-tuple-element.43.refs_0_, bf16[256,512]{1,0:T(8,128)(2,1)S(1)} %get-tuple-element.61.refs_1_, bf16[256,512]{1,0:T(8,128)(2,1)S(1)} %get-tuple-element.62.refs_2_, bf16[256,512]{1,0:T(8,128)(2,1)S(1)} %collective-permute-done.13.refs_3_, ...), custom_call_target="tpu_custom_call" | custom-call | flops 939524096 | bytes 1835008 | tf_op jit(solution)/shard_map/pallas_call | solution.py:220
  45.0 5.8 %collective-permute-done.8.refs_1_ = bf16[448,512]{1,0:T(8,128)(2,1)S(1)} collective-permute-done((bf16[448,512]{1,0:T(8,128)(2,1)S(1)}, bf16[448,512]{1,0:T(8,128)(2,1)S(1)}, u32[]{:S(2)}, u32[]{:S(2)}) %collective-permute-start.8) | collective-permute-done | bytes 458784 | tf_op jit(solution)/shard_map/ppermute | solution.py:48
  50.8 0.1 shard_map.84
  50.9 0.7 collective-permute-done.15.refs_1_
  51.6 0.2 shard_map.91
  51.7 0.0 copy-start.3
  51.7 0.0 copy-start.4
  51.7 1.3 %collective-permute-start.16 = (bf16[448,512]{1,0:T(8,128)(2,1)S(1)}, bf16[448,512]{1,0:T(8,128)(2,1)S(1)}, u32[]{:S(2)}, u32[]{:S(2)}) collective-permute-start(bf16[448,512]{1,0:T(8,128)(2,1)S(1)} %get-tuple-element.64), channel_id=1, source_target_pairs={{0,16},{1,17},{2,18},{3,19},{4,20},{5,21},{6,22},{7,23},{8,72},{9,... | collective-permute-start | bytes 1376264 | tf_op jit(solution)/shard_map/ppermute | solution.py:48
  53.0 2.5 %collective-permute-start.9 = (bf16[224,512]{1,0:T(8,128)(2,1)S(1)}, bf16[224,512]{1,0:T(8,128)(2,1)S(1)}, u32[]{:S(2)}, u32[]{:S(2)}) collective-permute-start(bf16[224,512]{1,0:T(8,128)(2,1)S(1)} %get-tuple-element.55.refs_2_), channel_id=1, source_target_pairs={{0,48},{1,49},{2,50},{3,51},{4,52},{5,53},{6,54},{7,55},{8,73},{9,... | collective-permute-start | bytes 688136 | tf_op jit(solution)/shard_map/ppermute | solution.py:48
  55.6 4.7 %collective-permute-done.16.refs_1_ = bf16[448,512]{1,0:T(8,128)(2,1)S(1)} collective-permute-done((bf16[448,512]{1,0:T(8,128)(2,1)S(1)}, bf16[448,512]{1,0:T(8,128)(2,1)S(1)}, u32[]{:S(2)}, u32[]{:S(2)}) %collective-permute-start.16) | collective-permute-done | bytes 458784 | tf_op jit(solution)/shard_map/ppermute | solution.py:48
  60.3 0.1 shard_map.92
  60.4 1.8 %collective-permute-start.17 = (bf16[224,512]{1,0:T(8,128)(2,1)S(1)}, bf16[224,512]{1,0:T(8,128)(2,1)S(1)}, u32[]{:S(2)}, u32[]{:S(2)}) collective-permute-start(bf16[224,512]{1,0:T(8,128)(2,1)S(1)} %get-tuple-element.66), channel_id=1, source_target_pairs={{0,64},{1,65},{2,66},{3,67},{4,68},{5,69},{6,70},{7,71},{8,24},{9,... | collective-permute-start | bytes 688136 | tf_op jit(solution)/shard_map/ppermute | solution.py:48
  62.2 2.1 %collective-permute-start.10 = (bf16[112,512]{1,0:T(8,128)(2,1)S(1)}, bf16[112,512]{1,0:T(8,128)(2,1)S(1)}, u32[]{:S(2)}, u32[]{:S(2)}) collective-permute-start(bf16[112,512]{1,0:T(8,128)(2,1)S(1)} %get-tuple-element.57), channel_id=1, source_target_pairs={{0,65},{1,64},{2,67},{3,66},{4,69},{5,68},{6,71},{7,70},{8,56},{9,... | collective-permute-start | bytes 344072 | tf_op jit(solution)/shard_map/ppermute | solution.py:48
  64.4 2.1 %collective-permute-done.17.refs_1_ = bf16[224,512]{1,0:T(8,128)(2,1)S(1)} collective-permute-done((bf16[224,512]{1,0:T(8,128)(2,1)S(1)}, bf16[224,512]{1,0:T(8,128)(2,1)S(1)}, u32[]{:S(2)}, u32[]{:S(2)}) %collective-permute-start.17) | collective-permute-done | bytes 229408 | tf_op jit(solution)/shard_map/ppermute | solution.py:48
  66.5 3.1 %collective-permute-start.18 = (bf16[112,512]{1,0:T(8,128)(2,1)S(1)}, bf16[112,512]{1,0:T(8,128)(2,1)S(1)}, u32[]{:S(2)}, u32[]{:S(2)}) collective-permute-start(bf16[112,512]{1,0:T(8,128)(2,1)S(1)} %get-tuple-element.67.refs_4_), channel_id=1, source_target_pairs={{0,65},{1,64},{2,67},{3,66},{4,69},{5,68},{6,71},{7,70},{8,56},{9,... | collective-permute-start | bytes 344072 | tf_op jit(solution)/shard_map/ppermute | solution.py:48
  69.6 0.2 shard_map.94
  69.9 1.3 %collective-permute-start.21 = (bf16[112,512]{1,0:T(8,128)(2,1)S(1)}, bf16[112,512]{1,0:T(8,128)(2,1)S(1)}, u32[]{:S(2)}, u32[]{:S(2)}) collective-permute-start(bf16[112,512]{1,0:T(8,128)(2,1)S(1)} %get-tuple-element.74.own), channel_id=1, source_target_pairs={{0,2},{1,3},{2,0},{3,1},{4,6},{5,7},{6,4},{7,5},{8,14},{9,15},{10,... | collective-permute-start | bytes 344072 | tf_op jit(solution)/shard_map/ppermute | solution.py:48
  71.1 1.5 %collective-permute-done.18.refs_1_ = bf16[112,512]{1,0:T(8,128)(2,1)S(1)} collective-permute-done((bf16[112,512]{1,0:T(8,128)(2,1)S(1)}, bf16[112,512]{1,0:T(8,128)(2,1)S(1)}, u32[]{:S(2)}, u32[]{:S(2)}) %collective-permute-start.18) | collective-permute-done | bytes 114720 | tf_op jit(solution)/shard_map/ppermute | solution.py:48
  72.6 0.2 shard_map.95
  72.8 1.3 %collective-permute-start.19 = (bf16[112,512]{1,0:T(8,128)(2,1)S(1)}, bf16[112,512]{1,0:T(8,128)(2,1)S(1)}, u32[]{:S(2)}, u32[]{:S(2)}) collective-permute-start(bf16[112,512]{1,0:T(8,128)(2,1)S(1)} %get-tuple-element.73.own), channel_id=1, source_target_pairs={{0,2},{1,3},{2,0},{3,1},{4,6},{5,7},{6,4},{7,5},{8,14},{9,15},{10,... | collective-permute-start | bytes 344072 | tf_op jit(solution)/shard_map/ppermute | solution.py:48
  74.1 0.6 collective-permute-done.21.got
  74.7 2.8 %collective-permute-start.22 = (bf16[224,512]{1,0:T(8,128)(2,1)S(1)}, bf16[224,512]{1,0:T(8,128)(2,1)S(1)}, u32[]{:S(2)}, u32[]{:S(2)}) collective-permute-start(bf16[224,512]{1,0:T(8,128)(2,1)S(1)} %shard_map.97.refs_1_), channel_id=1, source_target_pairs={{0,6},{1,7},{2,4},{3,5},{4,2},{5,3},{6,0},{7,1},{8,10},{9,11},{10,... | collective-permute-start | bytes 688136 | tf_op jit(solution)/shard_map/ppermute | solution.py:48
  77.6 1.4 %collective-permute-done.19.got = bf16[112,512]{1,0:T(8,128)(2,1)S(1)} collective-permute-done((bf16[112,512]{1,0:T(8,128)(2,1)S(1)}, bf16[112,512]{1,0:T(8,128)(2,1)S(1)}, u32[]{:S(2)}, u32[]{:S(2)}) %collective-permute-start.19) | collective-permute-done | bytes 114720 | tf_op jit(solution)/shard_map/ppermute | solution.py:48
  79.0 2.8 %collective-permute-start.20 = (bf16[224,512]{1,0:T(8,128)(2,1)S(1)}, bf16[224,512]{1,0:T(8,128)(2,1)S(1)}, u32[]{:S(2)}, u32[]{:S(2)}) collective-permute-start(bf16[224,512]{1,0:T(8,128)(2,1)S(1)} %shard_map.96.refs_2_), channel_id=1, source_target_pairs={{0,6},{1,7},{2,4},{3,5},{4,2},{5,3},{6,0},{7,1},{8,10},{9,11},{10,... | collective-permute-start | bytes 688136 | tf_op jit(solution)/shard_map/ppermute | solution.py:48
  81.9 1.0 %maximum_bitcast_fusion = (f32[1,112,1024]{2,1,0:T(8,128)}, f32[1,112,1024]{2,1,0:T(8,128)}) fusion(f32[112,512]{1,0:T(8,128)S(1)} %get-tuple-element.70, f32[112,512]{1,0:T(8,128)S(1)} %get-tuple-element.68, f32[112,512]{1,0:T(8,128)S(1)} %get-tuple-element.72, f32[112,512]{1,0:T(8,128)S(1)} %get-tuple-element.71), kind=kLoop, calls=%fused_computation | loop fusion | flops 229376 | bytes 1835008 | tf_op jit(solution)/shard_map/reshape | solution.py:342
  82.8 1.1 %shard_map.98.refs_3_ = f32[448,2048]{1,0:T(8,128)S(1)} custom-call(bf16[1024,2048]{1,0:T(8,128)(2,1)S(1)} %shard_map.86.refs_0_.refs_1_, bf16[224,512]{1,0:T(8,128)(2,1)S(1)} %shard_map.97.refs_1_, bf16[224,512]{1,0:T(8,128)(2,1)S(1)} %collective-permute-done.22.refs_2_), custom_call_target="tpu_custom_call" | custom-call | flops 939524096 | bytes 5767168 | tf_op jit(solution)/shard_map/pallas_call | solution.py:220
  84.0 1.9 %shard_map.99.refs_4_ = bf16[4,112,2048]{2,1,0:T(8,128)(2,1)} custom-call(s32[4]{0:T(128)S(1)} %pad_add_fusion.refs_2_.pos.refs_0_, bf16[1024,2048]{1,0:T(8,128)(2,1)S(1)} %shard_map.86.refs_0_.refs_1_, bf16[224,512]{1,0:T(8,128)(2,1)S(1)} %shard_map.96.refs_2_, f32[448,2048]{1,0:T(8,128)S(1)} %shard_map.98.refs_3_), custom_call_target="tpu_custom_call" | custom-call | flops 469762048 | bytes 2097152 | tf_op jit(solution)/shard_map/pallas_call | solution.py:329
  85.9 0.4 collective-permute-done.20.refs_2_
  86.3 1.9 %shard_map.100 = bf16[4,112,2048]{2,1,0:T(8,128)(2,1)} custom-call(s32[4]{0:T(128)S(1)} %pad_add_fusion.refs_2_.pos.refs_0_, bf16[1024,2048]{1,0:T(8,128)(2,1)S(1)} %shard_map.86.refs_0_.refs_1_, bf16[224,512]{1,0:T(8,128)(2,1)S(1)} %collective-permute-done.20.refs_2_, f32[448,2048]{1,0:T(8,128)S(1)} %shard_map.98.refs_3_, ...), custom_call_target="tpu_custom_call", output_to_operand_aliasing={{}: (4, {})} | custom-call | flops 469762048 | bytes 2097152 | tf_op jit(solution)/shard_map/pallas_call | solution.py:329
  (20 shorter events, 0.2 us)
Async XLA Ops:
  0.7 2.2 %copy-start.1 = (bf16[512,2048]{1,0:T(8,128)(2,1)S(1)}, bf16[512,2048]{1,0:T(8,128)(2,1)}, u32[]{:S(2)}) copy-start(bf16[512,2048]{1,0:T(8,128)(2,1)} %refs_0_.3) | copy-start | bytes 6291460
  3.0 2.9 %copy-start = (bf16[2048,1024]{1,0:T(8,128)(2,1)S(1)}, bf16[2048,1024]{1,0:T(8,128)(2,1)}, u32[]{:S(2)}) copy-start(bf16[2048,1024]{1,0:T(8,128)(2,1)} %projection.1) | copy-start | bytes 12582916
  4.2 9.3 %collective-permute-start = (bf16[512,512]{1,0:T(8,128)(2,1)S(1)}, bf16[512,512]{1,0:T(8,128)(2,1)S(1)}, u32[]{:S(2)}, u32[]{:S(2)}) collective-permute-start(bf16[512,512]{1,0:T(8,128)(2,1)S(1)} %get-tuple-element.44), channel_id=1, source_target_pairs={{0,2},{1,3},{2,0},{3,1},{4,6},{5,7},{6,4},{7,5},{8,14},{9,15},{10,... | collective-permute-start | bytes 1572872 | tf_op jit(solution)/shard_map/ppermute | solution.py:48
  5.9 2.2 %copy-start.2 = (bf16[512,3584]{1,0:T(8,128)(2,1)S(1)}, bf16[512,3584]{1,0:T(8,128)(2,1)}, u32[]{:S(2)}) copy-start(bf16[512,3584]{1,0:T(8,128)(2,1)} %hidden.1) | copy-start | bytes 11010052
  7.2 14.6 %collective-permute-start.11 = (bf16[512,512]{1,0:T(8,128)(2,1)S(1)}, bf16[512,512]{1,0:T(8,128)(2,1)S(1)}, u32[]{:S(2)}, u32[]{:S(2)}) collective-permute-start(bf16[512,512]{1,0:T(8,128)(2,1)S(1)} %get-tuple-element.58), channel_id=1, source_target_pairs={{0,2},{1,3},{2,0},{3,1},{4,6},{5,7},{6,4},{7,5},{8,14},{9,15},{10,... | collective-permute-start | bytes 1572872 | tf_op jit(solution)/shard_map/ppermute | solution.py:48
  9.9 15.5 %collective-permute-start.5 = (bf16[560,512]{1,0:T(8,128)(2,1)S(1)}, bf16[560,512]{1,0:T(8,128)(2,1)S(1)}, u32[]{:S(2)}, u32[]{:S(2)}) collective-permute-start(bf16[560,512]{1,0:T(8,128)(2,1)S(1)} %get-tuple-element.50), channel_id=1, source_target_pairs={{0,8},{1,9},{2,10},{3,11},{4,12},{5,13},{6,14},{7,15},{8,0},{9,1},... | collective-permute-start | bytes 1720328 | tf_op jit(solution)/shard_map/ppermute | solution.py:48
  13.9 11.1 %collective-permute-start.1 = (bf16[512,512]{1,0:T(8,128)(2,1)S(1)}, bf16[512,512]{1,0:T(8,128)(2,1)S(1)}, u32[]{:S(2)}, u32[]{:S(2)}) collective-permute-start(bf16[512,512]{1,0:T(8,128)(2,1)S(1)} %get-tuple-element.46._), channel_id=1, source_target_pairs={{0,6},{1,7},{2,4},{3,5},{4,2},{5,3},{6,0},{7,1},{8,10},{9,11},{10,... | collective-permute-start | bytes 1572872 | tf_op jit(solution)/shard_map/ppermute | solution.py:48
  16.9 9.0 %collective-permute-start.4 = (bf16[672,512]{1,0:T(8,128)(2,1)S(1)}, bf16[672,512]{1,0:T(8,128)(2,1)S(1)}, u32[]{:S(2)}, u32[]{:S(2)}) collective-permute-start(bf16[672,512]{1,0:T(8,128)(2,1)S(1)} %get-tuple-element.49), channel_id=1, source_target_pairs={{0,8},{1,9},{2,10},{3,11},{4,12},{5,13},{6,14},{7,15},{8,0},{9,1},... | collective-permute-start | bytes 2064392 | tf_op jit(solution)/shard_map/ppermute | solution.py:48
  16.9 9.0 %collective-permute-start.6 = (bf16[560,512]{1,0:T(8,128)(2,1)S(1)}, bf16[560,512]{1,0:T(8,128)(2,1)S(1)}, u32[]{:S(2)}, u32[]{:S(2)}) collective-permute-start(bf16[560,512]{1,0:T(8,128)(2,1)S(1)} %get-tuple-element.51), channel_id=1, source_target_pairs={{0,8},{1,9},{2,10},{3,11},{4,12},{5,13},{6,14},{7,15},{8,0},{9,1},... | collective-permute-start | bytes 1720328 | tf_op jit(solution)/shard_map/ppermute | solution.py:48
  22.2 10.5 %collective-permute-start.12 = (bf16[512,512]{1,0:T(8,128)(2,1)S(1)}, bf16[512,512]{1,0:T(8,128)(2,1)S(1)}, u32[]{:S(2)}, u32[]{:S(2)}) collective-permute-start(bf16[512,512]{1,0:T(8,128)(2,1)S(1)} %get-tuple-element.60), channel_id=1, source_target_pairs={{0,6},{1,7},{2,4},{3,5},{4,2},{5,3},{6,0},{7,1},{8,10},{9,11},{10,... | collective-permute-start | bytes 1572872 | tf_op jit(solution)/shard_map/ppermute | solution.py:48
  25.3 1.6 %collective-permute-start.2 = (bf16[256,512]{1,0:T(8,128)(2,1)S(1)}, bf16[256,512]{1,0:T(8,128)(2,1)S(1)}, u32[]{:S(2)}, u32[]{:S(2)}) collective-permute-start(bf16[256,512]{1,0:T(8,128)(2,1)S(1)} %get-tuple-element.47.refs_1_), channel_id=1, source_target_pairs={{0,8},{1,9},{2,10},{3,11},{4,12},{5,13},{6,14},{7,15},{8,0},{9,1},... | collective-permute-start | bytes 786440 | tf_op jit(solution)/shard_map/ppermute | solution.py:48
  25.4 1.9 %collective-permute-start.3 = (bf16[256,512]{1,0:T(8,128)(2,1)S(1)}, bf16[256,512]{1,0:T(8,128)(2,1)S(1)}, u32[]{:S(2)}, u32[]{:S(2)}) collective-permute-start(bf16[256,512]{1,0:T(8,128)(2,1)S(1)} %get-tuple-element.48.refs_2_), channel_id=1, source_target_pairs={{0,8},{1,9},{2,10},{3,11},{4,12},{5,13},{6,14},{7,15},{8,0},{9,1},... | collective-permute-start | bytes 786440 | tf_op jit(solution)/shard_map/ppermute | solution.py:48
  28.4 13.5 %collective-permute-start.7 = (bf16[896,512]{1,0:T(8,128)(2,1)S(1)}, bf16[896,512]{1,0:T(8,128)(2,1)S(1)}, u32[]{:S(2)}, u32[]{:S(2)}) collective-permute-start(bf16[896,512]{1,0:T(8,128)(2,1)S(1)} %shard_map.82.refs_0_), channel_id=1, source_target_pairs={{0,16},{1,17},{2,18},{3,19},{4,20},{5,21},{6,22},{7,23},{8,72},{9,... | collective-permute-start | bytes 2752520 | tf_op jit(solution)/shard_map/ppermute | solution.py:48
  32.9 1.7 %collective-permute-start.13 = (bf16[256,512]{1,0:T(8,128)(2,1)S(1)}, bf16[256,512]{1,0:T(8,128)(2,1)S(1)}, u32[]{:S(2)}, u32[]{:S(2)}) collective-permute-start(bf16[256,512]{1,0:T(8,128)(2,1)S(1)} %get-tuple-element.61.refs_1_), channel_id=1, source_target_pairs={{0,8},{1,9},{2,10},{3,11},{4,12},{5,13},{6,14},{7,15},{8,0},{9,1},... | collective-permute-start | bytes 786440 | tf_op jit(solution)/shard_map/ppermute | solution.py:48
  33.0 1.9 %collective-permute-start.14 = (bf16[256,512]{1,0:T(8,128)(2,1)S(1)}, bf16[256,512]{1,0:T(8,128)(2,1)S(1)}, u32[]{:S(2)}, u32[]{:S(2)}) collective-permute-start(bf16[256,512]{1,0:T(8,128)(2,1)S(1)} %get-tuple-element.62.refs_2_), channel_id=1, source_target_pairs={{0,8},{1,9},{2,10},{3,11},{4,12},{5,13},{6,14},{7,15},{8,0},{9,1},... | collective-permute-start | bytes 786440 | tf_op jit(solution)/shard_map/ppermute | solution.py:48
  36.1 15.5 %collective-permute-start.15 = (bf16[896,512]{1,0:T(8,128)(2,1)S(1)}, bf16[896,512]{1,0:T(8,128)(2,1)S(1)}, u32[]{:S(2)}, u32[]{:S(2)}) collective-permute-start(bf16[896,512]{1,0:T(8,128)(2,1)S(1)} %shard_map.90), channel_id=1, source_target_pairs={{0,48},{1,49},{2,50},{3,51},{4,52},{5,53},{6,54},{7,55},{8,73},{9,... | collective-permute-start | bytes 2752520 | tf_op jit(solution)/shard_map/ppermute | solution.py:48
  42.0 8.7 %collective-permute-start.8 = (bf16[448,512]{1,0:T(8,128)(2,1)S(1)}, bf16[448,512]{1,0:T(8,128)(2,1)S(1)}, u32[]{:S(2)}, u32[]{:S(2)}) collective-permute-start(bf16[448,512]{1,0:T(8,128)(2,1)S(1)} %get-tuple-element.53), channel_id=1, source_target_pairs={{0,64},{1,65},{2,66},{3,67},{4,68},{5,69},{6,70},{7,71},{8,24},{9,... | collective-permute-start | bytes 1376264 | tf_op jit(solution)/shard_map/ppermute | solution.py:48
  51.7 17.9 %copy-start.3 = (f32[1,112,1024]{2,1,0:T(8,128)S(1)}, f32[1,112,1024]{2,1,0:T(8,128)}, u32[]{:S(2)}) copy-start(f32[1,112,1024]{2,1,0:T(8,128)} %refs_2_.3) | copy-start | bytes 1376260
  51.7 17.9 %copy-start.4 = (f32[1,112,1024]{2,1,0:T(8,128)S(1)}, f32[1,112,1024]{2,1,0:T(8,128)}, u32[]{:S(2)}) copy-start(f32[1,112,1024]{2,1,0:T(8,128)} %refs_3_.3) | copy-start | bytes 1376260
  51.7 8.6 %collective-permute-start.16 = (bf16[448,512]{1,0:T(8,128)(2,1)S(1)}, bf16[448,512]{1,0:T(8,128)(2,1)S(1)}, u32[]{:S(2)}, u32[]{:S(2)}) collective-permute-start(bf16[448,512]{1,0:T(8,128)(2,1)S(1)} %get-tuple-element.64), channel_id=1, source_target_pairs={{0,16},{1,17},{2,18},{3,19},{4,20},{5,21},{6,22},{7,23},{8,72},{9,... | collective-permute-start | bytes 1376264 | tf_op jit(solution)/shard_map/ppermute | solution.py:48
  53.0 9.1 %collective-permute-start.9 = (bf16[224,512]{1,0:T(8,128)(2,1)S(1)}, bf16[224,512]{1,0:T(8,128)(2,1)S(1)}, u32[]{:S(2)}, u32[]{:S(2)}) collective-permute-start(bf16[224,512]{1,0:T(8,128)(2,1)S(1)} %get-tuple-element.55.refs_2_), channel_id=1, source_target_pairs={{0,48},{1,49},{2,50},{3,51},{4,52},{5,53},{6,54},{7,55},{8,73},{9,... | collective-permute-start | bytes 688136 | tf_op jit(solution)/shard_map/ppermute | solution.py:48
  60.4 6.1 %collective-permute-start.17 = (bf16[224,512]{1,0:T(8,128)(2,1)S(1)}, bf16[224,512]{1,0:T(8,128)(2,1)S(1)}, u32[]{:S(2)}, u32[]{:S(2)}) collective-permute-start(bf16[224,512]{1,0:T(8,128)(2,1)S(1)} %get-tuple-element.66), channel_id=1, source_target_pairs={{0,64},{1,65},{2,66},{3,67},{4,68},{5,69},{6,70},{7,71},{8,24},{9,... | collective-permute-start | bytes 688136 | tf_op jit(solution)/shard_map/ppermute | solution.py:48
  62.2 7.4 %collective-permute-start.10 = (bf16[112,512]{1,0:T(8,128)(2,1)S(1)}, bf16[112,512]{1,0:T(8,128)(2,1)S(1)}, u32[]{:S(2)}, u32[]{:S(2)}) collective-permute-start(bf16[112,512]{1,0:T(8,128)(2,1)S(1)} %get-tuple-element.57), channel_id=1, source_target_pairs={{0,65},{1,64},{2,67},{3,66},{4,69},{5,68},{6,71},{7,70},{8,56},{9,... | collective-permute-start | bytes 344072 | tf_op jit(solution)/shard_map/ppermute | solution.py:48
  66.5 6.1 %collective-permute-start.18 = (bf16[112,512]{1,0:T(8,128)(2,1)S(1)}, bf16[112,512]{1,0:T(8,128)(2,1)S(1)}, u32[]{:S(2)}, u32[]{:S(2)}) collective-permute-start(bf16[112,512]{1,0:T(8,128)(2,1)S(1)} %get-tuple-element.67.refs_4_), channel_id=1, source_target_pairs={{0,65},{1,64},{2,67},{3,66},{4,69},{5,68},{6,71},{7,70},{8,56},{9,... | collective-permute-start | bytes 344072 | tf_op jit(solution)/shard_map/ppermute | solution.py:48
  69.9 4.9 %collective-permute-start.21 = (bf16[112,512]{1,0:T(8,128)(2,1)S(1)}, bf16[112,512]{1,0:T(8,128)(2,1)S(1)}, u32[]{:S(2)}, u32[]{:S(2)}) collective-permute-start(bf16[112,512]{1,0:T(8,128)(2,1)S(1)} %get-tuple-element.74.own), channel_id=1, source_target_pairs={{0,2},{1,3},{2,0},{3,1},{4,6},{5,7},{6,4},{7,5},{8,14},{9,15},{10,... | collective-permute-start | bytes 344072 | tf_op jit(solution)/shard_map/ppermute | solution.py:48
  72.8 6.2 %collective-permute-start.19 = (bf16[112,512]{1,0:T(8,128)(2,1)S(1)}, bf16[112,512]{1,0:T(8,128)(2,1)S(1)}, u32[]{:S(2)}, u32[]{:S(2)}) collective-permute-start(bf16[112,512]{1,0:T(8,128)(2,1)S(1)} %get-tuple-element.73.own), channel_id=1, source_target_pairs={{0,2},{1,3},{2,0},{3,1},{4,6},{5,7},{6,4},{7,5},{8,14},{9,15},{10,... | collective-permute-start | bytes 344072 | tf_op jit(solution)/shard_map/ppermute | solution.py:48
  74.7 8.1 %collective-permute-start.22 = (bf16[224,512]{1,0:T(8,128)(2,1)S(1)}, bf16[224,512]{1,0:T(8,128)(2,1)S(1)}, u32[]{:S(2)}, u32[]{:S(2)}) collective-permute-start(bf16[224,512]{1,0:T(8,128)(2,1)S(1)} %shard_map.97.refs_1_), channel_id=1, source_target_pairs={{0,6},{1,7},{2,4},{3,5},{4,2},{5,3},{6,0},{7,1},{8,10},{9,11},{10,... | collective-permute-start | bytes 688136 | tf_op jit(solution)/shard_map/ppermute | solution.py:48
  79.0 7.3 %collective-permute-start.20 = (bf16[224,512]{1,0:T(8,128)(2,1)S(1)}, bf16[224,512]{1,0:T(8,128)(2,1)S(1)}, u32[]{:S(2)}, u32[]{:S(2)}) collective-permute-start(bf16[224,512]{1,0:T(8,128)(2,1)S(1)} %shard_map.96.refs_2_), channel_id=1, source_target_pairs={{0,6},{1,7},{2,4},{3,5},{4,2},{5,3},{6,0},{7,1},{8,10},{9,11},{10,... | collective-permute-start | bytes 688136 | tf_op jit(solution)/shard_map/ppermute | solution.py:48

commit v5 on v4

--- a/solution.py
+++ b/solution.py
@@ -124,9 +124,9 @@
 
 def lowrank_kernel(order, leaving, mine, *refs):
     ps, qs, other, out = refs[:SHARES], refs[SHARES : 2 * SHARES], refs[2 * SHARES : 2 * SHARES + len(PARTS)], refs[-1]
-    tokens = ps[0].shape[0]
     bit = 3 - order[0]
     for at in tiles(out.shape[1]):
+        p, q = (jnp.concatenate([share[:, at] for share in shares], axis=0) for shares in (ps, qs))
         base = 0
         for blocks, there in zip(PARTS, other):
             taken = [k for k in range(blocks) if (base + k >> bit & 1) == leaving]
@@ -137,12 +137,9 @@
                 else:
                     runs.append([k, k + 1])
             for first, end in runs:
-                part = jnp.zeros(((end - first) * ROWS, at.stop - at.start), F32)
-                for k, (p, q) in enumerate(zip(ps, qs)):
-                    share = slice(k * tokens, (k + 1) * tokens)
-                    here = slice((base + first) * ROWS, (base + end) * ROWS)
-                    part += jnp.dot(mine[here, share], p[:, at], preferred_element_type=F32)
-                    part += jnp.dot(there[first * ROWS : end * ROWS, share], q[:, at], preferred_element_type=F32)
+                here = slice((base + first) * ROWS, (base + end) * ROWS)
+                part = jnp.dot(mine[here, :], p, preferred_element_type=F32)
+                part += jnp.dot(there[first * ROWS : end * ROWS, :], q, preferred_element_type=F32)
                 for k in range(first, end):
                     to = 0
                     for step in order[1:]:

time: 88.6 us -> 88.6 us (level)
  no operation moved by 1% of the time
where the time goes in v5:
time: 88.6 us; the launch traced here: 88.4 us
  starting transfers between devices  37.9 us (43%)
  waiting for transfers between devices  28.8 us (33%)
  Pallas kernels  17.4 us (20%)
  local copies, waits for them, and re-layouts  2.24 us (3%)
  other arithmetic  1.07 us (1%)
  between operations  1.03 us (1%)
    ppermute x23, starting transfers between devices, exchange(): return lax.ppermute(array, AXES, pairs)  37.9 us
    ppermute x23, waiting for transfers between devices, exchange(): return lax.ppermute(array, AXES, pairs)  28.8 us
    pallas_call x23, Pallas kernels, run(): pl.pallas_call(kernel, out_shape=[jax.ShapeDtypeStruct(s, t) for s, t in...  13.5 us
    pallas_call x2, Pallas kernels, local(): pl.pallas_call(lambda *refs, far=far: finish_kernel(STARTS[1], far, *refs...  3.89 us
    slice x1, local copies, waits for them, and re-layouts, local(): first_columns = first_columns[:, :WIDTHS[0]]  1.88 us
  transfers between devices with their start and end apart: 23, of which 15 were waited for; matrix products, arithmetic and copies ran while one was open for 1% of the time, Pallas kernels for 16%

profile of v5, /device:TPU:0, one launch (start us, length us, event | category | flops | bytes accessed | tf_op | source)
XLA Modules:
  0.0 88.4 jit_solution(3957688935402830145)
XLA Ops:
  0.7 0.1 pad_add_fusion.refs_2_.pos.refs_0_
  0.8 1.9 %slice.3.refs_1_ = bf16[2048,512]{1,0:T(8,128)(2,1)S(1)} slice(bf16[2048,1024]{1,0:T(8,128)(2,1)} %projection.1), slice={[0:2048], [0:512]} | slice | bytes 4194304 | tf_op jit(solution)/shard_map/slice | solution.py:240
  2.6 0.3 copy-done.1
  3.0 1.3 %shard_map.76 = (f32[512,512]{1,0:T(8,128)S(1)}, bf16[512,512]{1,0:T(8,128)(2,1)S(1)}) custom-call(bf16[512,2048]{1,0:T(8,128)(2,1)S(1)} %copy-done.1, bf16[2048,512]{1,0:T(8,128)(2,1)S(1)} %slice.3.refs_1_, s32[4]{0:T(128)S(1)} %pad_add_fusion.refs_2_.pos.refs_0_), custom_call_target="tpu_custom_call" | custom-call | flops 1073741824 | bytes 4194304 | tf_op jit(solution)/shard_map/pallas_call | solution.py:217
  4.2 1.7 %collective-permute-start = (bf16[512,512]{1,0:T(8,128)(2,1)S(1)}, bf16[512,512]{1,0:T(8,128)(2,1)S(1)}, u32[]{:S(2)}, u32[]{:S(2)}) collective-permute-start(bf16[512,512]{1,0:T(8,128)(2,1)S(1)} %get-tuple-element.44), channel_id=1, source_target_pairs={{0,2},{1,3},{2,0},{3,1},{4,6},{5,7},{6,4},{7,5},{8,14},{9,15},{10,... | collective-permute-start | bytes 1572872 | tf_op jit(solution)/shard_map/ppermute | solution.py:48
  5.9 1.2 %shard_map.77 = (f32[512,512]{1,0:T(8,128)S(1)}, bf16[512,512]{1,0:T(8,128)(2,1)S(1)}) custom-call(bf16[512,2048]{1,0:T(8,128)(2,1)S(1)} %copy-done.1, bf16[2048,1024]{1,0:T(8,128)(2,1)S(1)} %copy-done, f32[512,512]{1,0:T(8,128)S(1)} %get-tuple-element.41.refs_2_.total), custom_call_target="tpu_custom_call" | custom-call | flops 1073741824 | bytes 4194304 | tf_op jit(solution)/shard_map/pallas_call | solution.py:217
  7.2 0.9 %collective-permute-start.11 = (bf16[512,512]{1,0:T(8,128)(2,1)S(1)}, bf16[512,512]{1,0:T(8,128)(2,1)S(1)}, u32[]{:S(2)}, u32[]{:S(2)}) collective-permute-start(bf16[512,512]{1,0:T(8,128)(2,1)S(1)} %get-tuple-element.58), channel_id=1, source_target_pairs={{0,2},{1,3},{2,0},{3,1},{4,6},{5,7},{6,4},{7,5},{8,14},{9,15},{10,... | collective-permute-start | bytes 1572872 | tf_op jit(solution)/shard_map/ppermute | solution.py:48
  8.1 1.8 %shard_map.78 = (bf16[1792,512]{1,0:T(8,128)(2,1)S(1)}, bf16[672,512]{1,0:T(8,128)(2,1)S(1)}, bf16[560,512]{1,0:T(8,128)(2,1)S(1)}, bf16[560,512]{1,0:T(8,128)(2,1)S(1)}) custom-call(s32[4]{0:T(128)S(1)} %pad_add_fusion.refs_2_.pos.refs_0_, bf16[512,3584]{1,0:T(8,128)(2,1)S(1)} %copy-done.2, f32[512,512]{1,0:T(8,128)S(1)} %get-tuple-element.42._.total), custom_call_target="tpu_custom_call" | custom-call | bytes 7340032 | tf_op jit(solution)/shard_map/pallas_call | solution.py:217
  9.9 0.9 %collective-permute-start.5 = (bf16[560,512]{1,0:T(8,128)(2,1)S(1)}, bf16[560,512]{1,0:T(8,128)(2,1)S(1)}, u32[]{:S(2)}, u32[]{:S(2)}) collective-permute-start(bf16[560,512]{1,0:T(8,128)(2,1)S(1)} %get-tuple-element.50), channel_id=1, source_target_pairs={{0,8},{1,9},{2,10},{3,11},{4,12},{5,13},{6,14},{7,15},{8,0},{9,1},... | collective-permute-start | bytes 1720328 | tf_op jit(solution)/shard_map/ppermute | solution.py:48
  10.8 2.7 %collective-permute-done.got = bf16[512,512]{1,0:T(8,128)(2,1)S(1)} collective-permute-done((bf16[512,512]{1,0:T(8,128)(2,1)S(1)}, bf16[512,512]{1,0:T(8,128)(2,1)S(1)}, u32[]{:S(2)}, u32[]{:S(2)}) %collective-permute-start) | collective-permute-done | bytes 524320 | tf_op jit(solution)/shard_map/ppermute | solution.py:48
  13.5 0.4 shard_map.79
  13.9 2.9 %collective-permute-start.1 = (bf16[512,512]{1,0:T(8,128)(2,1)S(1)}, bf16[512,512]{1,0:T(8,128)(2,1)S(1)}, u32[]{:S(2)}, u32[]{:S(2)}) collective-permute-start(bf16[512,512]{1,0:T(8,128)(2,1)S(1)} %get-tuple-element.46._), channel_id=1, source_target_pairs={{0,6},{1,7},{2,4},{3,5},{4,2},{5,3},{6,0},{7,1},{8,10},{9,11},{10,... | collective-permute-start | bytes 1572872 | tf_op jit(solution)/shard_map/ppermute | solution.py:48
  16.9 0.5 collective-permute-start.6
  17.4 1.2 %shard_map.86.refs_0_.refs_1_ = bf16[1024,2048]{1,0:T(8,128)(2,1)S(1)} custom-call(bf16[2048,1024]{1,0:T(8,128)(2,1)S(1)} %copy-done, bf16[512,512]{1,0:T(8,128)(2,1)S(1)} %get-tuple-element.46._), custom_call_target="tpu_custom_call" | custom-call | bytes 8388608 | tf_op jit(solution)/shard_map/pallas_call | solution.py:217
  18.6 3.2 %collective-permute-done.11.got = bf16[512,512]{1,0:T(8,128)(2,1)S(1)} collective-permute-done((bf16[512,512]{1,0:T(8,128)(2,1)S(1)}, bf16[512,512]{1,0:T(8,128)(2,1)S(1)}, u32[]{:S(2)}, u32[]{:S(2)}) %collective-permute-start.11) | collective-permute-done | bytes 524320 | tf_op jit(solution)/shard_map/ppermute | solution.py:48
  21.8 0.4 shard_map.87
  22.2 2.8 %collective-permute-start.12 = (bf16[512,512]{1,0:T(8,128)(2,1)S(1)}, bf16[512,512]{1,0:T(8,128)(2,1)S(1)}, u32[]{:S(2)}, u32[]{:S(2)}) collective-permute-start(bf16[512,512]{1,0:T(8,128)(2,1)S(1)} %get-tuple-element.60), channel_id=1, source_target_pairs={{0,6},{1,7},{2,4},{3,5},{4,2},{5,3},{6,0},{7,1},{8,10},{9,11},{10,... | collective-permute-start | bytes 1572872 | tf_op jit(solution)/shard_map/ppermute | solution.py:48
  25.0 0.3 shard_map.80
  25.3 0.1 collective-permute-start.2
  25.4 0.5 collective-permute-start.3
  25.9 1.0 %collective-permute-done.2.refs_3_ = bf16[256,512]{1,0:T(8,128)(2,1)S(1)} collective-permute-done((bf16[256,512]{1,0:T(8,128)(2,1)S(1)}, bf16[256,512]{1,0:T(8,128)(2,1)S(1)}, u32[]{:S(2)}, u32[]{:S(2)}) %collective-permute-start.2) | collective-permute-done | bytes 262176 | tf_op jit(solution)/shard_map/ppermute | solution.py:48
  26.9 0.4 collective-permute-done.3.refs_4_
  27.3 1.1 %shard_map.82.refs_0_ = bf16[896,512]{1,0:T(8,128)(2,1)S(1)} custom-call(bf16[1792,512]{1,0:T(8,128)(2,1)S(1)} %get-tuple-element.43.refs_0_, bf16[256,512]{1,0:T(8,128)(2,1)S(1)} %get-tuple-element.47.refs_1_, bf16[256,512]{1,0:T(8,128)(2,1)S(1)} %get-tuple-element.48.refs_2_, bf16[256,512]{1,0:T(8,128)(2,1)S(1)} %collective-permute-done.2.refs_3_, ...), custom_call_target="tpu_custom_call" | custom-call | flops 939524096 | bytes 1835008 | tf_op jit(solution)/shard_map/pallas_call | solution.py:217
  28.4 2.0 %collective-permute-start.7 = (bf16[896,512]{1,0:T(8,128)(2,1)S(1)}, bf16[896,512]{1,0:T(8,128)(2,1)S(1)}, u32[]{:S(2)}, u32[]{:S(2)}) collective-permute-start(bf16[896,512]{1,0:T(8,128)(2,1)S(1)} %shard_map.82.refs_0_), channel_id=1, source_target_pairs={{0,16},{1,17},{2,18},{3,19},{4,20},{5,21},{6,22},{7,23},{8,72},{9,... | collective-permute-start | bytes 2752520 | tf_op jit(solution)/shard_map/ppermute | solution.py:48
  30.4 2.3 %collective-permute-done.12.got = bf16[512,512]{1,0:T(8,128)(2,1)S(1)} collective-permute-done((bf16[512,512]{1,0:T(8,128)(2,1)S(1)}, bf16[512,512]{1,0:T(8,128)(2,1)S(1)}, u32[]{:S(2)}, u32[]{:S(2)}) %collective-permute-start.12) | collective-permute-done | bytes 524320 | tf_op jit(solution)/shard_map/ppermute | solution.py:48
  32.7 0.3 shard_map.88
  32.9 0.1 collective-permute-start.13
  33.0 0.5 collective-permute-start.14
  33.5 1.1 %shard_map.81.refs_0_.refs_8_ = f32[896,512]{1,0:T(8,128)S(1)} custom-call(bf16[1792,512]{1,0:T(8,128)(2,1)S(1)} %get-tuple-element.43.refs_0_, bf16[256,512]{1,0:T(8,128)(2,1)S(1)} %get-tuple-element.47.refs_1_, bf16[256,512]{1,0:T(8,128)(2,1)S(1)} %get-tuple-element.48.refs_2_, bf16[256,512]{1,0:T(8,128)(2,1)S(1)} %collective-permute-done.2.refs_3_, ...), custom_call_target="tpu_custom_call" | custom-call | flops 939524096 | bytes 1835008 | tf_op jit(solution)/shard_map/pallas_call | solution.py:217
  34.7 0.3 collective-permute-done.14.refs_4_
  34.9 1.2 %shard_map.90 = bf16[896,512]{1,0:T(8,128)(2,1)S(1)} custom-call(bf16[1792,512]{1,0:T(8,128)(2,1)S(1)} %get-tuple-element.43.refs_0_, bf16[256,512]{1,0:T(8,128)(2,1)S(1)} %get-tuple-element.61.refs_1_, bf16[256,512]{1,0:T(8,128)(2,1)S(1)} %get-tuple-element.62.refs_2_, bf16[256,512]{1,0:T(8,128)(2,1)S(1)} %collective-permute-done.13.refs_3_, ...), custom_call_target="tpu_custom_call" | custom-call | flops 939524096 | bytes 1835008 | tf_op jit(solution)/shard_map/pallas_call | solution.py:217
  36.1 4.1 %collective-permute-start.15 = (bf16[896,512]{1,0:T(8,128)(2,1)S(1)}, bf16[896,512]{1,0:T(8,128)(2,1)S(1)}, u32[]{:S(2)}, u32[]{:S(2)}) collective-permute-start(bf16[896,512]{1,0:T(8,128)(2,1)S(1)} %shard_map.90), channel_id=1, source_target_pairs={{0,48},{1,49},{2,50},{3,51},{4,52},{5,53},{6,54},{7,55},{8,73},{9,... | collective-permute-start | bytes 2752520 | tf_op jit(solution)/shard_map/ppermute | solution.py:48
  40.2 1.7 %collective-permute-done.7.refs_1_ = bf16[896,512]{1,0:T(8,128)(2,1)S(1)} collective-permute-done((bf16[896,512]{1,0:T(8,128)(2,1)S(1)}, bf16[896,512]{1,0:T(8,128)(2,1)S(1)}, u32[]{:S(2)}, u32[]{:S(2)}) %collective-permute-start.7) | collective-permute-done | bytes 917536 | tf_op jit(solution)/shard_map/ppermute | solution.py:48
  41.9 0.2 shard_map.83
  42.0 1.8 %collective-permute-start.8 = (bf16[448,512]{1,0:T(8,128)(2,1)S(1)}, bf16[448,512]{1,0:T(8,128)(2,1)S(1)}, u32[]{:S(2)}, u32[]{:S(2)}) collective-permute-start(bf16[448,512]{1,0:T(8,128)(2,1)S(1)} %get-tuple-element.53), channel_id=1, source_target_pairs={{0,64},{1,65},{2,66},{3,67},{4,68},{5,69},{6,70},{7,71},{8,24},{9,... | collective-permute-start | bytes 1376264 | tf_op jit(solution)/shard_map/ppermute | solution.py:48
  43.9 1.1 %shard_map.89.refs_0_ = f32[896,512]{1,0:T(8,128)S(1)} custom-call(bf16[1792,512]{1,0:T(8,128)(2,1)S(1)} %get-tuple-element.43.refs_0_, bf16[256,512]{1,0:T(8,128)(2,1)S(1)} %get-tuple-element.61.refs_1_, bf16[256,512]{1,0:T(8,128)(2,1)S(1)} %get-tuple-element.62.refs_2_, bf16[256,512]{1,0:T(8,128)(2,1)S(1)} %collective-permute-done.13.refs_3_, ...), custom_call_target="tpu_custom_call" | custom-call | flops 939524096 | bytes 1835008 | tf_op jit(solution)/shard_map/pallas_call | solution.py:217
  45.0 5.8 %collective-permute-done.8.refs_1_ = bf16[448,512]{1,0:T(8,128)(2,1)S(1)} collective-permute-done((bf16[448,512]{1,0:T(8,128)(2,1)S(1)}, bf16[448,512]{1,0:T(8,128)(2,1)S(1)}, u32[]{:S(2)}, u32[]{:S(2)}) %collective-permute-start.8) | collective-permute-done | bytes 458784 | tf_op jit(solution)/shard_map/ppermute | solution.py:48
  50.8 0.1 shard_map.84
  50.9 0.7 collective-permute-done.15.refs_1_
  51.6 0.2 shard_map.91
  51.7 0.0 copy-start.3
  51.7 0.0 copy-start.4
  51.7 1.3 %collective-permute-start.16 = (bf16[448,512]{1,0:T(8,128)(2,1)S(1)}, bf16[448,512]{1,0:T(8,128)(2,1)S(1)}, u32[]{:S(2)}, u32[]{:S(2)}) collective-permute-start(bf16[448,512]{1,0:T(8,128)(2,1)S(1)} %get-tuple-element.64), channel_id=1, source_target_pairs={{0,16},{1,17},{2,18},{3,19},{4,20},{5,21},{6,22},{7,23},{8,72},{9,... | collective-permute-start | bytes 1376264 | tf_op jit(solution)/shard_map/ppermute | solution.py:48
  53.0 2.5 %collective-permute-start.9 = (bf16[224,512]{1,0:T(8,128)(2,1)S(1)}, bf16[224,512]{1,0:T(8,128)(2,1)S(1)}, u32[]{:S(2)}, u32[]{:S(2)}) collective-permute-start(bf16[224,512]{1,0:T(8,128)(2,1)S(1)} %get-tuple-element.55.refs_2_), channel_id=1, source_target_pairs={{0,48},{1,49},{2,50},{3,51},{4,52},{5,53},{6,54},{7,55},{8,73},{9,... | collective-permute-start | bytes 688136 | tf_op jit(solution)/shard_map/ppermute | solution.py:48
  55.6 4.7 %collective-permute-done.16.refs_1_ = bf16[448,512]{1,0:T(8,128)(2,1)S(1)} collective-permute-done((bf16[448,512]{1,0:T(8,128)(2,1)S(1)}, bf16[448,512]{1,0:T(8,128)(2,1)S(1)}, u32[]{:S(2)}, u32[]{:S(2)}) %collective-permute-start.16) | collective-permute-done | bytes 458784 | tf_op jit(solution)/shard_map/ppermute | solution.py:48
  60.3 0.1 shard_map.92
  60.4 1.8 %collective-permute-start.17 = (bf16[224,512]{1,0:T(8,128)(2,1)S(1)}, bf16[224,512]{1,0:T(8,128)(2,1)S(1)}, u32[]{:S(2)}, u32[]{:S(2)}) collective-permute-start(bf16[224,512]{1,0:T(8,128)(2,1)S(1)} %get-tuple-element.66), channel_id=1, source_target_pairs={{0,64},{1,65},{2,66},{3,67},{4,68},{5,69},{6,70},{7,71},{8,24},{9,... | collective-permute-start | bytes 688136 | tf_op jit(solution)/shard_map/ppermute | solution.py:48
  62.2 2.1 %collective-permute-start.10 = (bf16[112,512]{1,0:T(8,128)(2,1)S(1)}, bf16[112,512]{1,0:T(8,128)(2,1)S(1)}, u32[]{:S(2)}, u32[]{:S(2)}) collective-permute-start(bf16[112,512]{1,0:T(8,128)(2,1)S(1)} %get-tuple-element.57), channel_id=1, source_target_pairs={{0,65},{1,64},{2,67},{3,66},{4,69},{5,68},{6,71},{7,70},{8,56},{9,... | collective-permute-start | bytes 344072 | tf_op jit(solution)/shard_map/ppermute | solution.py:48
  64.3 2.1 %collective-permute-done.17.refs_1_ = bf16[224,512]{1,0:T(8,128)(2,1)S(1)} collective-permute-done((bf16[224,512]{1,0:T(8,128)(2,1)S(1)}, bf16[224,512]{1,0:T(8,128)(2,1)S(1)}, u32[]{:S(2)}, u32[]{:S(2)}) %collective-permute-start.17) | collective-permute-done | bytes 229408 | tf_op jit(solution)/shard_map/ppermute | solution.py:48
  66.5 3.1 %collective-permute-start.18 = (bf16[112,512]{1,0:T(8,128)(2,1)S(1)}, bf16[112,512]{1,0:T(8,128)(2,1)S(1)}, u32[]{:S(2)}, u32[]{:S(2)}) collective-permute-start(bf16[112,512]{1,0:T(8,128)(2,1)S(1)} %get-tuple-element.67.refs_4_), channel_id=1, source_target_pairs={{0,65},{1,64},{2,67},{3,66},{4,69},{5,68},{6,71},{7,70},{8,56},{9,... | collective-permute-start | bytes 344072 | tf_op jit(solution)/shard_map/ppermute | solution.py:48
  69.6 0.2 shard_map.94
  69.9 1.3 %collective-permute-start.21 = (bf16[112,512]{1,0:T(8,128)(2,1)S(1)}, bf16[112,512]{1,0:T(8,128)(2,1)S(1)}, u32[]{:S(2)}, u32[]{:S(2)}) collective-permute-start(bf16[112,512]{1,0:T(8,128)(2,1)S(1)} %get-tuple-element.74.own), channel_id=1, source_target_pairs={{0,2},{1,3},{2,0},{3,1},{4,6},{5,7},{6,4},{7,5},{8,14},{9,15},{10,... | collective-permute-start | bytes 344072 | tf_op jit(solution)/shard_map/ppermute | solution.py:48
  71.1 1.5 %collective-permute-done.18.refs_1_ = bf16[112,512]{1,0:T(8,128)(2,1)S(1)} collective-permute-done((bf16[112,512]{1,0:T(8,128)(2,1)S(1)}, bf16[112,512]{1,0:T(8,128)(2,1)S(1)}, u32[]{:S(2)}, u32[]{:S(2)}) %collective-permute-start.18) | collective-permute-done | bytes 114720 | tf_op jit(solution)/shard_map/ppermute | solution.py:48
  72.6 0.2 shard_map.95
  72.8 1.3 %collective-permute-start.19 = (bf16[112,512]{1,0:T(8,128)(2,1)S(1)}, bf16[112,512]{1,0:T(8,128)(2,1)S(1)}, u32[]{:S(2)}, u32[]{:S(2)}) collective-permute-start(bf16[112,512]{1,0:T(8,128)(2,1)S(1)} %get-tuple-element.73.own), channel_id=1, source_target_pairs={{0,2},{1,3},{2,0},{3,1},{4,6},{5,7},{6,4},{7,5},{8,14},{9,15},{10,... | collective-permute-start | bytes 344072 | tf_op jit(solution)/shard_map/ppermute | solution.py:48
  74.1 0.6 collective-permute-done.21.got
  74.7 2.8 %collective-permute-start.22 = (bf16[224,512]{1,0:T(8,128)(2,1)S(1)}, bf16[224,512]{1,0:T(8,128)(2,1)S(1)}, u32[]{:S(2)}, u32[]{:S(2)}) collective-permute-start(bf16[224,512]{1,0:T(8,128)(2,1)S(1)} %shard_map.97.refs_1_), channel_id=1, source_target_pairs={{0,6},{1,7},{2,4},{3,5},{4,2},{5,3},{6,0},{7,1},{8,10},{9,11},{10,... | collective-permute-start | bytes 688136 | tf_op jit(solution)/shard_map/ppermute | solution.py:48
  77.6 1.4 %collective-permute-done.19.got = bf16[112,512]{1,0:T(8,128)(2,1)S(1)} collective-permute-done((bf16[112,512]{1,0:T(8,128)(2,1)S(1)}, bf16[112,512]{1,0:T(8,128)(2,1)S(1)}, u32[]{:S(2)}, u32[]{:S(2)}) %collective-permute-start.19) | collective-permute-done | bytes 114720 | tf_op jit(solution)/shard_map/ppermute | solution.py:48
  79.0 2.8 %collective-permute-start.20 = (bf16[224,512]{1,0:T(8,128)(2,1)S(1)}, bf16[224,512]{1,0:T(8,128)(2,1)S(1)}, u32[]{:S(2)}, u32[]{:S(2)}) collective-permute-start(bf16[224,512]{1,0:T(8,128)(2,1)S(1)} %shard_map.96.refs_2_), channel_id=1, source_target_pairs={{0,6},{1,7},{2,4},{3,5},{4,2},{5,3},{6,0},{7,1},{8,10},{9,11},{10,... | collective-permute-start | bytes 688136 | tf_op jit(solution)/shard_map/ppermute | solution.py:48
  81.8 1.0 %maximum_bitcast_fusion = (f32[1,112,1024]{2,1,0:T(8,128)}, f32[1,112,1024]{2,1,0:T(8,128)}) fusion(f32[112,512]{1,0:T(8,128)S(1)} %get-tuple-element.70, f32[112,512]{1,0:T(8,128)S(1)} %get-tuple-element.68, f32[112,512]{1,0:T(8,128)S(1)} %get-tuple-element.72, f32[112,512]{1,0:T(8,128)S(1)} %get-tuple-element.71), kind=kLoop, calls=%fused_computation | loop fusion | flops 229376 | bytes 1835008 | tf_op jit(solution)/shard_map/reshape | solution.py:339
  82.8 1.1 %shard_map.98.refs_3_ = f32[448,2048]{1,0:T(8,128)S(1)} custom-call(bf16[1024,2048]{1,0:T(8,128)(2,1)S(1)} %shard_map.86.refs_0_.refs_1_, bf16[224,512]{1,0:T(8,128)(2,1)S(1)} %shard_map.97.refs_1_, bf16[224,512]{1,0:T(8,128)(2,1)S(1)} %collective-permute-done.22.refs_2_), custom_call_target="tpu_custom_call" | custom-call | flops 939524096 | bytes 5767168 | tf_op jit(solution)/shard_map/pallas_call | solution.py:217
  84.0 1.9 %shard_map.99.refs_4_ = bf16[4,112,2048]{2,1,0:T(8,128)(2,1)} custom-call(s32[4]{0:T(128)S(1)} %pad_add_fusion.refs_2_.pos.refs_0_, bf16[1024,2048]{1,0:T(8,128)(2,1)S(1)} %shard_map.86.refs_0_.refs_1_, bf16[224,512]{1,0:T(8,128)(2,1)S(1)} %shard_map.96.refs_2_, f32[448,2048]{1,0:T(8,128)S(1)} %shard_map.98.refs_3_), custom_call_target="tpu_custom_call" | custom-call | flops 469762048 | bytes 2097152 | tf_op jit(solution)/shard_map/pallas_call | solution.py:326
  85.9 0.4 collective-permute-done.20.refs_2_
  86.3 1.9 %shard_map.100 = bf16[4,112,2048]{2,1,0:T(8,128)(2,1)} custom-call(s32[4]{0:T(128)S(1)} %pad_add_fusion.refs_2_.pos.refs_0_, bf16[1024,2048]{1,0:T(8,128)(2,1)S(1)} %shard_map.86.refs_0_.refs_1_, bf16[224,512]{1,0:T(8,128)(2,1)S(1)} %collective-permute-done.20.refs_2_, f32[448,2048]{1,0:T(8,128)S(1)} %shard_map.98.refs_3_, ...), custom_call_target="tpu_custom_call", output_to_operand_aliasing={{}: (4, {})} | custom-call | flops 469762048 | bytes 2097152 | tf_op jit(solution)/shard_map/pallas_call | solution.py:326
  (20 shorter events, 0.2 us)
Async XLA Ops:
  0.7 2.2 %copy-start.1 = (bf16[512,2048]{1,0:T(8,128)(2,1)S(1)}, bf16[512,2048]{1,0:T(8,128)(2,1)}, u32[]{:S(2)}) copy-start(bf16[512,2048]{1,0:T(8,128)(2,1)} %refs_0_.3) | copy-start | bytes 6291460
  3.0 2.9 %copy-start = (bf16[2048,1024]{1,0:T(8,128)(2,1)S(1)}, bf16[2048,1024]{1,0:T(8,128)(2,1)}, u32[]{:S(2)}) copy-start(bf16[2048,1024]{1,0:T(8,128)(2,1)} %projection.1) | copy-start | bytes 12582916
  4.2 9.3 %collective-permute-start = (bf16[512,512]{1,0:T(8,128)(2,1)S(1)}, bf16[512,512]{1,0:T(8,128)(2,1)S(1)}, u32[]{:S(2)}, u32[]{:S(2)}) collective-permute-start(bf16[512,512]{1,0:T(8,128)(2,1)S(1)} %get-tuple-element.44), channel_id=1, source_target_pairs={{0,2},{1,3},{2,0},{3,1},{4,6},{5,7},{6,4},{7,5},{8,14},{9,15},{10,... | collective-permute-start | bytes 1572872 | tf_op jit(solution)/shard_map/ppermute | solution.py:48
  5.9 2.2 %copy-start.2 = (bf16[512,3584]{1,0:T(8,128)(2,1)S(1)}, bf16[512,3584]{1,0:T(8,128)(2,1)}, u32[]{:S(2)}) copy-start(bf16[512,3584]{1,0:T(8,128)(2,1)} %hidden.1) | copy-start | bytes 11010052
  7.2 14.6 %collective-permute-start.11 = (bf16[512,512]{1,0:T(8,128)(2,1)S(1)}, bf16[512,512]{1,0:T(8,128)(2,1)S(1)}, u32[]{:S(2)}, u32[]{:S(2)}) collective-permute-start(bf16[512,512]{1,0:T(8,128)(2,1)S(1)} %get-tuple-element.58), channel_id=1, source_target_pairs={{0,2},{1,3},{2,0},{3,1},{4,6},{5,7},{6,4},{7,5},{8,14},{9,15},{10,... | collective-permute-start | bytes 1572872 | tf_op jit(solution)/shard_map/ppermute | solution.py:48
  9.9 15.5 %collective-permute-start.5 = (bf16[560,512]{1,0:T(8,128)(2,1)S(1)}, bf16[560,512]{1,0:T(8,128)(2,1)S(1)}, u32[]{:S(2)}, u32[]{:S(2)}) collective-permute-start(bf16[560,512]{1,0:T(8,128)(2,1)S(1)} %get-tuple-element.50), channel_id=1, source_target_pairs={{0,8},{1,9},{2,10},{3,11},{4,12},{5,13},{6,14},{7,15},{8,0},{9,1},... | collective-permute-start | bytes 1720328 | tf_op jit(solution)/shard_map/ppermute | solution.py:48
  13.9 11.1 %collective-permute-start.1 = (bf16[512,512]{1,0:T(8,128)(2,1)S(1)}, bf16[512,512]{1,0:T(8,128)(2,1)S(1)}, u32[]{:S(2)}, u32[]{:S(2)}) collective-permute-start(bf16[512,512]{1,0:T(8,128)(2,1)S(1)} %get-tuple-element.46._), channel_id=1, source_target_pairs={{0,6},{1,7},{2,4},{3,5},{4,2},{5,3},{6,0},{7,1},{8,10},{9,11},{10,... | collective-permute-start | bytes 1572872 | tf_op jit(solution)/shard_map/ppermute | solution.py:48
  16.9 9.0 %collective-permute-start.4 = (bf16[672,512]{1,0:T(8,128)(2,1)S(1)}, bf16[672,512]{1,0:T(8,128)(2,1)S(1)}, u32[]{:S(2)}, u32[]{:S(2)}) collective-permute-start(bf16[672,512]{1,0:T(8,128)(2,1)S(1)} %get-tuple-element.49), channel_id=1, source_target_pairs={{0,8},{1,9},{2,10},{3,11},{4,12},{5,13},{6,14},{7,15},{8,0},{9,1},... | collective-permute-start | bytes 2064392 | tf_op jit(solution)/shard_map/ppermute | solution.py:48
  16.9 9.0 %collective-permute-start.6 = (bf16[560,512]{1,0:T(8,128)(2,1)S(1)}, bf16[560,512]{1,0:T(8,128)(2,1)S(1)}, u32[]{:S(2)}, u32[]{:S(2)}) collective-permute-start(bf16[560,512]{1,0:T(8,128)(2,1)S(1)} %get-tuple-element.51), channel_id=1, source_target_pairs={{0,8},{1,9},{2,10},{3,11},{4,12},{5,13},{6,14},{7,15},{8,0},{9,1},... | collective-permute-start | bytes 1720328 | tf_op jit(solution)/shard_map/ppermute | solution.py:48
  22.2 10.5 %collective-permute-start.12 = (bf16[512,512]{1,0:T(8,128)(2,1)S(1)}, bf16[512,512]{1,0:T(8,128)(2,1)S(1)}, u32[]{:S(2)}, u32[]{:S(2)}) collective-permute-start(bf16[512,512]{1,0:T(8,128)(2,1)S(1)} %get-tuple-element.60), channel_id=1, source_target_pairs={{0,6},{1,7},{2,4},{3,5},{4,2},{5,3},{6,0},{7,1},{8,10},{9,11},{10,... | collective-permute-start | bytes 1572872 | tf_op jit(solution)/shard_map/ppermute | solution.py:48
  25.3 1.6 %collective-permute-start.2 = (bf16[256,512]{1,0:T(8,128)(2,1)S(1)}, bf16[256,512]{1,0:T(8,128)(2,1)S(1)}, u32[]{:S(2)}, u32[]{:S(2)}) collective-permute-start(bf16[256,512]{1,0:T(8,128)(2,1)S(1)} %get-tuple-element.47.refs_1_), channel_id=1, source_target_pairs={{0,8},{1,9},{2,10},{3,11},{4,12},{5,13},{6,14},{7,15},{8,0},{9,1},... | collective-permute-start | bytes 786440 | tf_op jit(solution)/shard_map/ppermute | solution.py:48
  25.4 1.9 %collective-permute-start.3 = (bf16[256,512]{1,0:T(8,128)(2,1)S(1)}, bf16[256,512]{1,0:T(8,128)(2,1)S(1)}, u32[]{:S(2)}, u32[]{:S(2)}) collective-permute-start(bf16[256,512]{1,0:T(8,128)(2,1)S(1)} %get-tuple-element.48.refs_2_), channel_id=1, source_target_pairs={{0,8},{1,9},{2,10},{3,11},{4,12},{5,13},{6,14},{7,15},{8,0},{9,1},... | collective-permute-start | bytes 786440 | tf_op jit(solution)/shard_map/ppermute | solution.py:48
  28.4 13.5 %collective-permute-start.7 = (bf16[896,512]{1,0:T(8,128)(2,1)S(1)}, bf16[896,512]{1,0:T(8,128)(2,1)S(1)}, u32[]{:S(2)}, u32[]{:S(2)}) collective-permute-start(bf16[896,512]{1,0:T(8,128)(2,1)S(1)} %shard_map.82.refs_0_), channel_id=1, source_target_pairs={{0,16},{1,17},{2,18},{3,19},{4,20},{5,21},{6,22},{7,23},{8,72},{9,... | collective-permute-start | bytes 2752520 | tf_op jit(solution)/shard_map/ppermute | solution.py:48
  32.9 1.7 %collective-permute-start.13 = (bf16[256,512]{1,0:T(8,128)(2,1)S(1)}, bf16[256,512]{1,0:T(8,128)(2,1)S(1)}, u32[]{:S(2)}, u32[]{:S(2)}) collective-permute-start(bf16[256,512]{1,0:T(8,128)(2,1)S(1)} %get-tuple-element.61.refs_1_), channel_id=1, source_target_pairs={{0,8},{1,9},{2,10},{3,11},{4,12},{5,13},{6,14},{7,15},{8,0},{9,1},... | collective-permute-start | bytes 786440 | tf_op jit(solution)/shard_map/ppermute | solution.py:48
  33.0 1.9 %collective-permute-start.14 = (bf16[256,512]{1,0:T(8,128)(2,1)S(1)}, bf16[256,512]{1,0:T(8,128)(2,1)S(1)}, u32[]{:S(2)}, u32[]{:S(2)}) collective-permute-start(bf16[256,512]{1,0:T(8,128)(2,1)S(1)} %get-tuple-element.62.refs_2_), channel_id=1, source_target_pairs={{0,8},{1,9},{2,10},{3,11},{4,12},{5,13},{6,14},{7,15},{8,0},{9,1},... | collective-permute-start | bytes 786440 | tf_op jit(solution)/shard_map/ppermute | solution.py:48
  36.1 15.5 %collective-permute-start.15 = (bf16[896,512]{1,0:T(8,128)(2,1)S(1)}, bf16[896,512]{1,0:T(8,128)(2,1)S(1)}, u32[]{:S(2)}, u32[]{:S(2)}) collective-permute-start(bf16[896,512]{1,0:T(8,128)(2,1)S(1)} %shard_map.90), channel_id=1, source_target_pairs={{0,48},{1,49},{2,50},{3,51},{4,52},{5,53},{6,54},{7,55},{8,73},{9,... | collective-permute-start | bytes 2752520 | tf_op jit(solution)/shard_map/ppermute | solution.py:48
  42.0 8.7 %collective-permute-start.8 = (bf16[448,512]{1,0:T(8,128)(2,1)S(1)}, bf16[448,512]{1,0:T(8,128)(2,1)S(1)}, u32[]{:S(2)}, u32[]{:S(2)}) collective-permute-start(bf16[448,512]{1,0:T(8,128)(2,1)S(1)} %get-tuple-element.53), channel_id=1, source_target_pairs={{0,64},{1,65},{2,66},{3,67},{4,68},{5,69},{6,70},{7,71},{8,24},{9,... | collective-permute-start | bytes 1376264 | tf_op jit(solution)/shard_map/ppermute | solution.py:48
  51.7 17.9 %copy-start.3 = (f32[1,112,1024]{2,1,0:T(8,128)S(1)}, f32[1,112,1024]{2,1,0:T(8,128)}, u32[]{:S(2)}) copy-start(f32[1,112,1024]{2,1,0:T(8,128)} %refs_2_.3) | copy-start | bytes 1376260
  51.7 17.9 %copy-start.4 = (f32[1,112,1024]{2,1,0:T(8,128)S(1)}, f32[1,112,1024]{2,1,0:T(8,128)}, u32[]{:S(2)}) copy-start(f32[1,112,1024]{2,1,0:T(8,128)} %refs_3_.3) | copy-start | bytes 1376260
  51.7 8.6 %collective-permute-start.16 = (bf16[448,512]{1,0:T(8,128)(2,1)S(1)}, bf16[448,512]{1,0:T(8,128)(2,1)S(1)}, u32[]{:S(2)}, u32[]{:S(2)}) collective-permute-start(bf16[448,512]{1,0:T(8,128)(2,1)S(1)} %get-tuple-element.64), channel_id=1, source_target_pairs={{0,16},{1,17},{2,18},{3,19},{4,20},{5,21},{6,22},{7,23},{8,72},{9,... | collective-permute-start | bytes 1376264 | tf_op jit(solution)/shard_map/ppermute | solution.py:48
  53.0 9.1 %collective-permute-start.9 = (bf16[224,512]{1,0:T(8,128)(2,1)S(1)}, bf16[224,512]{1,0:T(8,128)(2,1)S(1)}, u32[]{:S(2)}, u32[]{:S(2)}) collective-permute-start(bf16[224,512]{1,0:T(8,128)(2,1)S(1)} %get-tuple-element.55.refs_2_), channel_id=1, source_target_pairs={{0,48},{1,49},{2,50},{3,51},{4,52},{5,53},{6,54},{7,55},{8,73},{9,... | collective-permute-start | bytes 688136 | tf_op jit(solution)/shard_map/ppermute | solution.py:48
  60.4 6.1 %collective-permute-start.17 = (bf16[224,512]{1,0:T(8,128)(2,1)S(1)}, bf16[224,512]{1,0:T(8,128)(2,1)S(1)}, u32[]{:S(2)}, u32[]{:S(2)}) collective-permute-start(bf16[224,512]{1,0:T(8,128)(2,1)S(1)} %get-tuple-element.66), channel_id=1, source_target_pairs={{0,64},{1,65},{2,66},{3,67},{4,68},{5,69},{6,70},{7,71},{8,24},{9,... | collective-permute-start | bytes 688136 | tf_op jit(solution)/shard_map/ppermute | solution.py:48
  62.2 7.4 %collective-permute-start.10 = (bf16[112,512]{1,0:T(8,128)(2,1)S(1)}, bf16[112,512]{1,0:T(8,128)(2,1)S(1)}, u32[]{:S(2)}, u32[]{:S(2)}) collective-permute-start(bf16[112,512]{1,0:T(8,128)(2,1)S(1)} %get-tuple-element.57), channel_id=1, source_target_pairs={{0,65},{1,64},{2,67},{3,66},{4,69},{5,68},{6,71},{7,70},{8,56},{9,... | collective-permute-start | bytes 344072 | tf_op jit(solution)/shard_map/ppermute | solution.py:48
  66.5 6.1 %collective-permute-start.18 = (bf16[112,512]{1,0:T(8,128)(2,1)S(1)}, bf16[112,512]{1,0:T(8,128)(2,1)S(1)}, u32[]{:S(2)}, u32[]{:S(2)}) collective-permute-start(bf16[112,512]{1,0:T(8,128)(2,1)S(1)} %get-tuple-element.67.refs_4_), channel_id=1, source_target_pairs={{0,65},{1,64},{2,67},{3,66},{4,69},{5,68},{6,71},{7,70},{8,56},{9,... | collective-permute-start | bytes 344072 | tf_op jit(solution)/shard_map/ppermute | solution.py:48
  69.9 4.9 %collective-permute-start.21 = (bf16[112,512]{1,0:T(8,128)(2,1)S(1)}, bf16[112,512]{1,0:T(8,128)(2,1)S(1)}, u32[]{:S(2)}, u32[]{:S(2)}) collective-permute-start(bf16[112,512]{1,0:T(8,128)(2,1)S(1)} %get-tuple-element.74.own), channel_id=1, source_target_pairs={{0,2},{1,3},{2,0},{3,1},{4,6},{5,7},{6,4},{7,5},{8,14},{9,15},{10,... | collective-permute-start | bytes 344072 | tf_op jit(solution)/shard_map/ppermute | solution.py:48
  72.8 6.2 %collective-permute-start.19 = (bf16[112,512]{1,0:T(8,128)(2,1)S(1)}, bf16[112,512]{1,0:T(8,128)(2,1)S(1)}, u32[]{:S(2)}, u32[]{:S(2)}) collective-permute-start(bf16[112,512]{1,0:T(8,128)(2,1)S(1)} %get-tuple-element.73.own), channel_id=1, source_target_pairs={{0,2},{1,3},{2,0},{3,1},{4,6},{5,7},{6,4},{7,5},{8,14},{9,15},{10,... | collective-permute-start | bytes 344072 | tf_op jit(solution)/shard_map/ppermute | solution.py:48
  74.7 8.1 %collective-permute-start.22 = (bf16[224,512]{1,0:T(8,128)(2,1)S(1)}, bf16[224,512]{1,0:T(8,128)(2,1)S(1)}, u32[]{:S(2)}, u32[]{:S(2)}) collective-permute-start(bf16[224,512]{1,0:T(8,128)(2,1)S(1)} %shard_map.97.refs_1_), channel_id=1, source_target_pairs={{0,6},{1,7},{2,4},{3,5},{4,2},{5,3},{6,0},{7,1},{8,10},{9,11},{10,... | collective-permute-start | bytes 688136 | tf_op jit(solution)/shard_map/ppermute | solution.py:48
  79.0 7.3 %collective-permute-start.20 = (bf16[224,512]{1,0:T(8,128)(2,1)S(1)}, bf16[224,512]{1,0:T(8,128)(2,1)S(1)}, u32[]{:S(2)}, u32[]{:S(2)}) collective-permute-start(bf16[224,512]{1,0:T(8,128)(2,1)S(1)} %shard_map.96.refs_2_), channel_id=1, source_target_pairs={{0,6},{1,7},{2,4},{3,5},{4,2},{5,3},{6,0},{7,1},{8,10},{9,11},{10,... | collective-permute-start | bytes 688136 | tf_op jit(solution)/shard_map/ppermute | solution.py:48
